TPU v7x, 32 devices: a whole 2x2x4 slice. The times are simulated.
32 devices in a mesh: ta: 8 (over y, x, core), gz: 4 (over z).
Axes of the slice: x: 2, y: 2, z: 4, core: 2. Of those that a mesh axis runs over, the one named last changes fastest.
Arguments:
- gauge_links: float32 [4, 2, 3, 3, 8, 32, 1024], P(None, None, None, None, 'ta', 'gz'), may hold values from -1 to 1, as said below
Outputs:
- rotated: float32 [4, 2, 3, 3, 8, 32, 1024], P(None, None, None, None, 'ta', 'gz')
Inputs may be any that keep to these rules, and one draw needn't show every extreme that they name: `gauge_links`: every link is a special unitary 3x3 matrix.
All inputs are finite; a program needn't handle non-finite values.
Results may differ from a plain program's by a relative error of at most 0.0001.
Values sent between devices are 32-bit elements; how exact they have to be, the bound alone decides.
No kernel may reach another device: no remote copies, remote signals or barrier semaphores. Data moves between devices by JAX's collectives and lax.ppermute only.
A program may use at most 192 MiB of HBM per device.

v0:
```python
import jax
import jax.numpy as jnp
from jax import lax
from jax.sharding import PartitionSpec as P

LX = 32
LY = 32
ITERS = 2


def passed_along(block, axis, distance):
    devices = range(lax.axis_size(axis))
    route = [((i - distance) % len(devices), i) for i in devices]
    return lax.ppermute(block, axis, route)


def with_halo(block, sides, width):
    for axis, dim in sides:
        count = lax.axis_size(axis)
        forward = [(i, i + 1) for i in range(count - 1)]
        forward.append((count - 1, 0))
        backward = [(target, source) for source, target in forward]
        low = lax.ppermute(
            lax.slice_in_dim(block, block.shape[dim] - width, None, axis=dim), axis, forward
        )
        high = lax.ppermute(lax.slice_in_dim(block, 0, width, axis=dim), axis, backward)
        block = jnp.concatenate([low, block, high], axis=dim)
    return block


def matrix_product(left_real, left_imag, right_real, right_imag):
    out_real = []
    out_imag = []
    for row_index in range(3):
        real_row = []
        imag_row = []
        for column in range(3):
            total_real = (
                left_real[row_index, 0] * right_real[0, column]
                - left_imag[row_index, 0] * right_imag[0, column]
            )
            total_imag = (
                left_real[row_index, 0] * right_imag[0, column]
                + left_imag[row_index, 0] * right_real[0, column]
            )
            for inner_index in (1, 2):
                total_real = (
                    total_real
                    + left_real[row_index, inner_index] * right_real[inner_index, column]
                    - left_imag[row_index, inner_index] * right_imag[inner_index, column]
                )
                total_imag = (
                    total_imag
                    + left_real[row_index, inner_index] * right_imag[inner_index, column]
                    + left_imag[row_index, inner_index] * right_real[inner_index, column]
                )
            real_row.append(total_real)
            imag_row.append(total_imag)
        out_real.append(jnp.stack(real_row))
        out_imag.append(jnp.stack(imag_row))
    return (jnp.stack(out_real), jnp.stack(out_imag))


def adjoint(matrix_real, matrix_imag):
    return (jnp.swapaxes(matrix_real, 0, 1), -jnp.swapaxes(matrix_imag, 0, 1))


def identity_like(matrix_real):
    return jnp.eye(3, dtype=jnp.float32).reshape((3, 3) + (1,) * (matrix_real.ndim - 2))


def antihermitian(w_real, w_imag):
    part_real = 0.5 * (w_real - jnp.swapaxes(w_real, 0, 1))
    part_imag = 0.5 * (w_imag + jnp.swapaxes(w_imag, 0, 1))
    trace_third = (w_imag[0, 0] + w_imag[1, 1] + w_imag[2, 2]) / 3.0
    return (part_real, part_imag - identity_like(w_real) * trace_third[None, None])


def normalized(row_real, row_imag):
    factor = 1.0 / jnp.sqrt(jnp.sum(row_real * row_real + row_imag * row_imag, axis=0))
    return (row_real * factor, row_imag * factor)


def conjugate_cross(first_real, first_imag, second_real, second_imag):
    third_real = []
    third_imag = []
    for position in range(3):
        follow = (position + 1) % 3
        beyond = (position + 2) % 3
        cross_real = (
            first_real[follow] * second_real[beyond]
            - first_imag[follow] * second_imag[beyond]
            - (first_real[beyond] * second_real[follow] - first_imag[beyond] * second_imag[follow])
        )
        cross_imag = (
            first_real[follow] * second_imag[beyond]
            + first_imag[follow] * second_real[beyond]
            - (first_real[beyond] * second_imag[follow] + first_imag[beyond] * second_real[follow])
        )
        third_real.append(cross_real)
        third_imag.append(-cross_imag)
    return (jnp.stack(third_real), jnp.stack(third_imag))


def unitary_projection(power_real, power_imag):
    first_real, first_imag = normalized(power_real[0], power_imag[0])
    proj_real = jnp.sum(first_real * power_real[1] + first_imag * power_imag[1], axis=0)
    proj_imag = jnp.sum(first_real * power_imag[1] - first_imag * power_real[1], axis=0)
    second_real = power_real[1] - (proj_real * first_real - proj_imag * first_imag)
    second_imag = power_imag[1] - (proj_real * first_imag + proj_imag * first_real)
    second_real, second_imag = normalized(second_real, second_imag)
    third_real, third_imag = conjugate_cross(first_real, first_imag, second_real, second_imag)
    gauge_real = jnp.stack([first_real, second_real, third_real])
    gauge_imag = jnp.stack([first_imag, second_imag, third_imag])
    return (gauge_real, gauge_imag)


def second_order_exponential(smooth_real, smooth_imag):
    exponent_real = 0.04 * smooth_real
    exponent_imag = 0.04 * smooth_imag
    square_real, square_imag = matrix_product(
        exponent_real, exponent_imag, exponent_real, exponent_imag
    )
    power_real = identity_like(smooth_real) + exponent_real + 0.5 * square_real
    power_imag = exponent_imag + 0.5 * square_imag
    return unitary_projection(power_real, power_imag)


def rotate_link(left_side, link_now, right_side):
    product_real, product_imag = matrix_product(
        left_side[0], left_side[1], link_now[0], link_now[1]
    )
    adjoint_real, adjoint_imag = adjoint(right_side[0], right_side[1])
    new_real, new_imag = matrix_product(product_real, product_imag, adjoint_real, adjoint_imag)
    return jnp.stack([new_real, new_imag])


def displace(array, direction, amount):
    if direction == 1:
        return jnp.roll(array, amount * LX, axis=-1)
    sites = array.shape[-1]
    column_x = jnp.arange(sites, dtype=jnp.int32) % LX
    edge = 0 if amount == 1 else LX - 1
    inside = jnp.roll(array, amount, axis=-1)
    wrapped = jnp.roll(array, amount - amount * LX, axis=-1)
    return jnp.where(column_x == edge, wrapped, inside)


def lattice_sine(mode_index, length):
    sine_value = jnp.sin(jnp.pi * mode_index.astype(jnp.float32) / length)
    return 4.0 * sine_value * sine_value


def dense_table(first_length, second_length):
    count = first_length * second_length
    index = jnp.arange(count, dtype=jnp.int32)
    inner = index % first_length
    outer = index // first_length
    phase_inner = inner[:, None] * inner[None, :] % first_length
    phase_outer = outer[:, None] * outer[None, :] % second_length
    angles = (
        2.0
        * jnp.pi
        * (
            phase_inner.astype(jnp.float32) / first_length
            + phase_outer.astype(jnp.float32) / second_length
        )
    )
    cosine = jnp.cos(angles)
    sine_value = jnp.sin(angles)
    return jnp.concatenate(
        [
            jnp.concatenate([cosine, -sine_value], axis=1),
            jnp.concatenate([sine_value, cosine], axis=1),
        ],
        axis=0,
    )


def forward_apply(rows, table):
    return jnp.dot(rows, table, precision=lax.Precision.HIGHEST, preferred_element_type=jnp.float32)


def backward_apply(rows, table, factor):
    return (
        jnp.einsum(
            "rq,pq->rp",
            rows,
            table,
            precision=lax.Precision.HIGHEST,
            preferred_element_type=jnp.float32,
        )
        * factor
    )


def spectral_weight(time_length, depth_length, columns):
    plane_sites = LX * LY
    offset = lax.axis_index("ta") * (plane_sites // lax.axis_size("ta")) + lax.axis_index("gz") * (
        plane_sites // (lax.axis_size("ta") * lax.axis_size("gz"))
    )
    column_index = offset + jnp.arange(columns, dtype=jnp.int32)
    wave_y = column_index // LX
    wave_x = column_index % LX
    line_index = jnp.arange(time_length * depth_length, dtype=jnp.int32)
    time_modes = line_index // depth_length
    depth_modes = line_index % depth_length
    summed = (lattice_sine(wave_y, LY) + lattice_sine(wave_x, LX))[:, None] + (
        lattice_sine(time_modes, time_length) + lattice_sine(depth_modes, depth_length)
    )[None, :]
    anchor = (column_index[:, None] == 0) & (line_index[None, :] == 0)
    return jnp.where(anchor, 0.0, 16.0 / jnp.where(anchor, 1.0, summed))


def smooth_field(delta_real, delta_imag, plane_table, line_table):
    real_side = delta_real.reshape((9,) + delta_real.shape[2:])
    imag_side = delta_imag.reshape((9,) + delta_imag.shape[2:])
    stacked = jnp.stack([real_side, imag_side], axis=3)
    layout = stacked.shape
    count, local_time, local_depth, pair, sites = layout
    plane = forward_apply(
        stacked.reshape(count * local_time * local_depth, 2 * sites), plane_table
    ).reshape(layout)
    spectral = lax.all_to_all(
        lax.all_to_all(plane, "ta", split_axis=4, concat_axis=1, tiled=True),
        "gz",
        split_axis=4,
        concat_axis=2,
        tiled=True,
    )
    time_length = spectral.shape[1]
    depth_length = spectral.shape[2]
    columns = spectral.shape[4]
    lines = time_length * depth_length
    ordered = jnp.transpose(spectral, (0, 4, 3, 1, 2)).reshape(count * columns, 2 * lines)
    ordered = forward_apply(ordered, line_table).reshape(count, columns, 2, lines)
    ordered = ordered * spectral_weight(time_length, depth_length, columns)[None, :, None, :]
    ordered = backward_apply(ordered.reshape(count * columns, 2 * lines), line_table, 1.0 / lines)
    ordered = ordered.reshape(count, columns, 2, time_length, depth_length)
    spectral = jnp.transpose(ordered, (0, 3, 4, 2, 1)).reshape(
        count, time_length, depth_length, 2, 1, columns
    )
    spectral = lax.all_to_all(
        lax.all_to_all(spectral, "ta", split_axis=1, concat_axis=4, tiled=True),
        "gz",
        split_axis=2,
        concat_axis=5,
        tiled=True,
    )
    plane = spectral.reshape(count * local_time * local_depth, 2 * sites)
    smooth = backward_apply(plane, plane_table, 1.0 / sites).reshape(layout)
    real_part = smooth[:, :, :, 0]
    imag_part = smooth[:, :, :, 1]
    smooth_real = real_part.reshape((3, 3) + real_part.shape[1:])
    smooth_imag = imag_part.reshape((3, 3) + imag_part.shape[1:])
    return (smooth_real, smooth_imag)


def on_device(gauge_links):
    lattice = gauge_links
    local_time = lattice.shape[4]
    local_depth = lattice.shape[5]
    plane_table = dense_table(LX, LY)
    line_table = dense_table(local_depth * lax.axis_size("gz"), local_time * lax.axis_size("ta"))
    lower_time = passed_along(lattice[3, :, :, :, local_time - 1], "ta", 1)
    lower_depth = passed_along(lattice[2, :, :, :, :, local_depth - 1], "gz", 1)
    for iteration in range(ITERS):
        summed = jnp.zeros(lattice.shape[1:], jnp.float32)
        for direction in range(4):
            link_now = lattice[direction]
            if direction == 3:
                behind = jnp.concatenate(
                    [lower_time[:, :, :, None], link_now[:, :, :, :-1]], axis=3
                )
            elif direction == 2:
                behind = jnp.concatenate(
                    [lower_depth[:, :, :, :, None], link_now[:, :, :, :, :-1]], axis=4
                )
            else:
                behind = displace(link_now, direction, 1)
            summed = summed + behind - link_now
        delta_real, delta_imag = antihermitian(summed[0], summed[1])
        smooth_real, smooth_imag = smooth_field(delta_real, delta_imag, plane_table, line_table)
        gauge_real, gauge_imag = second_order_exponential(smooth_real, smooth_imag)
        gauge = jnp.stack([gauge_real, gauge_imag])
        padded = with_halo(gauge, (("ta", 3), ("gz", 4)), 1)
        rotated = []
        for direction in range(4):
            if direction == 3:
                forward = padded[:, :, :, 2:, 1:-1]
            elif direction == 2:
                forward = padded[:, :, :, 1:-1, 2:]
            else:
                forward = displace(gauge, direction, -1)
            rotated.append(rotate_link(gauge, lattice[direction], forward))
        if iteration + 1 < ITERS:
            lower_time = rotate_link(padded[:, :, :, 0, 1:-1], lower_time, gauge[:, :, :, 0])
            lower_depth = rotate_link(padded[:, :, :, 1:-1, 0], lower_depth, gauge[:, :, :, :, 0])
        lattice = jnp.stack(rotated)
    return lattice


def solution(mesh):
    in_specs = (P(None, None, None, None, "ta", "gz", None),)
    out_specs = P(None, None, None, None, "ta", "gz", None)
    return jax.shard_map(
        on_device, mesh=mesh, in_specs=in_specs, out_specs=out_specs, check_vma=False
    )
```

profile of v0, /device:TPU:0, one launch (start us, length us, event | category | flops | bytes accessed | tf_op | source)
XLA Modules:
  0.0 558.9 jit_solution(6694937170176805364)
XLA Ops:
  14.0 23.0 %fusion.8 = (f32[1024,1024]{0,1:T(8,128)}, f32[1024,1024]{0,1:T(8,128)}, f32[1024,1024]{0,1:T(8,128)}) fusion(s32[1024]{0:T(1024)S(1)} %get-tuple-element.179, s32[1024]{0:T(1024)S(1)} %get-tuple-element.180), kind=kLoop, calls=%fused_computation.26 | loop fusion | flops 30408704 | bytes 12591104 | tf_op jit(solution)/shard_map/neg | solution.py:173
  37.0 10.6 %maximum_maximum_fusion = f32[2048,2048]{0,1:T(8,128)S(1)} fusion(f32[1024,1024]{0,1:T(8,128)} %get-tuple-element.171, f32[1024,1024]{0,1:T(8,128)} %get-tuple-element.170, f32[1024,1024]{0,1:T(8,128)} %get-tuple-element.169), kind=kLoop, calls=%fused_computation | loop fusion | flops 12582912 | bytes 29360128 | tf_op jit(solution)/shard_map/concatenate | solution.py:171
  53.6 16.3 %convolution_bitcast_fusion.1 = f32[9,1,8,2,1024]{4,2,3,0,1:T(8,128)S(1)} fusion(f32[9,8,2048,1]{2,1,3,0:T(8,128)S(1)} %bitcast.5512, f32[2,1024,2048,1]{2,1,0,3:T(8,128)S(1)} %bitcast.5408), kind=kOutput, calls=%fused_computation.54 | convolution fusion | flops 3623878656 | bytes 17956864 | tf_op jit(solution)/shard_map/dot_general | solution.py:181
  76.2 8.6 %reshape.64562 = f32[8,1,18432]{2,1,0:T(1,128)} reshape(f32[1024,1,2,8,9]{4,3,2,1,0:T(8,128)} %bitcast.5397) | data formatting | bytes 1179648
  89.1 9.9 %all-to-all-done = f32[8,1,18432]{2,1,0:T(1,128)S(1)} async-done(((f32[8,1,18432]{2,1,0:T(1,128)}), f32[8,1,18432]{2,1,0:T(1,128)S(1)}, u32[]{:S(2)}, u32[]{:S(2)}) %all-to-all-start) | async-done | bytes 589856 | tf_op jit(solution)/shard_map/all_to_all | solution.py:225
  101.5 12.4 %reshape.64563 = f32[1024,1,2,8,9]{4,3,2,1,0:T(8,128)} reshape(f32[8,18432]{1,0:T(8,128)S(1)} %reduce.8) | data formatting | bytes 1179648
  121.8 8.6 %reshape.64564 = f32[4,1,36864]{2,1,0:T(1,128)} reshape(f32[128,8,2,8,9]{4,3,2,1,0:T(8,128)} %bitcast.5399) | data formatting | bytes 1179648
  137.1 12.0 %all-to-all-done.1 = f32[4,1,36864]{2,1,0:T(1,128)} async-done(((f32[4,1,36864]{2,1,0:T(1,128)}), f32[4,1,36864]{2,1,0:T(1,128)}, u32[]{:S(2)}, u32[]{:S(2)}) %all-to-all-start.1) | async-done | bytes 589856 | tf_op jit(solution)/shard_map/all_to_all | solution.py:224
  153.0 13.5 %reshape.64565 = f32[128,8,2,8,9]{4,3,2,1,0:T(8,128)} reshape(f32[4,36864]{1,0:T(4,128)} %reduce.9) | data formatting | bytes 1179648
  166.5 8.1 %copy.3858 = f32[9,8,8,2,4,32]{5,4,2,3,1,0:T(4,128)} copy(f32[9,8,8,2,4,32]{0,2,3,1,5,4:T(8,128)} %bitcast.5400) | data formatting | bytes 1179648 | tf_op jit(solution)/shard_map/all_to_all | solution.py:224
  203.0 14.3 %all_to_all.138 = f32[8,1,18432]{2,1,0:T(1,128)S(1)} all-to-all(f32[8,1,18432]{2,1,0:T(1,128)S(1)} %reshape.64566), channel_id=1, replica_groups=mesh['ta'=8,'gz'=4] {'ta'}, dimensions={0} | all-to-all | bytes 1179648 | tf_op jit(solution)/shard_map/all_to_all | solution.py:244
  238.4 12.4 %all-to-all-done.3 = f32[4,1,36864]{2,1,0:T(1,128)} async-done(((f32[4,1,36864]{2,1,0:T(1,128)}), f32[4,1,36864]{2,1,0:T(1,128)}, u32[]{:S(2)}, u32[]{:S(2)}) %all-to-all-start.3) | async-done | bytes 589856 | tf_op jit(solution)/shard_map/all_to_all | solution.py:243
  264.8 17.5 %convolution_multiply_fusion.1 = f32[72,2048]{1,0:T(8,128)S(1)} fusion(f32[72,2048]{1,0:T(8,128)S(1)} %reshape.63778, f32[1024,1024]{0,1:T(8,128)} %get-tuple-element.171, f32[1024,1024]{0,1:T(8,128)} %get-tuple-element.170, f32[1024,1024]{0,1:T(8,128)} %get-tuple-element.169), kind=kOutput, calls=%fused_computation.23 | convolution fusion | flops 3636609024 | bytes 13762560 | tf_op jit(solution)/shard_map/rq,pq->rp/dot_general | solution.py:186
  303.6 10.5 %collective-permute-done.5 = f32[2,3,3,3,1,1024]{5,4,1,2,3,0:T(1,128)S(1)} collective-permute-done((f32[2,3,3,3,1,1024]{5,4,1,2,3,0:T(1,128)S(1)}, f32[2,3,3,3,1,1024]{5,4,1,2,3,0:T(1,128)S(1)}, u32[]{:S(2)}, u32[]{:S(2)}) %collective-permute-start.5) | collective-permute-done | bytes 221216 | tf_op jit(solution)/shard_map/ppermute | solution.py:26
  327.6 16.4 %convolution_bitcast_fusion = f32[9,1,8,2,1024]{4,2,3,0,1:T(8,128)S(1)} fusion(f32[9,8,2048,1]{2,1,3,0:T(8,128)S(1)} %bitcast.5511, f32[2,1024,2048,1]{2,1,0,3:T(8,128)S(1)} %bitcast.5411), kind=kOutput, calls=%fused_computation.53 | convolution fusion | flops 3623878656 | bytes 17956864 | tf_op jit(solution)/shard_map/dot_general | solution.py:181
  358.2 13.1 %all_to_all.139 = f32[8,1,18432]{2,1,0:T(1,128)S(1)} all-to-all(f32[8,1,18432]{2,1,0:T(1,128)S(1)} %reshape.64570), channel_id=1, replica_groups=mesh['ta'=8,'gz'=4] {'ta'}, dimensions={0} | all-to-all | bytes 1179648 | tf_op jit(solution)/shard_map/all_to_all | solution.py:225
  373.2 12.4 %reshape.64571 = f32[1024,1,2,8,9]{4,3,2,1,0:T(8,128)} reshape(f32[8,18432]{1,0:T(8,128)S(1)} %reduce.12) | data formatting | bytes 1179648
  401.5 18.9 %all_to_all.140 = f32[4,1,36864]{2,1,0:T(1,128)S(1)} all-to-all(f32[4,1,36864]{2,1,0:T(1,128)S(1)} %reshape.64572), channel_id=1, replica_groups=mesh['ta'=8,'gz'=4] {'gz'}, dimensions={0} | all-to-all | bytes 1179648 | tf_op jit(solution)/shard_map/all_to_all | solution.py:224
  422.6 12.4 %reshape.64573 = f32[128,8,2,8,9]{4,3,2,1,0:T(8,128)} reshape(f32[4,36864]{1,0:T(4,128)S(1)} %reduce.13) | data formatting | bytes 1179648
  435.1 8.1 %copy.3859 = f32[9,8,8,2,4,32]{5,4,2,3,1,0:T(4,128)} copy(f32[9,8,8,2,4,32]{0,2,3,1,5,4:T(8,128)} %bitcast.5404) | data formatting | bytes 1179648 | tf_op jit(solution)/shard_map/all_to_all | solution.py:224
  462.3 12.8 %all_to_all.141 = f32[8,1,18432]{2,1,0:T(1,128)S(1)} all-to-all(f32[8,1,18432]{2,1,0:T(1,128)S(1)} %reshape.64574), channel_id=1, replica_groups=mesh['ta'=8,'gz'=4] {'ta'}, dimensions={0} | all-to-all | bytes 1179648 | tf_op jit(solution)/shard_map/all_to_all | solution.py:244
  481.7 18.7 %all_to_all.142 = f32[4,1,36864]{2,1,0:T(1,128)S(1)} all-to-all(f32[4,1,36864]{2,1,0:T(1,128)S(1)} %reshape.64576), channel_id=1, replica_groups=mesh['ta'=8,'gz'=4] {'gz'}, dimensions={0} | all-to-all | bytes 1179648 | tf_op jit(solution)/shard_map/all_to_all | solution.py:243
  507.4 17.7 %convolution_multiply_fusion = f32[72,2048]{1,0:T(8,128)S(1)} fusion(f32[72,2048]{1,0:T(8,128)S(1)} %reshape.63784, f32[1024,1024]{0,1:T(8,128)} %get-tuple-element.171, f32[1024,1024]{0,1:T(8,128)} %get-tuple-element.170, f32[1024,1024]{0,1:T(8,128)} %get-tuple-element.169), kind=kOutput, calls=%fused_computation.22 | convolution fusion | flops 3636609024 | bytes 13762560 | tf_op jit(solution)/shard_map/rq,pq->rp/dot_general | solution.py:186
  536.2 12.2 %collective-permute-done.6 = f32[2,3,3,1,8,1024]{5,4,2,1,3,0:T(8,128)S(1)} collective-permute-done((f32[2,3,3,1,8,1024]{5,4,2,1,3,0:T(8,128)S(1)}, f32[2,3,3,1,8,1024]{5,4,2,1,3,0:T(8,128)S(1)}, u32[]{:S(2)}, u32[]{:S(2)}) %collective-permute-start.6) | collective-permute-done | bytes 589856 | tf_op jit(solution)/shard_map/ppermute | solution.py:23
  (872 shorter events, 233.3 us)
Async XLA Ops:
  3.0 44.8 %collective-permute-start.1 = (f32[2,3,3,8,1024]{4,3,2,1,0:T(8,128)}, f32[2,3,3,8,1024]{4,3,2,1,0:T(8,128)S(1)}, u32[]{:S(2)}, u32[]{:S(2)}) collective-permute-start(f32[2,3,3,8,1024]{4,3,2,1,0:T(8,128)} %get-tuple-element.30), channel_id=1, source_target_pairs={{28,0},{0,4},{4,8},{8,12},{12,16},{16,20},{20,24},{24,28},{29,1},{... | collective-permute-start | bytes 1769480 | tf_op jit(solution)/shard_map/ppermute | solution.py:14
  4.1 43.6 %collective-permute-start = (f32[2,3,3,1,1024]{4,3,2,1,0:T(1,128)}, f32[2,3,3,1,1024]{4,3,2,1,0:T(1,128)}, u32[]{:S(2)}, u32[]{:S(2)}) collective-permute-start(f32[2,3,3,1,1024]{4,3,2,1,0:T(1,128)} %slice_bitcast_fusion.33), channel_id=1, source_target_pairs={{3,0},{0,1},{1,2},{2,3},{7,4},{4,5},{5,6},{6,7},{11,8},{8,9},{9,10... | collective-permute-start | bytes 221192 | tf_op jit(solution)/shard_map/ppermute | solution.py:14
  37.0 10.7 %copy-start.37 = (f32[2,3,3,1,8,1024]{5,4,2,1,0,3:T(8,128)S(1)}, f32[2,3,3,1,8,1024]{5,4,2,1,0,3:T(8,128)}, u32[]{:S(2)}) copy-start(f32[2,3,3,1,8,1024]{5,4,2,1,0,3:T(8,128)} %get-tuple-element.29) | copy-start | bytes 1769476
  37.0 10.8 %copy-start.38 = (f32[2,3,3,8,1023]{4,3,2,1,0:T(8,128)S(1)}, f32[2,3,3,8,1023]{4,3,2,1,0:T(8,128)}, u32[]{:S(2)}) copy-start(f32[2,3,3,8,1023]{4,3,2,1,0:T(8,128)} %slice_bitcast_fusion.3) | copy-start | bytes 1767748
  37.0 10.8 %copy-start.39 = (f32[2,3,3,8,993]{4,3,2,1,0:T(8,128)S(1)}, f32[2,3,3,8,993]{4,3,2,1,0:T(8,128)}, u32[]{:S(2)}) copy-start(f32[2,3,3,8,993]{4,3,2,1,0:T(8,128)} %slice_bitcast_fusion.4) | copy-start | bytes 1715908
  37.0 10.8 %copy-start.58 = (f32[2,3,3,8,31]{4,3,2,1,0:T(8,128)S(1)}, f32[2,3,3,8,31]{4,3,2,1,0:T(8,128)}, u32[]{:S(2)}) copy-start(f32[2,3,3,8,31]{4,3,2,1,0:T(8,128)} %slice_bitcast_fusion.32) | copy-start | bytes 53572
  37.0 10.8 %copy-start.59 = (f32[2,3,3,8,1]{4,3,2,1,0:T(8,128)S(1)}, f32[2,3,3,8,1]{4,3,2,1,0:T(8,128)}, u32[]{:S(2)}) copy-start(f32[2,3,3,8,1]{4,3,2,1,0:T(8,128)} %copy.3069) | copy-start | bytes 1732
  47.6 6.0 %copy-start.1 = (f32[2048,2048]{0,1:T(8,128)}, f32[2048,2048]{0,1:T(8,128)S(1)}, u32[]{:S(2)}) copy-start(f32[2048,2048]{0,1:T(8,128)S(1)} %maximum_maximum_fusion) | copy-start | bytes 50331652
  84.8 14.2 %all-to-all-start = ((f32[8,1,18432]{2,1,0:T(1,128)}), f32[8,1,18432]{2,1,0:T(1,128)S(1)}, u32[]{:S(2)}, u32[]{:S(2)}) async-start(f32[8,1,18432]{2,1,0:T(1,128)} %reshape.64562), calls=%async_computation | async-start | bytes 1179648 | tf_op jit(solution)/shard_map/all_to_all | solution.py:225
  121.7 15.2 %copy-start.60 = (pred[32]{0:T(512)(128)(4,1)S(1)}, pred[32]{0:T(512)(128)(4,1)}, u32[]{:S(2)}) copy-start(pred[32]{0:T(512)(128)(4,1)} %fusion.771) | copy-start | bytes 100
  130.4 18.7 %all-to-all-start.1 = ((f32[4,1,36864]{2,1,0:T(1,128)}), f32[4,1,36864]{2,1,0:T(1,128)}, u32[]{:S(2)}, u32[]{:S(2)}) async-start(f32[4,1,36864]{2,1,0:T(1,128)} %reshape.64564), calls=%async_computation.1 | async-start | bytes 1179648 | tf_op jit(solution)/shard_map/all_to_all | solution.py:224
  137.0 47.6 %copy-start.6 = (f32[512,512]{0,1:T(8,128)}, f32[512,512]{0,1:T(8,128)S(1)}, u32[]{:S(2)}) copy-start(f32[512,512]{0,1:T(8,128)S(1)} %maximum_maximum_fusion.1) | copy-start | bytes 3145732
  137.1 47.5 %copy-start.56 = (f32[32,256]{1,0:T(8,128)}, f32[32,256]{1,0:T(8,128)S(1)}, u32[]{:S(2)}) copy-start(f32[32,256]{1,0:T(8,128)S(1)} %and_select_fusion) | copy-start | bytes 98308
  230.4 20.5 %all-to-all-start.3 = ((f32[4,1,36864]{2,1,0:T(1,128)}), f32[4,1,36864]{2,1,0:T(1,128)}, u32[]{:S(2)}, u32[]{:S(2)}) async-start(f32[4,1,36864]{2,1,0:T(1,128)} %reshape.64568), calls=%async_computation.3 | async-start | bytes 1179648 | tf_op jit(solution)/shard_map/all_to_all | solution.py:243
  284.2 16.5 %collective-permute-start.2 = (f32[2,3,3,1,8,1024]{5,4,1,2,3,0:T(8,128)S(1)}, f32[2,3,3,1,8,1024]{5,4,1,2,3,0:T(8,128)S(1)}, u32[]{:S(2)}, u32[]{:S(2)}) collective-permute-start(f32[2,3,3,1,8,1024]{5,4,1,2,3,0:T(8,128)S(1)} %pad_maximum_fusion), channel_id=1, source_target_pairs={{0,4},{4,8},{8,12},{12,16},{16,20},{20,24},{24,28},{28,0},{1,5},{5... | collective-permute-start | bytes 1769480 | tf_op jit(solution)/shard_map/ppermute | solution.py:23
  284.3 16.4 %collective-permute-start.3 = (f32[2,3,3,1,8,1024]{5,4,1,2,3,0:T(8,128)S(1)}, f32[2,3,3,1,8,1024]{5,4,1,2,3,0:T(8,128)S(1)}, u32[]{:S(2)}, u32[]{:S(2)}) collective-permute-start(f32[2,3,3,1,8,1024]{5,4,1,2,3,0:T(8,128)S(1)} %pad_maximum_fusion), channel_id=1, source_target_pairs={{4,0},{8,4},{12,8},{16,12},{20,16},{24,20},{28,24},{0,28},{5,1},{9... | collective-permute-start | bytes 1769480 | tf_op jit(solution)/shard_map/ppermute | solution.py:26
  301.0 13.1 %collective-permute-start.5 = (f32[2,3,3,3,1,1024]{5,4,1,2,3,0:T(1,128)S(1)}, f32[2,3,3,3,1,1024]{5,4,1,2,3,0:T(1,128)S(1)}, u32[]{:S(2)}, u32[]{:S(2)}) collective-permute-start(f32[2,3,3,3,1,1024]{5,4,1,2,3,0:T(1,128)S(1)} %get-tuple-element.38), channel_id=1, source_target_pairs={{1,0},{2,1},{3,2},{0,3},{5,4},{6,5},{7,6},{4,7},{9,8},{10,9},{11,1... | collective-permute-start | bytes 663560 | tf_op jit(solution)/shard_map/ppermute | solution.py:26
  302.6 13.6 %collective-permute-start.4 = (f32[2,3,3,3,1,1024]{5,3,4,2,1,0:T(4,128)S(1)}, f32[2,3,3,3,1,1024]{5,3,4,2,1,0:T(4,128)S(1)}, u32[]{:S(2)}, u32[]{:S(2)}) collective-permute-start(f32[2,3,3,3,1,1024]{5,3,4,2,1,0:T(4,128)S(1)} %copy.3863), channel_id=1, source_target_pairs={{0,1},{1,2},{2,3},{3,0},{4,5},{5,6},{6,7},{7,4},{8,9},{9,10},{10,1... | collective-permute-start | bytes 663560 | tf_op jit(solution)/shard_map/ppermute | solution.py:23
  316.0 10.3 %slice-start = ((s8[16777216]{0:T(1024)(128)(4,1)}), s8[4194304]{0:T(1024)(128)(4,1)S(1)}, s32[]{:S(2)}) async-start(s8[16777216]{0:T(1024)(128)(4,1)} %bitcast.5409), calls=%async_computation.8 | async-start | bytes 8388608
  317.9 8.4 %slice-start.1 = ((s8[16777216]{0:T(1024)(128)(4,1)}), s8[4194304]{0:T(1024)(128)(4,1)S(1)}, s32[]{:S(2)}) async-start(s8[16777216]{0:T(1024)(128)(4,1)} %bitcast.5409), calls=%async_computation.9 | async-start | bytes 8388608
  321.2 5.1 slice-start.2
  531.9 16.5 %collective-permute-start.6 = (f32[2,3,3,1,8,1024]{5,4,2,1,3,0:T(8,128)S(1)}, f32[2,3,3,1,8,1024]{5,4,2,1,3,0:T(8,128)S(1)}, u32[]{:S(2)}, u32[]{:S(2)}) collective-permute-start(f32[2,3,3,1,8,1024]{5,4,2,1,3,0:T(8,128)S(1)} %pad_maximum_fusion.1), channel_id=1, source_target_pairs={{0,4},{4,8},{8,12},{12,16},{16,20},{20,24},{24,28},{28,0},{1,5},{5... | collective-permute-start | bytes 1769480 | tf_op jit(solution)/shard_map/ppermute | solution.py:23
  531.9 16.4 %collective-permute-start.7 = (f32[2,3,3,1,8,1024]{5,4,2,1,3,0:T(8,128)S(1)}, f32[2,3,3,1,8,1024]{5,4,2,1,3,0:T(8,128)S(1)}, u32[]{:S(2)}, u32[]{:S(2)}) collective-permute-start(f32[2,3,3,1,8,1024]{5,4,2,1,3,0:T(8,128)S(1)} %pad_maximum_fusion.1), channel_id=1, source_target_pairs={{4,0},{8,4},{12,8},{16,12},{20,16},{24,20},{28,24},{0,28},{5,1},{9... | collective-permute-start | bytes 1769480 | tf_op jit(solution)/shard_map/ppermute | solution.py:26
  548.5 6.8 %collective-permute-start.8 = (f32[2,3,3,3,1,1024]{5,4,2,1,3,0:T(1,128)S(1)}, f32[2,3,3,3,1,1024]{5,4,2,1,3,0:T(1,128)S(1)}, u32[]{:S(2)}, u32[]{:S(2)}) collective-permute-start(f32[2,3,3,3,1,1024]{5,4,2,1,3,0:T(1,128)S(1)} %pad_maximum_fusion.21), channel_id=1, source_target_pairs={{1,0},{2,1},{3,2},{0,3},{5,4},{6,5},{7,6},{4,7},{9,8},{10,9},{11,1... | collective-permute-start | bytes 663560 | tf_op jit(solution)/shard_map/ppermute | solution.py:26
  (53 other events, 105.8 us)
where the time goes:
time: 565 us; the launch traced here: 559 us
  local copies, waits for them, and re-layouts  224 us (40%)
  other arithmetic  88.1 us (16%)
  blocking collectives  77.8 us (14%)
  matrix products  74.4 us (13%)
  waiting for transfers between devices  64.3 us (11%)
  starting transfers between devices  24.9 us (4%)
    unnamed x153, local copies, waits for them, and re-layouts  116 us
    dot_general x4, matrix products, backward_apply(): jnp.einsum('rq,pq->rp', rows, table, precision=lax.Precision.HIGHEST, pre...  38.3 us
    dot_general x4, matrix products, forward_apply(): jnp.dot(rows, table, precision=lax.Precision.HIGHEST, preferred_element_t...  36.1 us
    all_to_all x2, blocking collectives, smooth_field(): lax.all_to_all(spectral, 'ta', split_axis=1, concat_axis=4, tiled=True)  27.1 us
    neg x2, other arithmetic, dense_table(): -sine_value  24.2 us
    all_to_all x4, local copies, waits for them, and re-layouts, smooth_field(): lax.all_to_all(lax.all_to_all(plane, 'ta', split_axis=4, concat_axis=1, t...  21.5 us
    all_to_all x1, blocking collectives, smooth_field(): lax.all_to_all(lax.all_to_all(plane, 'ta', split_axis=4, concat_axis=1, t...  18.9 us
    all_to_all x1, blocking collectives, smooth_field(): lax.all_to_all(lax.all_to_all(spectral, 'ta', split_axis=1, concat_axis=4...  18.7 us
  transfers between devices with their start and end apart: 12, of which 7 were waited for; matrix products, arithmetic and copies ran while one was open for 11% of the time, Pallas kernels for 0%

commit v1 on v0

v1 whole, which is shorter than its diff:
```python
import functools

import jax
import jax.numpy as jnp
import ml_dtypes
import numpy as np
from jax import lax
from jax.experimental import pallas as pl
from jax.experimental.pallas import tpu as pltpu
from jax.sharding import PartitionSpec as P

LX = 32
LY = 32
ITERS = 2
LANES = 128
COMPS = 8
VMEM_LIMIT = 24 * 1024 * 1024


def hartley(length):
    index = np.arange(length)
    angles = 2.0 * np.pi * (np.outer(index, index) % length) / length
    return np.cos(angles) + np.sin(angles)


def split_table(table):
    single = table.astype(np.float32)
    high = single.astype(ml_dtypes.bfloat16)
    low = (single - high.astype(np.float32)).astype(ml_dtypes.bfloat16)
    return np.stack([high, low])


def wave_order():
    modes = np.arange(LY)
    return np.concatenate([modes[modes % 2 == 1], modes[modes % 4 == 2], modes[modes % 4 == 0]])


def padded(table, rows, columns):
    return np.pad(table, ((0, rows - table.shape[0]), (0, columns - table.shape[1])))


def rounded_up(count):
    return -(-count // 16) * 16


def line_tables(time_length, depth_length):
    half = depth_length // 2
    along_t = hartley(time_length) / np.sqrt(time_length)
    along_z = hartley(depth_length) / np.sqrt(depth_length)
    same_t = np.eye(time_length)
    forward = np.concatenate([np.kron(along_t, along_z[:, :half]), np.kron(along_t, along_z[:, half : half + 1])], axis=1)
    edges = np.concatenate([np.kron(same_t, along_z[z : z + 1]) for z in (half, 0)], axis=0)
    inward = np.kron(along_t, along_z[:half])
    spread = np.zeros((time_length, half + 1, half + 1, time_length))
    for z in range(half + 1):
        spread[:, z, z, :] = along_t
    spread = np.concatenate([spread[:, :half].reshape(time_length * half, -1), spread[:, half].reshape(time_length, -1)])
    forward = padded(forward, forward.shape[0], rounded_up(forward.shape[1]))
    spread = padded(spread, rounded_up(spread.shape[0]), rounded_up(spread.shape[1]))
    return [jnp.asarray(split_table(t)) for t in (forward, edges, inward, spread)]


def response_table(time_length, depth_length, plane_sum):
    half = depth_length // 2
    total = plane_sum[:, None, :] + eigenvalues(time_length)[None, :, None]
    cosh = 1.0 + 0.5 * total
    ratio = 1.0 / (cosh + np.sqrt(cosh * cosh - 1.0))
    out = []
    below = np.where(total == 0.0, 1.0, 1.0 - ratio ** (2 * half))
    for z in range(half + 1):
        left = half - z
        out.append(np.where(total == 0.0, left / half, ratio**z * (1.0 - ratio ** (2 * left)) / below))
    return jnp.asarray(np.stack(out, axis=1).astype(np.float32))


def eigenvalues(length):
    return 4.0 * np.sin(np.pi * np.arange(length) / length) ** 2


def split_high_low(value):
    high = value.astype(jnp.bfloat16)
    low = (value - high.astype(jnp.float32)).astype(jnp.bfloat16)
    return high, low


def dot(left, right):
    return lax.dot_general(
        left, right, (((1,), (0,)), ((), ())), preferred_element_type=jnp.float32
    )


def product(left, right):
    rows = len(left)
    out = []
    for i in range(rows):
        row = []
        for j in range(3):
            real = None
            imag = None
            for k in range(3):
                ar, ai = left[i][k]
                br, bi = right[k][j]
                tr = ar * br - ai * bi
                ti = ar * bi + ai * br
                real = tr if real is None else real + tr
                imag = ti if imag is None else imag + ti
            row.append((real, imag))
        out.append(row)
    return out


def product_adjoint(left, right):
    rows = len(left)
    out = []
    for i in range(rows):
        row = []
        for j in range(3):
            real = None
            imag = None
            for k in range(3):
                ar, ai = left[i][k]
                br, bi = right[j][k]
                tr = ar * br + ai * bi
                ti = ai * br - ar * bi
                real = tr if real is None else real + tr
                imag = ti if imag is None else imag + ti
            row.append((real, imag))
        out.append(row)
    return out


def conjugate_cross(first, second):
    out = []
    for position in range(3):
        f = (position + 1) % 3
        b = (position + 2) % 3
        (afr, afi), (abr, abi) = first[f], first[b]
        (bfr, bfi), (bbr, bbi) = second[f], second[b]
        real = afr * bbr - afi * bbi - (abr * bfr - abi * bfi)
        imag = afr * bbi + afi * bbr - (abr * bfi + abi * bfr)
        out.append((real, -imag))
    return out


def norm_factor(row):
    total = None
    for real, imag in row:
        term = real * real + imag * imag
        total = term if total is None else total + term
    guess = lax.rsqrt(total)
    return guess * (1.5 - (0.5 * total) * (guess * guess))


def exponential(comps):
    ar, ai, br, bi, cr, ci, d0, d1 = [0.04 * v for v in comps]
    d2 = -(d0 + d1)
    a2 = ar * ar + ai * ai
    b2 = br * br + bi * bi
    c2 = cr * cr + ci * ci
    s00 = -(d0 * d0 + a2 + b2)
    s11 = -(d1 * d1 + a2 + c2)
    s01r = d2 * ai - (br * cr + bi * ci)
    s01i = -d2 * ar - (bi * cr - br * ci)
    s02r = d1 * bi + (ar * cr - ai * ci)
    s02i = -d1 * br + (ar * ci + ai * cr)
    s12r = d0 * ci - (ar * br + ai * bi)
    s12i = -d0 * cr - (ar * bi - ai * br)
    r0 = [
        (1.0 + 0.5 * s00, d0),
        (ar + 0.5 * s01r, ai + 0.5 * s01i),
        (br + 0.5 * s02r, bi + 0.5 * s02i),
    ]
    r1 = [
        (-ar + 0.5 * s01r, ai - 0.5 * s01i),
        (1.0 + 0.5 * s11, d1),
        (cr + 0.5 * s12r, ci + 0.5 * s12i),
    ]
    factor = norm_factor(r0)
    u0 = [(x * factor, y * factor) for x, y in r0]
    pr = None
    pi = None
    for (x, y), (z, w) in zip(u0, r1):
        tr = x * z + y * w
        ti = x * w - y * z
        pr = tr if pr is None else pr + tr
        pi = ti if pi is None else pi + ti
    v = [(z - (pr * x - pi * y), w - (pr * y + pi * x)) for (x, y), (z, w) in zip(u0, r1)]
    factor = norm_factor(v)
    u1 = [(x * factor, y * factor) for x, y in v]
    return [u0, u1, conjugate_cross(u0, u1)]


def gradient_part(link):
    third = (link[0][0][1] + link[1][1][1] + link[2][2][1]) * (1.0 / 3.0)
    out = []
    for i, j in ((0, 1), (0, 2), (1, 2)):
        out.append(0.5 * (link[i][j][0] - link[j][i][0]))
        out.append(0.5 * (link[i][j][1] + link[j][i][1]))
    out.append(link[0][0][1] - third)
    out.append(link[1][1][1] - third)
    return out


def flat(matrix):
    return [part for row in matrix for entry in row for part in entry]


def unflat(values):
    return [[(values[6 * i + 2 * j], values[6 * i + 2 * j + 1]) for j in range(3)] for i in range(3)]


def lane_index(shape):
    return lax.broadcasted_iota(jnp.int32, shape, len(shape) - 1)


def row_index(shape):
    return lax.broadcasted_iota(jnp.int32, shape, len(shape) - 2)


def from_x_before(value, edge):
    return jnp.where(edge, pltpu.roll(value, LANES - LX + 1, 1), pltpu.roll(value, 1, 1))


def from_x_after(value, edge):
    return jnp.where(edge, pltpu.roll(value, LX - 1, 1), pltpu.roll(value, LANES - 1, 1))


def load_link(ref, mu, at):
    return [[(ref[mu, 0, i, j, 0, :, at], ref[mu, 1, i, j, 0, :, at]) for j in range(3)] for i in range(3)]


def store_link(ref, mu, at, link):
    for i in range(3):
        for j in range(3):
            ref[mu, 0, i, j, 0, :, at] = link[i][j][0]
            ref[mu, 1, i, j, 0, :, at] = link[i][j][1]


def rotated_link(gauge, link, beyond):
    rows = product_adjoint(product(gauge[:2], link), beyond)
    return rows + [conjugate_cross(rows[0], rows[1])]


def chunk_at(step):
    return pl.ds(pl.multiple_of(step * LANES, LANES), LANES)


def dot_split(value, table_ref, group):
    rows = value.shape[0]
    high, low = split_high_low(value)
    half = table_ref.shape[2]
    quarter = half // 2
    if group == 0:
        at = (slice(0, half), slice(0, half))
    else:
        at = (slice(half, half + quarter), slice((group - 1) * quarter, group * quarter))
    both = dot(jnp.concatenate([high, low], axis=0), table_ref[(0,) + at])
    return both[:rows] + both[rows:] + dot(high, table_ref[(1,) + at])


def to_modes(value, table_ref):
    sites = value.shape[1]
    half = sites // 2
    quarter = sites // 4
    lower, upper = value[:, :half], value[:, half:]
    summed, differs = lower + upper, lower - upper
    lower, upper = summed[:, :quarter], summed[:, quarter:]
    parts = (differs, lower - upper, lower + upper)
    return [dot_split(part, table_ref, n) for n, part in enumerate(parts)]


def to_sites(value, table_ref):
    sites = value.shape[1]
    half = sites // 2
    quarter = sites // 4
    parts = (value[:, :half], value[:, half : half + quarter], value[:, half + quarter :])
    odd, two, zero = [dot_split(part, table_ref, n) for n, part in enumerate(parts)]
    even = jnp.concatenate([zero + two, zero - two], axis=1)
    return jnp.concatenate([even + odd, even - odd], axis=1)


def send_modes(space_ref, time_ref, edge_ref, table_ref, out_ref):
    columns, group_count, _, comps, width = out_ref.shape
    sites = space_ref.shape[2]
    rows = 8 * COMPS
    value = jnp.concatenate([r[...].reshape(-1, sites) for r in (space_ref, time_ref, edge_ref)], axis=0)
    start = 0
    for part in to_modes(value, table_ref):
        for inner in range(0, part.shape[1], width):
            column = (start + inner) // width
            piece = part[:, inner : inner + width]
            for g in range(group_count):
                size = 8 * comps
                space = piece[g * size : (g + 1) * size]
                time = piece[rows + g * size : rows + (g + 1) * size]
                out_ref[column, g, 0:8] = space.reshape(8, comps, width)
                out_ref[column, g, 8:16] = time.reshape(8, comps, width)
                out_ref[column, g, 16] = piece[2 * rows + 8 * g : 2 * rows + 8 * g + comps]
        start += part.shape[1]


def cosine_and_sine(count, length):
    angle = (2.0 * np.pi / length) * lax.rem(count, length).astype(jnp.float32)
    return np.sqrt(2.0) * jnp.cos(angle - 0.25 * np.pi)


def fill_plane_table(table_ref, backward):
    _, rows, columns = table_ref.shape
    blocks = rows // LX
    half, quarter = LY // 2, LY // 4
    row = lax.broadcasted_iota(jnp.int32, (blocks, columns), 0)
    column = lax.broadcasted_iota(jnp.int32, (blocks, columns), 1) // LX
    lower = row - half
    if backward:
        odd = (2 * row + 1) * column
        two = (4 * lower + 2) * column
        zero = (4 * lower) * (column - quarter)
    else:
        odd = row * (2 * column + 1)
        two = lower * (4 * column + 2)
        zero = lower * (4 * (column - quarter))
    count = jnp.where(row < half, odd, jnp.where(column < quarter, two, zero))
    along_y = cosine_and_sine(count, LY)
    x = lax.broadcasted_iota(jnp.int32, (LX, LANES), 0)
    mode = lax.broadcasted_iota(jnp.int32, (LX, LANES), 1) % LX
    along_x = cosine_and_sine(x * mode, LX) * (1.0 / np.sqrt(LX * LY))
    along_x = jnp.concatenate([along_x] * (columns // LANES), axis=1)
    for block in range(blocks):
        high, low = split_high_low(along_y[block : block + 1] * along_x)
        table_ref[0, block * LX : (block + 1) * LX, :] = high
        table_ref[1, block * LX : (block + 1) * LX, :] = low


def store_edges(edge_ref, at, part_z, row):
    group_count = edge_ref.shape[0]
    comps = COMPS // group_count
    for g in range(group_count):
        tile = jnp.zeros_like(part_z[0])
        for j in range(comps):
            tile = jnp.where(row == j, pltpu.roll(part_z[g * comps + j], j + 1, 0), tile)
        edge_ref[g, :, at] = tile


def add_y_difference(space_ref, y_ref):
    for c in range(COMPS):
        part = y_ref[c]
        space_ref[c] = space_ref[c] + pltpu.roll(part, LX, 1) - part


def first_gradient_kernel(
    links_hbm, links_ref, table_ref, out_ref, space_ref, time_ref, edge_ref, y_ref, arrived
):
    copies = [pltpu.make_async_copy(links_hbm.at[mu], links_ref.at[mu], arrived.at[mu]) for mu in range(4)]
    for copy in copies:
        copy.start()
    fill_plane_table(table_ref, False)
    chunks = links_ref.shape[-1] // LANES
    shape = (8, LANES)

    def along_x(step, carry):
        at = chunk_at(step)
        first_x = lane_index(shape) % LX == 0
        part = gradient_part(load_link(links_ref, 0, at))
        for c in range(COMPS):
            space_ref[c, :, at] = from_x_before(part[c], first_x) - part[c]
        return carry

    def along_y(step, carry):
        at = chunk_at(step)
        part = gradient_part(load_link(links_ref, 1, at))
        for c in range(COMPS):
            y_ref[c, :, at] = part[c]
        return carry

    def along_z(step, carry):
        at = chunk_at(step)
        row = row_index(shape)
        part = gradient_part(load_link(links_ref, 2, at))
        for c in range(COMPS):
            behind = jnp.where(row == 0, 0.0, pltpu.roll(part[c], 1, 0))
            space_ref[c, :, at] = space_ref[c, :, at] + (behind - part[c])
        store_edges(edge_ref, at, part, row)
        return carry

    def along_t(step, carry):
        at = chunk_at(step)
        part = gradient_part(load_link(links_ref, 3, at))
        for c in range(COMPS):
            time_ref[c, :, at] = part[c]
            space_ref[c, :, at] = space_ref[c, :, at] - part[c]
        return carry

    for mu, body in enumerate((along_x, along_y, along_z, along_t)):
        copies[mu].wait()
        lax.fori_loop(0, chunks, body, 0, unroll=4)
    add_y_difference(space_ref, y_ref)
    send_modes(space_ref, time_ref, edge_ref, table_ref, out_ref)


def table_product(table_ref, value):
    high, low = split_high_low(value)
    table = table_ref[0]
    return dot(table, high) + dot(table, low) + dot(table_ref[1], high)


def group_of_device(time_axis, depth_axis, group_count):
    half = lax.axis_size(depth_axis) // 2
    return (lax.axis_index(time_axis) * half + lax.rem(lax.axis_index(depth_axis), half)) // group_count


def modes_kernel(
    group_count, half_devices, spectral_ref, table_ref, edges_ref, line_ref, plane_ref, modes_ref, sent_ref, total_ref
):
    count, _, comps, width = spectral_ref.shape
    times = count // half_devices
    lines = count * 8
    group = group_of_device("ta", "gz", group_count)
    row = row_index((count, 8, width))
    space = spectral_ref[:, 0:8].reshape(count, 8 * comps, width)
    time = spectral_ref[:, 8:16].reshape(count, 8 * comps, width)
    time = jnp.concatenate([time[-half_devices:], time[:-half_devices]], axis=0)
    edge = spectral_ref[:, 16].reshape(times, half_devices, comps, width)
    beyond = edge[:, half_devices - 1]
    edge = jnp.concatenate([jnp.zeros_like(edge[:, :1]), edge[:, :-1]], axis=1).reshape(count, comps, width)
    pieces = []
    for c in range(comps):
        at = slice(8 * c, 8 * c + 8)
        first = jnp.where(row == 0, jnp.broadcast_to(edge[:, c : c + 1], row.shape), 0.0)
        own = (space[:, at] + time[:, at] + first).reshape(lines, width)
        after = beyond[:, c : c + 1].reshape(times, width)
        rest = table_ref.shape[2] - lines - times
        tail = [jnp.zeros((rest, width), jnp.float32)] if rest else []
        pieces.append(jnp.concatenate([own, after] + tail, axis=0))
    data = pieces[0] if comps == 1 else jnp.concatenate(pieces, axis=1)
    data = table_product(table_ref, data)
    summed = line_ref[...] + plane_ref[group]
    weight = jnp.where(summed == 0.0, 0.0, 16.0 / jnp.where(summed == 0.0, 1.0, summed))
    anchor = jnp.where(summed[0:8] == 0.0, 1.0, 0.0)
    if comps > 1:
        weight = jnp.concatenate([weight] * comps, axis=1)
        anchor = jnp.concatenate([anchor] * comps, axis=1)
    total_ref[...] = data[0:8] * anchor
    data = data * weight
    modes_ref[...] = data
    sent_ref[...] = table_product(edges_ref, data)


def inward_kernel(modes_ref, table_ref, own_ref, *plane_refs):
    own_ref[...] = table_product(table_ref, modes_ref[...])
    for plane_ref in plane_refs:
        fill_plane_table(plane_ref, True)


def halves_of_next_pair(own, half_devices):
    pairs = own.reshape((-1, 2, half_devices) + own.shape[1:])
    following = jnp.concatenate([pairs[1:, 0], pairs[:1, 0]], axis=0)
    halves = jnp.stack([following[:, :, :4], following[:, :, 4:]], axis=1)
    return halves.reshape((own.shape[0], 4, own.shape[2]))


def couple_kernel(
    group_count, half_devices, own_ref, sent_ref, arrived_ref, total_ref, response_ref, table_ref, out_ref
):
    count, _, comps, width = out_ref.shape
    times = count // half_devices
    sites = 8 * half_devices
    columns = own_ref.shape[1]
    group = group_of_device("ta", "gz", group_count)
    first = arrived_ref[0:times]
    after_last = arrived_ref[times:]
    total = total_ref[...]
    if times > 8:
        total = jnp.concatenate([total, jnp.zeros((times - 8, columns), jnp.float32)], axis=0)
    response = [response_ref[group, z] for z in range(sites + 1)]
    if comps > 1:
        response = [jnp.concatenate([r] * comps, axis=1) for r in response]
    rows = []
    for z in range(sites):
        left = sites - z
        bend = 16.0 / (2.0 * sites) ** 0.5 * 0.5 * z * left
        value = response[z] * first
        if z:
            value = value + response[left] * after_last + bend * total
        rows.append(value)
    rows.append(after_last + sent_ref[0:times])
    rest = table_ref.shape[2] - (sites + 1) * times
    if rest:
        rows.append(jnp.zeros((rest, columns), jnp.float32))
    spread = table_product(table_ref, jnp.concatenate(rows, axis=0))
    lines = times * sites
    data = own_ref[...] + spread[:lines]
    beyond = spread[lines : lines + times]
    every = []
    later = []
    follows = []
    for c in range(comps):
        at = slice(c * width, (c + 1) * width)
        own = data[:, at].reshape(count, 8, width)
        every.append(own)
        later.append(halves_of_next_pair(own, half_devices))
        inner = own.reshape(times, half_devices, 8, width)[:, 1:, 0:1]
        after = beyond[:, at].reshape(times, 1, 1, width)
        follows.append(jnp.concatenate([inner, after], axis=1).reshape(count, 1, width))
    if comps > 1:
        every = [jnp.concatenate(every, axis=1)]
        later = [jnp.concatenate(later, axis=1)]
        follows = [jnp.concatenate(follows, axis=1)]
    out_ref[:, 0:8] = every[0].reshape(count, 8, comps, width)
    out_ref[:, 8:12] = later[0].reshape(count, 4, comps, width)
    out_ref[:, 12] = follows[0].reshape(count, comps, width)


def smooth_kernel(
    group_count, spectral_ref, table_ref, smooth_ref, after_ref, part_ref, sent_ref, rows_ref
):
    count, _, _, width = spectral_ref.shape
    pieces = ([], [], [])
    for g in range(count // group_count):
        part = spectral_ref[g * group_count : (g + 1) * group_count]
        pieces[0].append(part[:, 0:8].reshape(8 * COMPS, width))
        pieces[1].append(part[:, 8:12].reshape(4 * COMPS, width))
        pieces[2].append(part[:, 12].reshape(COMPS, width))
    total = to_sites(jnp.concatenate([jnp.concatenate(p, axis=1) for p in pieces], axis=0), table_ref)
    sites = total.shape[1]
    rows = 8 * COMPS
    smooth = total[:rows].reshape(COMPS, 8, sites)
    part = total[rows : rows + 4 * COMPS].reshape(COMPS, 4, sites)
    part = jnp.concatenate([part, part], axis=1)
    smooth_ref[...] = smooth
    part_ref[...] = part
    sent_ref[...] = jnp.where(first_core(), part, smooth)
    rows_ref[...] = total[rows + 4 * COMPS :]
    for c in range(COMPS):
        for k in range(sites // LANES):
            after_ref[c, k : k + 1, :] = rows_ref[c : c + 1, k * LANES : (k + 1) * LANES]


def first_core():
    return lax.rem(lax.axis_index("ta"), 2) == 0


def gauge_matrices(smooth_ref, after_ref, gauge_ref, beyond_ref):
    chunks = smooth_ref.shape[-1] // LANES
    beyond = flat(exponential([after_ref[c] for c in range(COMPS)]))
    for n in range(18):
        beyond_ref[n] = beyond[n]

    def matrices(step, carry):
        at = chunk_at(step)
        gauge = flat(exponential([smooth_ref[c, :, at] for c in range(COMPS)]))
        for n in range(18):
            gauge_ref[n, :, at] = gauge[n]
        return carry

    lax.fori_loop(0, chunks, matrices, 0, unroll=4)


def rotate_x(links_ref, at, own):
    last_x = lane_index(own[0].shape) % LX == LX - 1
    return rotated_link(unflat(own), load_link(links_ref, 0, at), unflat([from_x_after(v, last_x) for v in own]))


def rotate_y(links_ref, at, own, gauge_ref, at_next):
    first_y = lane_index(own[0].shape) < LX
    beyond = [pltpu.roll(jnp.where(first_y, gauge_ref[n, :, at_next], own[n]), LANES - LX, 1) for n in range(18)]
    return rotated_link(unflat(own), load_link(links_ref, 1, at), unflat(beyond))


def rotate_z(links_ref, at, own, beyond_ref, step):
    shape = own[0].shape
    row = row_index(shape)
    beyond = [
        jnp.where(row == 7, jnp.broadcast_to(beyond_ref[n, pl.ds(step, 1), :], shape), pltpu.roll(own[n], 7, 0))
        for n in range(18)
    ]
    return rotated_link(unflat(own), load_link(links_ref, 2, at), unflat(beyond))


def turn_time(links_ref, at, own, turned_ref):
    rows = product(unflat(own)[:2], load_link(links_ref, 3, at))
    for n, part in enumerate(flat(rows)):
        turned_ref[n, :, at] = part


def finish_time(turned_ref, part_ref, arrived_ref, at):
    row = row_index((8, LANES))
    arrived = first_core() | (row < 4)
    later = [jnp.where(arrived, arrived_ref[c, :, at], part_ref[c, :, at]) for c in range(COMPS)]
    values = [turned_ref[n, :, at] for n in range(12)]
    rows = [[(values[6 * i + 2 * j], values[6 * i + 2 * j + 1]) for j in range(3)] for i in range(2)]
    rows = product_adjoint(rows, exponential(later))
    return rows + [conjugate_cross(rows[0], rows[1])]


def space_links_kernel(
    links_ref,
    smooth_ref,
    after_ref,
    links_out_ref,
    turned_ref,
    space_ref,
    edge_ref,
    gauge_ref,
    beyond_ref,
    y_ref,
):
    chunks = links_ref.shape[-1] // LANES
    shape = (8, LANES)
    gauge_matrices(smooth_ref, after_ref, gauge_ref, beyond_ref)

    def body(step, carry):
        at = chunk_at(step)
        at_next = chunk_at(lax.rem(step + 1, chunks))
        row = row_index(shape)
        first_x = lane_index(shape) % LX == 0
        own = [gauge_ref[n, :, at] for n in range(18)]
        link = rotate_x(links_ref, at, own)
        store_link(links_out_ref, 0, at, link)
        part = gradient_part(link)
        delta = [from_x_before(part[c], first_x) - part[c] for c in range(COMPS)]
        link = rotate_y(links_ref, at, own, gauge_ref, at_next)
        store_link(links_out_ref, 1, at, link)
        part = gradient_part(link)
        for c in range(COMPS):
            y_ref[c, :, at] = part[c]
        link = rotate_z(links_ref, at, own, beyond_ref, step)
        store_link(links_out_ref, 2, at, link)
        part = gradient_part(link)
        for c in range(COMPS):
            behind = jnp.where(row == 0, 0.0, pltpu.roll(part[c], 1, 0))
            space_ref[c, :, at] = delta[c] + (behind - part[c])
        store_edges(edge_ref, at, part, row)
        turn_time(links_ref, at, own, turned_ref)
        return carry

    lax.fori_loop(0, chunks, body, 0, unroll=2)
    add_y_difference(space_ref, y_ref)


def time_links_kernel(
    turned_ref, part_ref, arrived_ref, space_ref, edge_ref, table_ref, rotated_hold, links_ref, out_ref, sum_ref, time_ref
):
    chunks = arrived_ref.shape[-1] // LANES

    def body(step, carry):
        at = chunk_at(step)
        link = finish_time(turned_ref, part_ref, arrived_ref, at)
        store_link(links_ref, 3, at, link)
        part = gradient_part(link)
        for c in range(COMPS):
            time_ref[c, :, at] = part[c]
            sum_ref[c, :, at] = space_ref[c, :, at] - part[c]
        return carry

    lax.fori_loop(0, chunks, body, 0, unroll=2)
    send_modes(sum_ref, time_ref, edge_ref, table_ref, out_ref)


def last_space_links_kernel(links_ref, smooth_ref, after_ref, out_ref, turned_ref, gauge_ref, beyond_ref):
    chunks = links_ref.shape[-1] // LANES
    gauge_matrices(smooth_ref, after_ref, gauge_ref, beyond_ref)

    def body(step, carry):
        at = chunk_at(step)
        at_next = chunk_at(lax.rem(step + 1, chunks))
        own = [gauge_ref[n, :, at] for n in range(18)]
        store_link(out_ref, 0, at, rotate_x(links_ref, at, own))
        store_link(out_ref, 1, at, rotate_y(links_ref, at, own, gauge_ref, at_next))
        store_link(out_ref, 2, at, rotate_z(links_ref, at, own, beyond_ref, step))
        turn_time(links_ref, at, own, turned_ref)
        return carry

    lax.fori_loop(0, chunks, body, 0, unroll=2)


def last_time_links_kernel(turned_ref, part_ref, arrived_ref, space_ref, out_hbm, time_ref, sent):
    copies = [pltpu.make_async_copy(space_ref, out_hbm.at[0:3], sent.at[0])]
    copies[0].start()
    sites = arrived_ref.shape[-1]
    chunks = sites // LANES

    def body(step, carry):
        at = chunk_at(step)
        store_link(time_ref, 0, at, finish_time(turned_ref, part_ref, arrived_ref, at))
        return carry

    for part in range(2):
        lax.fori_loop(part * chunks // 2, (part + 1) * chunks // 2, body, 0, unroll=2)
        at = pl.ds(part * sites // 2, sites // 2)
        source = time_ref.at[:, :, :, :, :, :, at]
        target = out_hbm.at[3:4, :, :, :, :, :, at]
        copies.append(pltpu.make_async_copy(source, target, sent.at[1 + part]))
        copies[-1].start()
    for copy in copies:
        copy.wait()


def in_vmem():
    return pl.BlockSpec(memory_space=pltpu.VMEM)


def in_hbm():
    return pl.BlockSpec(memory_space=pltpu.HBM)


def shaped(*shape):
    return pltpu.VMEM(shape, jnp.float32)


scratch = shaped


def call(kernel, name, operands, out_specs, out_shape, scratch_shapes=(), in_specs=None, aliases=None):
    if in_specs is None:
        in_specs = [in_vmem()] * len(operands)
    operands = [
        pltpu.with_memory_space_constraint(v, spec.memory_space)
        if spec.memory_space in (pltpu.VMEM, pltpu.HBM)
        else v
        for v, spec in zip(operands, in_specs)
    ]
    return pl.pallas_call(
        kernel,
        in_specs=in_specs,
        out_specs=out_specs,
        out_shape=out_shape,
        scratch_shapes=scratch_shapes,
        input_output_aliases=aliases or {},
        compiler_params=pltpu.CompilerParams(vmem_limit_bytes=VMEM_LIMIT),
        name=name,
    )(*operands)


def passed(block, axis, distance):
    size = lax.axis_size(axis)
    return lax.ppermute(block, axis, [((i - distance) % size, i) for i in range(size)])


def exchanged(block):
    depth = lax.axis_size("gz")
    half = depth // 2
    groups = [
        [t * depth + h * half + z for t in range(lax.axis_size("ta")) for z in range(half)] for h in range(2)
    ]
    return lax.all_to_all(
        block, ("ta", "gz"), split_axis=0, concat_axis=0, axis_index_groups=groups, tiled=True
    )


def on_device(gauge_links):
    local = gauge_links.shape
    sites = local[-1]
    chunks = sites // LANES
    time_devices = lax.axis_size("ta")
    depth_devices = lax.axis_size("gz")
    half_devices = depth_devices // 2
    devices = time_devices * half_devices
    assert local[4] == 1 and local[5] == 8 and ITERS == 2 and depth_devices % 2 == 0 and time_devices % 2 == 0
    time_length = local[4] * time_devices
    depth_length = local[5] * depth_devices
    share = COMPS * sites // devices
    width = min(LANES, share)
    comps = share // width
    group_count = COMPS // comps
    columns = sites // width

    plane_table = pltpu.VMEM((2, sites * 3 // 4, sites // 2), jnp.bfloat16)
    line_forward, line_edges, line_inward, line_spread = line_tables(time_length, depth_length)
    line_sum = (eigenvalues(time_length)[:, None] + eigenvalues(depth_length)[None, :]).reshape(-1, 1)
    line_sum = jnp.asarray(np.broadcast_to(line_sum, (time_length * depth_length, width)).astype(np.float32))
    plane_sum = (eigenvalues(LY)[wave_order()][:, None] + eigenvalues(LX)[None, :]).reshape(columns, width)
    response = response_table(time_length, depth_length, plane_sum)
    plane_sum = jnp.asarray(plane_sum.astype(np.float32).reshape(columns, 1, width))

    field = (COMPS, 8, sites)
    sent_shape = shaped(columns, group_count, 17, comps, width)
    edge_scratch = scratch(group_count, 8, sites)
    links, forward, spectral = call(
        first_gradient_kernel,
        "first_gradient",
        [gauge_links],
        [in_vmem()] * 3,
        [shaped(*local), plane_table, sent_shape],
        [
            scratch(*field),
            scratch(*field),
            edge_scratch,
            scratch(*field),
            pltpu.SemaphoreType.DMA((4,)),
        ],
        in_specs=[in_hbm()],
    )
    for iteration in range(ITERS):
        spectral = exchanged(spectral.reshape(devices, 17, comps, width))
        modes, sent, total = call(
            functools.partial(modes_kernel, group_count, half_devices),
            "filtered_modes",
            [spectral, line_forward, line_edges, line_sum, plane_sum],
            [in_vmem()] * 3,
            [
                shaped(time_length * depth_length, comps * width),
                shaped(2 * time_length, comps * width),
                shaped(8, comps * width),
            ],
        )
        arrived = passed(sent, "gz", half_devices)
        first = iteration == 0
        own, *tables = call(
            inward_kernel,
            "own_half",
            [modes, line_inward],
            [in_vmem()] * (1 + first),
            [shaped(devices * 8, comps * width)] + [plane_table] * first,
        )
        if first:
            backward = tables[0]
        spectral = call(
            functools.partial(couple_kernel, group_count, half_devices),
            "coupled_halves",
            [own, sent, arrived, total, response, line_spread],
            in_vmem(),
            shaped(devices, 13, comps, width),
        )
        spectral = exchanged(spectral)
        smooth, after, part, sent = call(
            functools.partial(smooth_kernel, group_count),
            "smooth_field",
            [spectral, backward],
            [in_vmem()] * 4,
            [shaped(*field), shaped(COMPS, chunks, LANES), shaped(*field), shaped(*field)],
            [scratch(COMPS, sites)],
        )
        arrived = lax.ppermute(sent, "ta", [(t, t + 1 - 2 * (t % 2)) for t in range(time_devices)])
        gauge_scratch = [scratch(18, 8, sites), scratch(18, chunks, LANES)]
        if iteration + 1 < ITERS:
            links, turned, space, edge = call(
                space_links_kernel,
                "space_links",
                [links, smooth, after],
                [in_vmem()] * 4,
                [shaped(*local), shaped(12, 8, sites), shaped(*field), edge_scratch],
                gauge_scratch + [scratch(*field)],
            )
            links, spectral = call(
                time_links_kernel,
                "time_links",
                [turned, part, arrived, space, edge, forward, links],
                [in_vmem()] * 2,
                [shaped(*local), sent_shape],
                [scratch(*field), scratch(*field)],
                aliases={6: 0},
            )
        else:
            space_links, turned = call(
                last_space_links_kernel,
                "last_space_links",
                [links, smooth, after],
                [in_vmem()] * 2,
                [shaped(3, *local[1:]), shaped(12, 8, sites)],
                gauge_scratch,
            )
            rotated = call(
                last_time_links_kernel,
                "last_time_links",
                [turned, part, arrived, space_links],
                in_hbm(),
                pltpu.HBM(local, jnp.float32),
                [scratch(1, *local[1:]), pltpu.SemaphoreType.DMA((3,))],
            )
    return rotated


def solution(mesh):
    in_specs = (P(None, None, None, None, "ta", "gz", None),)
    out_specs = P(None, None, None, None, "ta", "gz", None)
    return jax.shard_map(
        on_device, mesh=mesh, in_specs=in_specs, out_specs=out_specs, check_vma=False
    )
```

time: 565 us -> 75 us (0.13); the launches traced: 559 us -> 74.7 us
  local copies, waits for them, and re-layouts: 224 us -> 0.03 us
  other arithmetic: 88.1 us -> 0 us
  matrix products: 74.4 us -> 0 us
  waiting for transfers between devices: 64.3 us -> 4.48 us
  blocking collectives: 77.8 us -> 51.9 us
  starting transfers between devices: 24.9 us -> 5.4 us
  Pallas kernels: 0 us -> 12.8 us
    unnamed x153 -> x14, local copies, waits for them, and re-layouts: 116 us -> 0.03 us
    dot_general x8 -> x0, matrix products: 74.4 us -> none  [the longest x4 38.3 us: backward_apply(): jnp.einsum('rq,pq->rp', rows, table, precision=lax.Precision.HIGHEST, pre...]
    all_to_all x15 -> x0, local copies, waits for them, and re-layouts: 50.7 us -> none  [the longest x4 21.5 us: smooth_field(): lax.all_to_all(lax.all_to_all(plane, 'ta', split_axis=4, concat_axis=1, t...]
    all_to_all x3 -> x0, waiting for transfers between devices: 34.2 us -> none  [the longest x1 12.4 us: smooth_field(): lax.all_to_all(lax.all_to_all(spectral, 'ta', split_axis=1, concat_axis=4...]
    all_to_all x5 -> x4, blocking collectives: 77.8 us -> 51.9 us  [exchanged(): lax.all_to_all(block, ('ta', 'gz'), split_axis=0, concat_axis=0, axis_ind...]
    ppermute x9 -> x4, waiting for transfers between devices: 30.1 us -> 4.48 us  [the longest x2 4.48 us: passed(): lax.ppermute(block, axis, [((i - distance) % size, i) for i in range(size)])]
    neg x8 -> x0, other arithmetic: 24.7 us -> none  [the longest x2 24.2 us: dense_table(): -sine_value]
    all_to_all x8 -> x0, other arithmetic: 19.5 us -> none  [the longest x2 6.23 us: smooth_field(): lax.all_to_all(lax.all_to_all(plane, 'ta', split_axis=4, concat_axis=1, t...]
  transfers between devices with their start and end apart: 12 -> 4, of which waited for: 7 -> 2; matrix products, arithmetic and copies ran while one was open for 11% -> 0% of each run, Pallas kernels for 0% -> 6%
where the time goes in v1:
time: 75 us; the launch traced here: 74.7 us
  blocking collectives  51.9 us (69%)
  Pallas kernels  12.8 us (17%)
  starting transfers between devices  5.4 us (7%)
  waiting for transfers between devices  4.48 us (6%)
    all_to_all x4, blocking collectives, exchanged(): lax.all_to_all(block, ('ta', 'gz'), split_axis=0, concat_axis=0, axis_ind...  51.9 us
    pallas_call x13, Pallas kernels, call(): pl.pallas_call(kernel, in_specs=in_specs, out_specs=out_specs, out_shape=...  12.8 us
    ppermute x2, starting transfers between devices, passed(): lax.ppermute(block, axis, [((i - distance) % size, i) for i in range(size)])  4.86 us
    ppermute x2, waiting for transfers between devices, passed(): lax.ppermute(block, axis, [((i - distance) % size, i) for i in range(size)])  4.48 us
  transfers between devices with their start and end apart: 4, of which 2 were waited for; matrix products, arithmetic and copies ran while one was open for 0% of the time, Pallas kernels for 6%

profile of v1, /device:TPU:0, one launch (start us, length us, event | category | flops | bytes accessed | tf_op | source)
XLA Modules:
  0.0 74.7 jit_solution(16275267190272974683)
XLA Ops:
  0.0 0.0 copy-start
  0.0 2.4 %first_gradient.1 = (f32[4,2,3,3,1,8,1024]{6,5,4,3,2,1,0:T(8,128)S(1)}, bf16[2,768,512]{2,1,0:T(8,128)(2,1)S(1)}, f32[8,2,17,4,128]{4,3,2,1,0:T(4,128)S(1)}) custom-call(f32[4,2,3,3,1,8,1024]{6,5,4,3,2,1,0:T(8,128)} %links_hbm.1), custom_call_target="tpu_custom_call" | custom-call | tf_op jit(solution)/shard_map/first_gradient/pallas_call | solution.py:722
  2.5 16.9 %all_to_all.20.spectral_ref = f32[16,17,4,128]{3,2,1,0:T(4,128)S(1)} all-to-all(f32[16,17,4,128]{3,2,1,0:T(4,128)S(1)} %bitcast.3), channel_id=1, replica_groups={{0,1,4,5,8,9,12,13,16,17,20,21,24,25,28,29},{2,3,6,7,10,11,14,15,18,19,..., dimensions={0} | all-to-all | bytes 1114112 | tf_op jit(solution)/shard_map/all_to_all | solution.py:745
  19.4 0.6 filtered_modes.2
  20.0 2.6 %collective-permute-start = (f32[16,512]{1,0:T(8,128)S(1)}, f32[16,512]{1,0:T(8,128)S(1)}, u32[]{:S(2)}, u32[]{:S(2)}) collective-permute-start(f32[16,512]{1,0:T(8,128)S(1)} %get-tuple-element.36.sent_ref), channel_id=1, source_target_pairs={{2,0},{3,1},{0,2},{1,3},{6,4},{7,5},{4,6},{5,7},{10,8},{11,9},{8,1... | collective-permute-start | bytes 98312 | tf_op jit(solution)/shard_map/ppermute | solution.py:736
  22.6 0.7 own_half.2
  23.3 1.9 %collective-permute-done.arrived_ref = f32[16,512]{1,0:T(8,128)S(1)} collective-permute-done((f32[16,512]{1,0:T(8,128)S(1)}, f32[16,512]{1,0:T(8,128)S(1)}, u32[]{:S(2)}, u32[]{:S(2)}) %collective-permute-start) | collective-permute-done | bytes 32800 | tf_op jit(solution)/shard_map/ppermute | solution.py:736
  25.2 0.4 coupled_halves.2
  25.5 10.5 %all_to_all.21.spectral_ref = f32[16,13,4,128]{3,2,1,0:T(4,128)S(1)} all-to-all(f32[16,13,4,128]{3,2,1,0:T(4,128)S(1)} %coupled_halves.2), channel_id=1, replica_groups={{0,1,4,5,8,9,12,13,16,17,20,21,24,25,28,29},{2,3,6,7,10,11,14,15,18,19,..., dimensions={0} | all-to-all | bytes 851968 | tf_op jit(solution)/shard_map/all_to_all | solution.py:745
  36.0 0.5 smooth_field.2
  36.6 0.3 collective-permute-start.1
  36.8 2.1 %space_links.1 = (f32[4,2,3,3,1,8,1024]{6,5,4,3,2,1,0:T(8,128)S(1)}, f32[12,8,1024]{2,1,0:T(8,128)S(1)}, f32[8,8,1024]{2,1,0:T(8,128)S(1)}, f32[2,8,1024]{2,1,0:T(8,128)S(1)}) custom-call(f32[4,2,3,3,1,8,1024]{6,5,4,3,2,1,0:T(8,128)S(1)} %get-tuple-element.32.links_ref, f32[8,8,1024]{2,1,0:T(8,128)S(1)} %get-tuple-element.39.smooth_ref, ...), custom_call_target="tpu_custom_call" | custom-call | tf_op jit(solution)/shard_map/space_links/pallas_call | solution.py:722
  38.9 1.1 %time_links.1 = (f32[4,2,3,3,1,8,1024]{6,5,4,3,2,1,0:T(8,128)S(1)}, f32[8,2,17,4,128]{4,3,2,1,0:T(4,128)S(1)}) custom-call(f32[12,8,1024]{2,1,0:T(8,128)S(1)} %get-tuple-element.41.turned_ref, f32[8,8,1024]{2,1,0:T(8,128)S(1)} %get-tuple-element.42.part_ref, f32[8,8,1024]{2,1,0:T(8,128)S(1)} %collective-permute-done.1.arrived_ref, ...), custom_call_target="tpu_custom_call", output_to_operand_aliasing={{0}: (6, {})} | custom-call | tf_op jit(solution)/shard_map/time_links/pallas_call | solution.py:722
  40.0 14.1 %all_to_all.22.spectral_ref = f32[16,17,4,128]{3,2,1,0:T(4,128)S(1)} all-to-all(f32[16,17,4,128]{3,2,1,0:T(4,128)S(1)} %bitcast.2), channel_id=1, replica_groups={{0,1,4,5,8,9,12,13,16,17,20,21,24,25,28,29},{2,3,6,7,10,11,14,15,18,19,..., dimensions={0} | all-to-all | bytes 1114112 | tf_op jit(solution)/shard_map/all_to_all | solution.py:745
  54.1 0.6 filtered_modes.3
  54.7 2.3 %collective-permute-start.2 = (f32[16,512]{1,0:T(8,128)S(1)}, f32[16,512]{1,0:T(8,128)S(1)}, u32[]{:S(2)}, u32[]{:S(2)}) collective-permute-start(f32[16,512]{1,0:T(8,128)S(1)} %get-tuple-element.51.sent_ref), channel_id=1, source_target_pairs={{2,0},{3,1},{0,2},{1,3},{6,4},{7,5},{4,6},{5,7},{10,8},{11,9},{8,1... | collective-permute-start | bytes 98312 | tf_op jit(solution)/shard_map/ppermute | solution.py:736
  57.0 0.3 own_half.3.own_ref
  57.3 2.6 %collective-permute-done.2.arrived_ref = f32[16,512]{1,0:T(8,128)S(1)} collective-permute-done((f32[16,512]{1,0:T(8,128)S(1)}, f32[16,512]{1,0:T(8,128)S(1)}, u32[]{:S(2)}, u32[]{:S(2)}) %collective-permute-start.2) | collective-permute-done | bytes 32800 | tf_op jit(solution)/shard_map/ppermute | solution.py:736
  59.9 0.3 coupled_halves.3
  60.2 10.5 %all_to_all.23.spectral_ref = f32[16,13,4,128]{3,2,1,0:T(4,128)S(1)} all-to-all(f32[16,13,4,128]{3,2,1,0:T(4,128)S(1)} %coupled_halves.3), channel_id=1, replica_groups={{0,1,4,5,8,9,12,13,16,17,20,21,24,25,28,29},{2,3,6,7,10,11,14,15,18,19,..., dimensions={0} | all-to-all | bytes 851968 | tf_op jit(solution)/shard_map/all_to_all | solution.py:745
  70.7 0.5 smooth_field.3
  71.3 0.3 collective-permute-start.3
  71.5 1.7 %last_space_links.1 = (f32[3,2,3,3,1,8,1024]{6,5,4,3,2,1,0:T(8,128)S(1)}, f32[12,8,1024]{2,1,0:T(8,128)S(1)}) custom-call(f32[4,2,3,3,1,8,1024]{6,5,4,3,2,1,0:T(8,128)S(1)} %get-tuple-element.48.links_ref, f32[8,8,1024]{2,1,0:T(8,128)S(1)} %get-tuple-element.53.smooth_ref, f32[8,8,128]{2,1,0:T(8,128)S(1)} %get-tuple-element.54.after_ref), custom_call_target="tpu_custom_call" | custom-call | tf_op jit(solution)/shard_map/last_space_links/pallas_call | solution.py:722
  73.3 1.4 %last_time_links.1 = f32[4,2,3,3,1,8,1024]{6,5,4,3,2,1,0:T(8,128)} custom-call(f32[12,8,1024]{2,1,0:T(8,128)S(1)} %get-tuple-element.55.turned_ref, f32[8,8,1024]{2,1,0:T(8,128)S(1)} %get-tuple-element.56.part_ref, f32[8,8,1024]{2,1,0:T(8,128)S(1)} %collective-permute-done.3.arrived_ref, f32[3,2,3,3,1,8,1024]{6,5,4,3,2,1,0:T(8,128)S(1)} %get-tuple-element.58.space_ref), custom_call_target="tpu_custom_call" | custom-call | tf_op jit(solution)/shard_map/last_time_links/pallas_call | solution.py:722
  (15 shorter events, 0.0 us)
Async XLA Ops:
  0.0 19.4 %copy-start.6 = (f32[8,1,128]{2,1,0:T(1,128)S(1)}, f32[8,1,128]{2,1,0:T(1,128)}, u32[]{:S(2)}) copy-start(f32[8,1,128]{2,1,0:T(1,128)} %constant.20.clone.plane_ref) | copy-start | bytes 12292
  0.0 19.4 %copy-start.4 = (f32[256,128]{1,0:T(8,128)S(1)}, f32[256,128]{1,0:T(8,128)}, u32[]{:S(2)}) copy-start(f32[256,128]{1,0:T(8,128)} %constant.18.clone.line_ref) | copy-start | bytes 393220
  0.0 19.4 %copy-start.5 = (bf16[2,16,256]{2,1,0:T(8,128)(2,1)S(1)}, bf16[2,16,256]{2,1,0:T(8,128)(2,1)}, u32[]{:S(2)}) copy-start(bf16[2,16,256]{2,1,0:T(8,128)(2,1)} %constant.15.clone.edges_ref) | copy-start | bytes 49156
  0.0 19.4 %copy-start.1 = (bf16[2,256,144]{2,1,0:T(8,128)(2,1)S(1)}, bf16[2,256,144]{2,1,0:T(8,128)(2,1)}, u32[]{:S(2)}) copy-start(bf16[2,256,144]{2,1,0:T(8,128)(2,1)} %constant.14.clone.table_ref) | copy-start | bytes 442372
  0.0 22.6 %copy-start.3 = (bf16[2,128,256]{2,1,0:T(8,128)(2,1)S(1)}, bf16[2,128,256]{2,1,0:T(8,128)(2,1)}, u32[]{:S(2)}) copy-start(bf16[2,128,256]{2,1,0:T(8,128)(2,1)} %constant.16.clone.table_ref) | copy-start | bytes 393220
  0.0 25.2 %copy-start = (f32[8,17,8,128]{3,2,1,0:T(8,128)S(1)}, f32[8,17,8,128]{3,2,1,0:T(8,128)}, u32[]{:S(2)}) copy-start(f32[8,17,8,128]{3,2,1,0:T(8,128)} %constant.19.clone.response_ref) | copy-start | bytes 1671172
  0.0 25.2 %copy-start.2 = (bf16[2,144,144]{2,1,0:T(8,128)(2,1)S(1)}, bf16[2,144,144]{2,1,0:T(8,128)(2,1)}, u32[]{:S(2)}) copy-start(bf16[2,144,144]{2,1,0:T(8,128)(2,1)} %constant.17.clone.table_ref) | copy-start | bytes 248836
  20.0 5.2 %collective-permute-start = (f32[16,512]{1,0:T(8,128)S(1)}, f32[16,512]{1,0:T(8,128)S(1)}, u32[]{:S(2)}, u32[]{:S(2)}) collective-permute-start(f32[16,512]{1,0:T(8,128)S(1)} %get-tuple-element.36.sent_ref), channel_id=1, source_target_pairs={{2,0},{3,1},{0,2},{1,3},{6,4},{7,5},{4,6},{5,7},{10,8},{11,9},{8,1... | collective-permute-start | bytes 98312 | tf_op jit(solution)/shard_map/ppermute | solution.py:736
  36.6 2.3 %collective-permute-start.1 = (f32[8,8,1024]{2,1,0:T(8,128)S(1)}, f32[8,8,1024]{2,1,0:T(8,128)S(1)}, u32[]{:S(2)}, u32[]{:S(2)}) collective-permute-start(f32[8,8,1024]{2,1,0:T(8,128)S(1)} %get-tuple-element.43), channel_id=1, source_target_pairs={{0,4},{4,0},{8,12},{12,8},{16,20},{20,16},{24,28},{28,24},{1,5},{5... | collective-permute-start | bytes 786440 | tf_op jit(solution)/shard_map/ppermute | solution.py:833
  54.7 5.2 %collective-permute-start.2 = (f32[16,512]{1,0:T(8,128)S(1)}, f32[16,512]{1,0:T(8,128)S(1)}, u32[]{:S(2)}, u32[]{:S(2)}) collective-permute-start(f32[16,512]{1,0:T(8,128)S(1)} %get-tuple-element.51.sent_ref), channel_id=1, source_target_pairs={{2,0},{3,1},{0,2},{1,3},{6,4},{7,5},{4,6},{5,7},{10,8},{11,9},{8,1... | collective-permute-start | bytes 98312 | tf_op jit(solution)/shard_map/ppermute | solution.py:736
  71.3 2.0 %collective-permute-start.3 = (f32[8,8,1024]{2,1,0:T(8,128)S(1)}, f32[8,8,1024]{2,1,0:T(8,128)S(1)}, u32[]{:S(2)}, u32[]{:S(2)}) collective-permute-start(f32[8,8,1024]{2,1,0:T(8,128)S(1)} %get-tuple-element.57), channel_id=1, source_target_pairs={{0,4},{4,0},{8,12},{12,8},{16,20},{20,16},{24,28},{28,24},{1,5},{5... | collective-permute-start | bytes 786440 | tf_op jit(solution)/shard_map/ppermute | solution.py:833

commit v2 on v1

--- a/solution.py
+++ b/solution.py
@@ -279,23 +279,26 @@
     return jnp.concatenate([even + odd, even - odd], axis=1)
 
 
-def send_modes(space_ref, time_ref, edge_ref, table_ref, out_ref):
+def send_kernel(space_ref, time_ref, arrived_ref, edge_ref, table_ref, out_ref):
     columns, group_count, _, comps, width = out_ref.shape
     sites = space_ref.shape[2]
-    rows = 8 * COMPS
-    value = jnp.concatenate([r[...].reshape(-1, sites) for r in (space_ref, time_ref, edge_ref)], axis=0)
+    time = time_ref[...]
+    arrived = arrived_ref[...]
+    space = space_ref[...] - time + jnp.where(first_core(), 0.0, arrived)
+    half = jnp.where(first_core(), arrived[:, :4], time[:, 4:])
+    value = jnp.concatenate([v.reshape(-1, sites) for v in (space, half, edge_ref[...])], axis=0)
     start = 0
     for part in to_modes(value, table_ref):
         for inner in range(0, part.shape[1], width):
             column = (start + inner) // width
             piece = part[:, inner : inner + width]
             for g in range(group_count):
-                size = 8 * comps
-                space = piece[g * size : (g + 1) * size]
-                time = piece[rows + g * size : rows + (g + 1) * size]
-                out_ref[column, g, 0:8] = space.reshape(8, comps, width)
-                out_ref[column, g, 8:16] = time.reshape(8, comps, width)
-                out_ref[column, g, 16] = piece[2 * rows + 8 * g : 2 * rows + 8 * g + comps]
+                at = 8 * comps * g
+                out_ref[column, g, 0:8] = piece[at : at + 8 * comps].reshape(8, comps, width)
+                at = 8 * COMPS + 4 * comps * g
+                out_ref[column, g, 8:12] = piece[at : at + 4 * comps].reshape(4, comps, width)
+                at = 12 * COMPS + 8 * g
+                out_ref[column, g, 12] = piece[at : at + comps]
         start += part.shape[1]
 
 
@@ -347,54 +350,46 @@
         space_ref[c] = space_ref[c] + pltpu.roll(part, LX, 1) - part
 
 
-def first_gradient_kernel(
-    links_hbm, links_ref, table_ref, out_ref, space_ref, time_ref, edge_ref, y_ref, arrived
-):
-    copies = [pltpu.make_async_copy(links_hbm.at[mu], links_ref.at[mu], arrived.at[mu]) for mu in range(4)]
-    for copy in copies:
-        copy.start()
+def time_gradient_kernel(links_hbm, table_ref, time_ref, links_ref, arrived):
+    copy = pltpu.make_async_copy(links_hbm.at[3:4], links_ref, arrived)
+    copy.start()
     fill_plane_table(table_ref, False)
-    chunks = links_ref.shape[-1] // LANES
+    copy.wait()
+
+    def along_t(step, carry):
+        at = chunk_at(step)
+        part = gradient_part(load_link(links_ref, 0, at))
+        for c in range(COMPS):
+            time_ref[c, :, at] = part[c]
+        return carry
+
+    lax.fori_loop(0, time_ref.shape[-1] // LANES, along_t, 0, unroll=4)
+
+
+def space_gradient_kernel(links_ref, space_ref, edge_ref, y_ref):
     shape = (8, LANES)
 
-    def along_x(step, carry):
+    def body(step, carry):
         at = chunk_at(step)
+        row = row_index(shape)
         first_x = lane_index(shape) % LX == 0
         part = gradient_part(load_link(links_ref, 0, at))
-        for c in range(COMPS):
-            space_ref[c, :, at] = from_x_before(part[c], first_x) - part[c]
-        return carry
-
-    def along_y(step, carry):
-        at = chunk_at(step)
+        delta = [from_x_before(part[c], first_x) - part[c] for c in range(COMPS)]
         part = gradient_part(load_link(links_ref, 1, at))
         for c in range(COMPS):
             y_ref[c, :, at] = part[c]
+        add_z_difference(gradient_part(load_link(links_ref, 2, at)), delta, space_ref, edge_ref, at, row)
         return carry
 
-    def along_z(step, carry):
-        at = chunk_at(step)
-        row = row_index(shape)
-        part = gradient_part(load_link(links_ref, 2, at))
-        for c in range(COMPS):
-            behind = jnp.where(row == 0, 0.0, pltpu.roll(part[c], 1, 0))
-            space_ref[c, :, at] = space_ref[c, :, at] + (behind - part[c])
-        store_edges(edge_ref, at, part, row)
-        return carry
-
-    def along_t(step, carry):
-        at = chunk_at(step)
-        part = gradient_part(load_link(links_ref, 3, at))
-        for c in range(COMPS):
-            time_ref[c, :, at] = part[c]
-            space_ref[c, :, at] = space_ref[c, :, at] - part[c]
-        return carry
-
-    for mu, body in enumerate((along_x, along_y, along_z, along_t)):
-        copies[mu].wait()
-        lax.fori_loop(0, chunks, body, 0, unroll=4)
+    lax.fori_loop(0, links_ref.shape[-1] // LANES, body, 0, unroll=2)
     add_y_difference(space_ref, y_ref)
-    send_modes(space_ref, time_ref, edge_ref, table_ref, out_ref)
+
+
+def add_z_difference(part, delta, space_ref, edge_ref, at, row):
+    for c in range(COMPS):
+        behind = jnp.where(row == 0, 0.0, pltpu.roll(part[c], 1, 0))
+        space_ref[c, :, at] = delta[c] + (behind - part[c])
+    store_edges(edge_ref, at, part, row)
 
 
 def table_product(table_ref, value):
@@ -417,16 +412,19 @@
     group = group_of_device("ta", "gz", group_count)
     row = row_index((count, 8, width))
     space = spectral_ref[:, 0:8].reshape(count, 8 * comps, width)
-    time = spectral_ref[:, 8:16].reshape(count, 8 * comps, width)
-    time = jnp.concatenate([time[-half_devices:], time[:-half_devices]], axis=0)
-    edge = spectral_ref[:, 16].reshape(times, half_devices, comps, width)
+    time = spectral_ref[:, 8:12].reshape(times // 2, 2, half_devices, 4 * comps, width)
+    time = jnp.concatenate([time[-1:], time[:-1]], axis=0)
+    edge = spectral_ref[:, 12].reshape(times, half_devices, comps, width)
     beyond = edge[:, half_devices - 1]
     edge = jnp.concatenate([jnp.zeros_like(edge[:, :1]), edge[:, :-1]], axis=1).reshape(count, comps, width)
     pieces = []
     for c in range(comps):
         at = slice(8 * c, 8 * c + 8)
         first = jnp.where(row == 0, jnp.broadcast_to(edge[:, c : c + 1], row.shape), 0.0)
-        own = (space[:, at] + time[:, at] + first).reshape(lines, width)
+        at_half = slice(4 * c, 4 * c + 4)
+        before = jnp.concatenate([time[:, 0, :, at_half], time[:, 1, :, at_half]], axis=2)
+        before = jnp.stack([before, jnp.zeros_like(before)], axis=1).reshape(row.shape)
+        own = (space[:, at] + before + first).reshape(lines, width)
         after = beyond[:, c : c + 1].reshape(times, width)
         rest = table_ref.shape[2] - lines - times
         tail = [jnp.zeros((rest, width), jnp.float32)] if rest else []
@@ -592,32 +590,48 @@
     return rows + [conjugate_cross(rows[0], rows[1])]
 
 
-def space_links_kernel(
-    links_ref,
-    smooth_ref,
-    after_ref,
-    links_out_ref,
-    turned_ref,
-    space_ref,
-    edge_ref,
-    gauge_ref,
-    beyond_ref,
-    y_ref,
+def x_links_kernel(
+    links_ref, smooth_ref, after_ref, links_out_ref, gauge_ref, beyond_ref, turned_ref, delta_ref
 ):
-    chunks = links_ref.shape[-1] // LANES
-    shape = (8, LANES)
     gauge_matrices(smooth_ref, after_ref, gauge_ref, beyond_ref)
 
     def body(step, carry):
         at = chunk_at(step)
-        at_next = chunk_at(lax.rem(step + 1, chunks))
-        row = row_index(shape)
-        first_x = lane_index(shape) % LX == 0
+        first_x = lane_index((8, LANES)) % LX == 0
         own = [gauge_ref[n, :, at] for n in range(18)]
         link = rotate_x(links_ref, at, own)
         store_link(links_out_ref, 0, at, link)
         part = gradient_part(link)
-        delta = [from_x_before(part[c], first_x) - part[c] for c in range(COMPS)]
+        for c in range(COMPS):
+            delta_ref[c, :, at] = from_x_before(part[c], first_x) - part[c]
+        turn_time(links_ref, at, own, turned_ref)
+        return carry
+
+    lax.fori_loop(0, links_ref.shape[-1] // LANES, body, 0, unroll=2)
+
+
+def time_links_kernel(rotated_ref, turned_ref, part_ref, arrived_ref, links_out_ref, time_ref):
+    def body(step, carry):
+        at = chunk_at(step)
+        link = finish_time(turned_ref, part_ref, arrived_ref, at)
+        store_link(links_out_ref, 3, at, link)
+        part = gradient_part(link)
+        for c in range(COMPS):
+            time_ref[c, :, at] = part[c]
+        return carry
+
+    lax.fori_loop(0, arrived_ref.shape[-1] // LANES, body, 0, unroll=2)
+
+
+def yz_links_kernel(
+    rotated_ref, links_ref, gauge_ref, beyond_ref, delta_ref, links_out_ref, space_ref, edge_ref, y_ref
+):
+    chunks = links_ref.shape[-1] // LANES
+
+    def body(step, carry):
+        at = chunk_at(step)
+        at_next = chunk_at(lax.rem(step + 1, chunks))
+        own = [gauge_ref[n, :, at] for n in range(18)]
         link = rotate_y(links_ref, at, own, gauge_ref, at_next)
         store_link(links_out_ref, 1, at, link)
         part = gradient_part(link)
@@ -625,35 +639,12 @@
             y_ref[c, :, at] = part[c]
         link = rotate_z(links_ref, at, own, beyond_ref, step)
         store_link(links_out_ref, 2, at, link)
-        part = gradient_part(link)
-        for c in range(COMPS):
-            behind = jnp.where(row == 0, 0.0, pltpu.roll(part[c], 1, 0))
-            space_ref[c, :, at] = delta[c] + (behind - part[c])
-        store_edges(edge_ref, at, part, row)
-        turn_time(links_ref, at, own, turned_ref)
+        delta = [delta_ref[c, :, at] for c in range(COMPS)]
+        add_z_difference(gradient_part(link), delta, space_ref, edge_ref, at, row_index((8, LANES)))
         return carry
 
     lax.fori_loop(0, chunks, body, 0, unroll=2)
     add_y_difference(space_ref, y_ref)
-
-
-def time_links_kernel(
-    turned_ref, part_ref, arrived_ref, space_ref, edge_ref, table_ref, rotated_hold, links_ref, out_ref, sum_ref, time_ref
-):
-    chunks = arrived_ref.shape[-1] // LANES
-
-    def body(step, carry):
-        at = chunk_at(step)
-        link = finish_time(turned_ref, part_ref, arrived_ref, at)
-        store_link(links_ref, 3, at, link)
-        part = gradient_part(link)
-        for c in range(COMPS):
-            time_ref[c, :, at] = part[c]
-            sum_ref[c, :, at] = space_ref[c, :, at] - part[c]
-        return carry
-
-    lax.fori_loop(0, chunks, body, 0, unroll=2)
-    send_modes(sum_ref, time_ref, edge_ref, table_ref, out_ref)
 
 
 def last_space_links_kernel(links_ref, smooth_ref, after_ref, out_ref, turned_ref, gauge_ref, beyond_ref):
@@ -736,6 +727,10 @@
     return lax.ppermute(block, axis, [((i - distance) % size, i) for i in range(size)])
 
 
+def from_other_core(block):
+    return lax.ppermute(block, "ta", [(t, t + 1 - 2 * (t % 2)) for t in range(lax.axis_size("ta"))])
+
+
 def exchanged(block):
     depth = lax.axis_size("gz")
     half = depth // 2
@@ -773,25 +768,33 @@
     plane_sum = jnp.asarray(plane_sum.astype(np.float32).reshape(columns, 1, width))
 
     field = (COMPS, 8, sites)
-    sent_shape = shaped(columns, group_count, 17, comps, width)
-    edge_scratch = scratch(group_count, 8, sites)
-    links, forward, spectral = call(
-        first_gradient_kernel,
-        "first_gradient",
+    sent_shape = shaped(columns, group_count, 13, comps, width)
+    sites_field = shaped(*field)
+    edge_field = shaped(group_count, 8, sites)
+    forward, time = call(
+        time_gradient_kernel,
+        "time_gradient",
         [gauge_links],
-        [in_vmem()] * 3,
-        [shaped(*local), plane_table, sent_shape],
-        [
-            scratch(*field),
-            scratch(*field),
-            edge_scratch,
-            scratch(*field),
-            pltpu.SemaphoreType.DMA((4,)),
-        ],
+        [in_vmem()] * 2,
+        [plane_table, sites_field],
+        [scratch(1, *local[1:]), pltpu.SemaphoreType.DMA],
         in_specs=[in_hbm()],
     )
+    arrived = from_other_core(time)
+    links = gauge_links
+    space, edge = call(
+        space_gradient_kernel,
+        "space_gradient",
+        [links],
+        [in_vmem()] * 2,
+        [sites_field, edge_field],
+        [scratch(*field)],
+    )
+    spectral = call(
+        send_kernel, "gradient_modes", [space, time, arrived, edge, forward], in_vmem(), sent_shape
+    )
     for iteration in range(ITERS):
-        spectral = exchanged(spectral.reshape(devices, 17, comps, width))
+        spectral = exchanged(spectral.reshape(devices, 13, comps, width))
         modes, sent, total = call(
             functools.partial(modes_kernel, group_count, half_devices),
             "filtered_modes",
@@ -830,25 +833,42 @@
             [shaped(*field), shaped(COMPS, chunks, LANES), shaped(*field), shaped(*field)],
             [scratch(COMPS, sites)],
         )
-        arrived = lax.ppermute(sent, "ta", [(t, t + 1 - 2 * (t % 2)) for t in range(time_devices)])
+        arrived = from_other_core(sent)
         gauge_scratch = [scratch(18, 8, sites), scratch(18, chunks, LANES)]
         if iteration + 1 < ITERS:
-            links, turned, space, edge = call(
-                space_links_kernel,
-                "space_links",
+            rotated, gauge, beyond, turned, delta = call(
+                x_links_kernel,
+                "x_links",
                 [links, smooth, after],
-                [in_vmem()] * 4,
-                [shaped(*local), shaped(12, 8, sites), shaped(*field), edge_scratch],
-                gauge_scratch + [scratch(*field)],
+                [in_vmem()] * 5,
+                [
+                    shaped(*local),
+                    shaped(18, 8, sites),
+                    shaped(18, chunks, LANES),
+                    shaped(12, 8, sites),
+                    sites_field,
+                ],
             )
-            links, spectral = call(
+            rotated, time = call(
                 time_links_kernel,
                 "time_links",
-                [turned, part, arrived, space, edge, forward, links],
+                [rotated, turned, part, arrived],
                 [in_vmem()] * 2,
-                [shaped(*local), sent_shape],
-                [scratch(*field), scratch(*field)],
-                aliases={6: 0},
+                [shaped(*local), sites_field],
+                aliases={0: 0},
+            )
+            arrived = from_other_core(time)
+            links, space, edge = call(
+                yz_links_kernel,
+                "yz_links",
+                [rotated, links, gauge, beyond, delta],
+                [in_vmem()] * 3,
+                [shaped(*local), sites_field, edge_field],
+                [scratch(*field)],
+                aliases={0: 0},
+            )
+            spectral = call(
+                send_kernel, "gradient_modes", [space, time, arrived, edge, forward], in_vmem(), sent_shape
             )
         else:
             space_links, turned = call(

time: 75 us -> 72.1 us (0.961)
  blocking collectives: 51.9 us -> 47 us
  starting transfers between devices: 5.4 us -> 6.86 us
    all_to_all x4, blocking collectives: 51.9 us -> 47 us  [exchanged(): lax.all_to_all(block, ('ta', 'gz'), split_axis=0, concat_axis=0, axis_ind...]
    ppermute x2 -> x4, starting transfers between devices: 0.54 us -> 1.43 us  [from_other_core(): lax.ppermute(block, 'ta', [(t, t + 1 - 2 * (t % 2)) for t in range(lax.ax...]
    pallas_call x13 -> x17, Pallas kernels: 12.8 us -> 13.1 us  [call(): pl.pallas_call(kernel, in_specs=in_specs, out_specs=out_specs, out_shape=...]
  transfers between devices with their start and end apart: 4 -> 6, of which waited for: 2 -> 4; matrix products, arithmetic and copies ran while one was open for 0% -> 0% of each run, Pallas kernels for 6% -> 8%
where the time goes in v2:
time: 72.1 us; the launch traced here: 71.8 us
  blocking collectives  47 us (65%)
  Pallas kernels  13.1 us (18%)
  starting transfers between devices  6.86 us (10%)
  waiting for transfers between devices  4.65 us (6%)
    all_to_all x4, blocking collectives, exchanged(): lax.all_to_all(block, ('ta', 'gz'), split_axis=0, concat_axis=0, axis_ind...  47 us
    pallas_call x17, Pallas kernels, call(): pl.pallas_call(kernel, in_specs=in_specs, out_specs=out_specs, out_shape=...  13.1 us
    ppermute x2, starting transfers between devices, passed(): lax.ppermute(block, axis, [((i - distance) % size, i) for i in range(size)])  5.43 us
    ppermute x2, waiting for transfers between devices, passed(): lax.ppermute(block, axis, [((i - distance) % size, i) for i in range(size)])  4.07 us
  transfers between devices with their start and end apart: 6, of which 4 were waited for; matrix products, arithmetic and copies ran while one was open for 0% of the time, Pallas kernels for 8%

profile of v2, /device:TPU:0, one launch (start us, length us, event | category | flops | bytes accessed | tf_op | source)
XLA Modules:
  0.0 71.8 jit_solution(11529815904722624915)
XLA Ops:
  0.0 1.3 %time_gradient.1 = (bf16[2,768,512]{2,1,0:T(8,128)(2,1)S(1)}, f32[8,8,1024]{2,1,0:T(8,128)S(1)}) custom-call(f32[4,2,3,3,1,8,1024]{6,5,4,3,2,1,0:T(8,128)} %links_ref.5), custom_call_target="tpu_custom_call" | custom-call | tf_op jit(solution)/shard_map/time_gradient/pallas_call | solution.py:713
  1.3 0.5 collective-permute-start
  1.8 0.6 space_gradient.1
  2.5 0.5 collective-permute-done.arrived_ref
  3.0 0.5 gradient_modes.2
  3.5 13.9 %all_to_all.20.spectral_ref = f32[16,13,4,128]{3,2,1,0:T(4,128)S(1)} all-to-all(f32[16,13,4,128]{3,2,1,0:T(4,128)S(1)} %bitcast.3), channel_id=1, replica_groups={{0,1,4,5,8,9,12,13,16,17,20,21,24,25,28,29},{2,3,6,7,10,11,14,15,18,19,..., dimensions={0} | all-to-all | bytes 851968 | tf_op jit(solution)/shard_map/all_to_all | solution.py:740
  17.4 0.6 filtered_modes.2
  18.1 2.6 %collective-permute-start.1 = (f32[16,512]{1,0:T(8,128)S(1)}, f32[16,512]{1,0:T(8,128)S(1)}, u32[]{:S(2)}, u32[]{:S(2)}) collective-permute-start(f32[16,512]{1,0:T(8,128)S(1)} %get-tuple-element.43.sent_ref), channel_id=1, source_target_pairs={{2,0},{3,1},{0,2},{1,3},{6,4},{7,5},{4,6},{5,7},{10,8},{11,9},{8,1... | collective-permute-start | bytes 98312 | tf_op jit(solution)/shard_map/ppermute | solution.py:727
  20.6 0.7 own_half.2
  21.4 1.7 %collective-permute-done.1.arrived_ref = f32[16,512]{1,0:T(8,128)S(1)} collective-permute-done((f32[16,512]{1,0:T(8,128)S(1)}, f32[16,512]{1,0:T(8,128)S(1)}, u32[]{:S(2)}, u32[]{:S(2)}) %collective-permute-start.1) | collective-permute-done | bytes 32800 | tf_op jit(solution)/shard_map/ppermute | solution.py:727
  23.4 11.2 %all_to_all.21.spectral_ref = f32[16,13,4,128]{3,2,1,0:T(4,128)S(1)} all-to-all(f32[16,13,4,128]{3,2,1,0:T(4,128)S(1)} %coupled_halves.2), channel_id=1, replica_groups={{0,1,4,5,8,9,12,13,16,17,20,21,24,25,28,29},{2,3,6,7,10,11,14,15,18,19,..., dimensions={0} | all-to-all | bytes 851968 | tf_op jit(solution)/shard_map/all_to_all | solution.py:740
  34.6 0.5 smooth_field.2
  35.4 1.4 %x_links.1 = (f32[4,2,3,3,1,8,1024]{6,5,4,3,2,1,0:T(8,128)S(1)}, f32[18,8,1024]{2,1,0:T(8,128)S(1)}, f32[18,8,128]{2,1,0:T(8,128)S(1)}, f32[12,8,1024]{2,1,0:T(8,128)S(1)}, f32[8,8,1024]{2,1,0:T(8,128)S(1)}) custom-call(f32[4,2,3,3,1,8,1024]{6,5,4,3,2,1,0:T(8,128)S(1)} %copy-done, f32[8,8,1024]{2,1,0:T(8,128)S(1)} %get-tuple-element.46.smooth_ref, ...), custom_call_target="tpu_custom_call" | custom-call | tf_op jit(solution)/shard_map/x_links/pallas_call | solution.py:713
  36.8 0.6 time_links.1
  37.8 1.1 %yz_links.1 = (f32[4,2,3,3,1,8,1024]{6,5,4,3,2,1,0:T(8,128)S(1)}, f32[8,8,1024]{2,1,0:T(8,128)S(1)}, f32[2,8,1024]{2,1,0:T(8,128)S(1)}) custom-call(f32[4,2,3,3,1,8,1024]{6,5,4,3,2,1,0:T(8,128)S(1)} %get-tuple-element.52.rotated_ref, f32[4,2,3,3,1,8,1024]{6,5,4,3,2,1,0:T(8,128)S(1)} %copy-done, ...), custom_call_target="tpu_custom_call", output_to_operand_aliasing={{0}: (0, {})} | custom-call | tf_op jit(solution)/shard_map/yz_links/pallas_call | solution.py:713
  39.0 0.5 gradient_modes.3
  39.5 11.2 %all_to_all.22.spectral_ref = f32[16,13,4,128]{3,2,1,0:T(4,128)S(1)} all-to-all(f32[16,13,4,128]{3,2,1,0:T(4,128)S(1)} %bitcast.2), channel_id=1, replica_groups={{0,1,4,5,8,9,12,13,16,17,20,21,24,25,28,29},{2,3,6,7,10,11,14,15,18,19,..., dimensions={0} | all-to-all | bytes 851968 | tf_op jit(solution)/shard_map/all_to_all | solution.py:740
  50.7 0.6 filtered_modes.3
  51.3 2.8 %collective-permute-start.4 = (f32[16,512]{1,0:T(8,128)S(1)}, f32[16,512]{1,0:T(8,128)S(1)}, u32[]{:S(2)}, u32[]{:S(2)}) collective-permute-start(f32[16,512]{1,0:T(8,128)S(1)} %get-tuple-element.61.sent_ref), channel_id=1, source_target_pairs={{2,0},{3,1},{0,2},{1,3},{6,4},{7,5},{4,6},{5,7},{10,8},{11,9},{8,1... | collective-permute-start | bytes 98312 | tf_op jit(solution)/shard_map/ppermute | solution.py:727
  54.4 2.4 %collective-permute-done.4.arrived_ref = f32[16,512]{1,0:T(8,128)S(1)} collective-permute-done((f32[16,512]{1,0:T(8,128)S(1)}, f32[16,512]{1,0:T(8,128)S(1)}, u32[]{:S(2)}, u32[]{:S(2)}) %collective-permute-start.4) | collective-permute-done | bytes 32800 | tf_op jit(solution)/shard_map/ppermute | solution.py:727
  57.2 10.7 %all_to_all.23.spectral_ref = f32[16,13,4,128]{3,2,1,0:T(4,128)S(1)} all-to-all(f32[16,13,4,128]{3,2,1,0:T(4,128)S(1)} %coupled_halves.3), channel_id=1, replica_groups={{0,1,4,5,8,9,12,13,16,17,20,21,24,25,28,29},{2,3,6,7,10,11,14,15,18,19,..., dimensions={0} | all-to-all | bytes 851968 | tf_op jit(solution)/shard_map/all_to_all | solution.py:740
  67.8 0.5 smooth_field.3
  68.7 1.7 %last_space_links.1 = (f32[3,2,3,3,1,8,1024]{6,5,4,3,2,1,0:T(8,128)S(1)}, f32[12,8,1024]{2,1,0:T(8,128)S(1)}) custom-call(f32[4,2,3,3,1,8,1024]{6,5,4,3,2,1,0:T(8,128)S(1)} %get-tuple-element.56.links_ref, f32[8,8,1024]{2,1,0:T(8,128)S(1)} %get-tuple-element.63.smooth_ref, f32[8,8,128]{2,1,0:T(8,128)S(1)} %get-tuple-element.64.after_ref), custom_call_target="tpu_custom_call" | custom-call | tf_op jit(solution)/shard_map/last_space_links/pallas_call | solution.py:713
  70.4 1.4 %last_time_links.1 = f32[4,2,3,3,1,8,1024]{6,5,4,3,2,1,0:T(8,128)} custom-call(f32[12,8,1024]{2,1,0:T(8,128)S(1)} %get-tuple-element.65.turned_ref, f32[8,8,1024]{2,1,0:T(8,128)S(1)} %get-tuple-element.66.part_ref, f32[8,8,1024]{2,1,0:T(8,128)S(1)} %collective-permute-done.5.arrived_ref, f32[3,2,3,3,1,8,1024]{6,5,4,3,2,1,0:T(8,128)S(1)} %get-tuple-element.68.space_ref), custom_call_target="tpu_custom_call" | custom-call | tf_op jit(solution)/shard_map/last_time_links/pallas_call | solution.py:713
  (25 shorter events, 2.1 us)
Async XLA Ops:
  0.0 1.8 %copy-start = (f32[4,2,3,3,1,8,1024]{6,5,4,3,2,1,0:T(8,128)S(1)}, f32[4,2,3,3,1,8,1024]{6,5,4,3,2,1,0:T(8,128)}, u32[]{:S(2)}) copy-start(f32[4,2,3,3,1,8,1024]{6,5,4,3,2,1,0:T(8,128)} %links_ref.5) | copy-start | bytes 7077892
  1.3 1.7 %collective-permute-start = (f32[8,8,1024]{2,1,0:T(8,128)S(1)}, f32[8,8,1024]{2,1,0:T(8,128)S(1)}, u32[]{:S(2)}, u32[]{:S(2)}) collective-permute-start(f32[8,8,1024]{2,1,0:T(8,128)S(1)} %get-tuple-element.38.time_ref), channel_id=1, source_target_pairs={{0,4},{4,0},{8,12},{12,8},{16,20},{20,16},{24,28},{28,24},{1,5},{5... | collective-permute-start | bytes 786440 | tf_op jit(solution)/shard_map/ppermute | solution.py:731
  2.5 15.0 %copy-start.2 = (bf16[2,256,144]{2,1,0:T(8,128)(2,1)S(1)}, bf16[2,256,144]{2,1,0:T(8,128)(2,1)}, u32[]{:S(2)}) copy-start(bf16[2,256,144]{2,1,0:T(8,128)(2,1)} %constant.14.clone.table_ref) | copy-start | bytes 442372
  2.5 15.0 %copy-start.5 = (f32[256,128]{1,0:T(8,128)S(1)}, f32[256,128]{1,0:T(8,128)}, u32[]{:S(2)}) copy-start(f32[256,128]{1,0:T(8,128)} %constant.18.clone.line_ref) | copy-start | bytes 393220
  2.5 14.9 %copy-start.6 = (bf16[2,16,256]{2,1,0:T(8,128)(2,1)S(1)}, bf16[2,16,256]{2,1,0:T(8,128)(2,1)}, u32[]{:S(2)}) copy-start(bf16[2,16,256]{2,1,0:T(8,128)(2,1)} %constant.15.clone.edges_ref) | copy-start | bytes 49156
  2.5 14.9 %copy-start.7 = (f32[8,1,128]{2,1,0:T(1,128)S(1)}, f32[8,1,128]{2,1,0:T(1,128)}, u32[]{:S(2)}) copy-start(f32[8,1,128]{2,1,0:T(1,128)} %constant.20.clone.plane_ref) | copy-start | bytes 12292
  2.5 18.1 %copy-start.4 = (bf16[2,128,256]{2,1,0:T(8,128)(2,1)S(1)}, bf16[2,128,256]{2,1,0:T(8,128)(2,1)}, u32[]{:S(2)}) copy-start(bf16[2,128,256]{2,1,0:T(8,128)(2,1)} %constant.16.clone.table_ref) | copy-start | bytes 393220
  3.0 20.0 %copy-start.1 = (f32[8,17,8,128]{3,2,1,0:T(8,128)S(1)}, f32[8,17,8,128]{3,2,1,0:T(8,128)}, u32[]{:S(2)}) copy-start(f32[8,17,8,128]{3,2,1,0:T(8,128)} %constant.19.clone.response_ref) | copy-start | bytes 1671172
  3.0 20.0 %copy-start.3 = (bf16[2,144,144]{2,1,0:T(8,128)(2,1)S(1)}, bf16[2,144,144]{2,1,0:T(8,128)(2,1)}, u32[]{:S(2)}) copy-start(bf16[2,144,144]{2,1,0:T(8,128)(2,1)} %constant.17.clone.table_ref) | copy-start | bytes 248836
  18.1 5.0 %collective-permute-start.1 = (f32[16,512]{1,0:T(8,128)S(1)}, f32[16,512]{1,0:T(8,128)S(1)}, u32[]{:S(2)}, u32[]{:S(2)}) collective-permute-start(f32[16,512]{1,0:T(8,128)S(1)} %get-tuple-element.43.sent_ref), channel_id=1, source_target_pairs={{2,0},{3,1},{0,2},{1,3},{6,4},{7,5},{4,6},{5,7},{10,8},{11,9},{8,1... | collective-permute-start | bytes 98312 | tf_op jit(solution)/shard_map/ppermute | solution.py:727
  35.2 1.7 %collective-permute-start.2 = (f32[8,8,1024]{2,1,0:T(8,128)S(1)}, f32[8,8,1024]{2,1,0:T(8,128)S(1)}, u32[]{:S(2)}, u32[]{:S(2)}) collective-permute-start(f32[8,8,1024]{2,1,0:T(8,128)S(1)} %get-tuple-element.51), channel_id=1, source_target_pairs={{0,4},{4,0},{8,12},{12,8},{16,20},{20,16},{24,28},{28,24},{1,5},{5... | collective-permute-start | bytes 786440 | tf_op jit(solution)/shard_map/ppermute | solution.py:731
  37.4 1.6 %collective-permute-start.3 = (f32[8,8,1024]{2,1,0:T(8,128)S(1)}, f32[8,8,1024]{2,1,0:T(8,128)S(1)}, u32[]{:S(2)}, u32[]{:S(2)}) collective-permute-start(f32[8,8,1024]{2,1,0:T(8,128)S(1)} %get-tuple-element.58.time_ref), channel_id=1, source_target_pairs={{0,4},{4,0},{8,12},{12,8},{16,20},{20,16},{24,28},{28,24},{1,5},{5... | collective-permute-start | bytes 786440 | tf_op jit(solution)/shard_map/ppermute | solution.py:731
  51.3 5.5 %collective-permute-start.4 = (f32[16,512]{1,0:T(8,128)S(1)}, f32[16,512]{1,0:T(8,128)S(1)}, u32[]{:S(2)}, u32[]{:S(2)}) collective-permute-start(f32[16,512]{1,0:T(8,128)S(1)} %get-tuple-element.61.sent_ref), channel_id=1, source_target_pairs={{2,0},{3,1},{0,2},{1,3},{6,4},{7,5},{4,6},{5,7},{10,8},{11,9},{8,1... | collective-permute-start | bytes 98312 | tf_op jit(solution)/shard_map/ppermute | solution.py:727
  68.4 2.0 %collective-permute-start.5 = (f32[8,8,1024]{2,1,0:T(8,128)S(1)}, f32[8,8,1024]{2,1,0:T(8,128)S(1)}, u32[]{:S(2)}, u32[]{:S(2)}) collective-permute-start(f32[8,8,1024]{2,1,0:T(8,128)S(1)} %get-tuple-element.67), channel_id=1, source_target_pairs={{0,4},{4,0},{8,12},{12,8},{16,20},{20,16},{24,28},{28,24},{1,5},{5... | collective-permute-start | bytes 786440 | tf_op jit(solution)/shard_map/ppermute | solution.py:731

commit v3 on v2

--- a/solution.py
+++ b/solution.py
@@ -350,10 +350,9 @@
         space_ref[c] = space_ref[c] + pltpu.roll(part, LX, 1) - part
 
 
-def time_gradient_kernel(links_hbm, table_ref, time_ref, links_ref, arrived):
+def time_gradient_kernel(links_hbm, time_ref, links_ref, arrived):
     copy = pltpu.make_async_copy(links_hbm.at[3:4], links_ref, arrived)
     copy.start()
-    fill_plane_table(table_ref, False)
     copy.wait()
 
     def along_t(step, carry):
@@ -366,8 +365,9 @@
     lax.fori_loop(0, time_ref.shape[-1] // LANES, along_t, 0, unroll=4)
 
 
-def space_gradient_kernel(links_ref, space_ref, edge_ref, y_ref):
+def space_gradient_kernel(links_ref, space_ref, edge_ref, table_ref, y_ref):
     shape = (8, LANES)
+    fill_plane_table(table_ref, False)
 
     def body(step, carry):
         at = chunk_at(step)
@@ -537,20 +537,17 @@
     return lax.rem(lax.axis_index("ta"), 2) == 0
 
 
-def gauge_matrices(smooth_ref, after_ref, gauge_ref, beyond_ref):
-    chunks = smooth_ref.shape[-1] // LANES
+def gauge_after(after_ref, beyond_ref):
     beyond = flat(exponential([after_ref[c] for c in range(COMPS)]))
     for n in range(18):
         beyond_ref[n] = beyond[n]
 
-    def matrices(step, carry):
-        at = chunk_at(step)
-        gauge = flat(exponential([smooth_ref[c, :, at] for c in range(COMPS)]))
-        for n in range(18):
-            gauge_ref[n, :, at] = gauge[n]
-        return carry
-
-    lax.fori_loop(0, chunks, matrices, 0, unroll=4)
+
+def gauge_here(smooth_ref, gauge_ref, at):
+    gauge = flat(exponential([smooth_ref[c, :, at] for c in range(COMPS)]))
+    for n in range(18):
+        gauge_ref[n, :, at] = gauge[n]
+    return gauge
 
 
 def rotate_x(links_ref, at, own):
@@ -593,12 +590,12 @@
 def x_links_kernel(
     links_ref, smooth_ref, after_ref, links_out_ref, gauge_ref, beyond_ref, turned_ref, delta_ref
 ):
-    gauge_matrices(smooth_ref, after_ref, gauge_ref, beyond_ref)
+    gauge_after(after_ref, beyond_ref)
 
     def body(step, carry):
         at = chunk_at(step)
         first_x = lane_index((8, LANES)) % LX == 0
-        own = [gauge_ref[n, :, at] for n in range(18)]
+        own = gauge_here(smooth_ref, gauge_ref, at)
         link = rotate_x(links_ref, at, own)
         store_link(links_out_ref, 0, at, link)
         part = gradient_part(link)
@@ -649,19 +646,25 @@
 
 def last_space_links_kernel(links_ref, smooth_ref, after_ref, out_ref, turned_ref, gauge_ref, beyond_ref):
     chunks = links_ref.shape[-1] // LANES
-    gauge_matrices(smooth_ref, after_ref, gauge_ref, beyond_ref)
-
-    def body(step, carry):
+    gauge_after(after_ref, beyond_ref)
+
+    def along_x(step, carry):
+        at = chunk_at(step)
+        own = gauge_here(smooth_ref, gauge_ref, at)
+        store_link(out_ref, 0, at, rotate_x(links_ref, at, own))
+        turn_time(links_ref, at, own, turned_ref)
+        return carry
+
+    def along_yz(step, carry):
         at = chunk_at(step)
         at_next = chunk_at(lax.rem(step + 1, chunks))
         own = [gauge_ref[n, :, at] for n in range(18)]
-        store_link(out_ref, 0, at, rotate_x(links_ref, at, own))
         store_link(out_ref, 1, at, rotate_y(links_ref, at, own, gauge_ref, at_next))
         store_link(out_ref, 2, at, rotate_z(links_ref, at, own, beyond_ref, step))
-        turn_time(links_ref, at, own, turned_ref)
         return carry
 
-    lax.fori_loop(0, chunks, body, 0, unroll=2)
+    lax.fori_loop(0, chunks, along_x, 0, unroll=2)
+    lax.fori_loop(0, chunks, along_yz, 0, unroll=2)
 
 
 def last_time_links_kernel(turned_ref, part_ref, arrived_ref, space_ref, out_hbm, time_ref, sent):
@@ -771,23 +774,23 @@
     sent_shape = shaped(columns, group_count, 13, comps, width)
     sites_field = shaped(*field)
     edge_field = shaped(group_count, 8, sites)
-    forward, time = call(
+    time = call(
         time_gradient_kernel,
         "time_gradient",
         [gauge_links],
-        [in_vmem()] * 2,
-        [plane_table, sites_field],
+        in_vmem(),
+        sites_field,
         [scratch(1, *local[1:]), pltpu.SemaphoreType.DMA],
         in_specs=[in_hbm()],
     )
     arrived = from_other_core(time)
     links = gauge_links
-    space, edge = call(
+    space, edge, forward = call(
         space_gradient_kernel,
         "space_gradient",
         [links],
-        [in_vmem()] * 2,
-        [sites_field, edge_field],
+        [in_vmem()] * 3,
+        [sites_field, edge_field, plane_table],
         [scratch(*field)],
     )
     spectral = call(

time: 72.1 us -> 72.3 us (level)
  transfers between devices with their start and end apart: 6 -> 6, of which waited for: 4 -> 4; matrix products, arithmetic and copies ran while one was open for 0% -> 0% of each run, Pallas kernels for 8% -> 9%
where the time goes in v3:
time: 72.3 us; the launch traced here: 72 us
  blocking collectives  47.1 us (65%)
  Pallas kernels  13.5 us (19%)
  starting transfers between devices  6.81 us (9%)
  waiting for transfers between devices  4.29 us (6%)
    all_to_all x4, blocking collectives, exchanged(): lax.all_to_all(block, ('ta', 'gz'), split_axis=0, concat_axis=0, axis_ind...  47.1 us
    pallas_call x17, Pallas kernels, call(): pl.pallas_call(kernel, in_specs=in_specs, out_specs=out_specs, out_shape=...  13.5 us
    ppermute x2, starting transfers between devices, passed(): lax.ppermute(block, axis, [((i - distance) % size, i) for i in range(size)])  5.44 us
    ppermute x2, waiting for transfers between devices, passed(): lax.ppermute(block, axis, [((i - distance) % size, i) for i in range(size)])  4.06 us
  transfers between devices with their start and end apart: 6, of which 4 were waited for; matrix products, arithmetic and copies ran while one was open for 0% of the time, Pallas kernels for 9%

profile of v3, /device:TPU:0, one launch (start us, length us, event | category | flops | bytes accessed | tf_op | source)
XLA Modules:
  0.0 72.0 jit_solution(1967354970790684518)
XLA Ops:
  0.0 1.3 %time_gradient.1.time_ref = f32[8,8,1024]{2,1,0:T(8,128)S(1)} custom-call(f32[4,2,3,3,1,8,1024]{6,5,4,3,2,1,0:T(8,128)} %links_ref.5), custom_call_target="tpu_custom_call" | custom-call | tf_op jit(solution)/shard_map/time_gradient/pallas_call | solution.py:716
  1.3 0.5 collective-permute-start
  1.8 1.2 %space_gradient.1 = (f32[8,8,1024]{2,1,0:T(8,128)S(1)}, f32[2,8,1024]{2,1,0:T(8,128)S(1)}, bf16[2,768,512]{2,1,0:T(8,128)(2,1)S(1)}) custom-call(f32[4,2,3,3,1,8,1024]{6,5,4,3,2,1,0:T(8,128)S(1)} %copy-done), custom_call_target="tpu_custom_call" | custom-call | tf_op jit(solution)/shard_map/space_gradient/pallas_call | solution.py:716
  3.1 0.5 gradient_modes.2
  3.6 14.0 %all_to_all.20.spectral_ref = f32[16,13,4,128]{3,2,1,0:T(4,128)S(1)} all-to-all(f32[16,13,4,128]{3,2,1,0:T(4,128)S(1)} %bitcast.3), channel_id=1, replica_groups={{0,1,4,5,8,9,12,13,16,17,20,21,24,25,28,29},{2,3,6,7,10,11,14,15,18,19,..., dimensions={0} | all-to-all | bytes 851968 | tf_op jit(solution)/shard_map/all_to_all | solution.py:743
  17.6 0.6 filtered_modes.2
  18.2 2.6 %collective-permute-start.1 = (f32[16,512]{1,0:T(8,128)S(1)}, f32[16,512]{1,0:T(8,128)S(1)}, u32[]{:S(2)}, u32[]{:S(2)}) collective-permute-start(f32[16,512]{1,0:T(8,128)S(1)} %get-tuple-element.41.sent_ref), channel_id=1, source_target_pairs={{2,0},{3,1},{0,2},{1,3},{6,4},{7,5},{4,6},{5,7},{10,8},{11,9},{8,1... | collective-permute-start | bytes 98312 | tf_op jit(solution)/shard_map/ppermute | solution.py:730
  20.8 0.7 own_half.2
  21.5 1.7 %collective-permute-done.1.arrived_ref = f32[16,512]{1,0:T(8,128)S(1)} collective-permute-done((f32[16,512]{1,0:T(8,128)S(1)}, f32[16,512]{1,0:T(8,128)S(1)}, u32[]{:S(2)}, u32[]{:S(2)}) %collective-permute-start.1) | collective-permute-done | bytes 32800 | tf_op jit(solution)/shard_map/ppermute | solution.py:730
  23.2 0.4 coupled_halves.2
  23.6 11.2 %all_to_all.21.spectral_ref = f32[16,13,4,128]{3,2,1,0:T(4,128)S(1)} all-to-all(f32[16,13,4,128]{3,2,1,0:T(4,128)S(1)} %coupled_halves.2), channel_id=1, replica_groups={{0,1,4,5,8,9,12,13,16,17,20,21,24,25,28,29},{2,3,6,7,10,11,14,15,18,19,..., dimensions={0} | all-to-all | bytes 851968 | tf_op jit(solution)/shard_map/all_to_all | solution.py:743
  34.8 0.5 smooth_field.2
  35.6 1.3 %x_links.1 = (f32[4,2,3,3,1,8,1024]{6,5,4,3,2,1,0:T(8,128)S(1)}, f32[18,8,1024]{2,1,0:T(8,128)S(1)}, f32[18,8,128]{2,1,0:T(8,128)S(1)}, f32[12,8,1024]{2,1,0:T(8,128)S(1)}, f32[8,8,1024]{2,1,0:T(8,128)S(1)}) custom-call(f32[4,2,3,3,1,8,1024]{6,5,4,3,2,1,0:T(8,128)S(1)} %copy-done, f32[8,8,1024]{2,1,0:T(8,128)S(1)} %get-tuple-element.44.smooth_ref, ...), custom_call_target="tpu_custom_call" | custom-call | tf_op jit(solution)/shard_map/x_links/pallas_call | solution.py:716
  36.9 0.6 time_links.1
  37.8 1.1 %yz_links.1 = (f32[4,2,3,3,1,8,1024]{6,5,4,3,2,1,0:T(8,128)S(1)}, f32[8,8,1024]{2,1,0:T(8,128)S(1)}, f32[2,8,1024]{2,1,0:T(8,128)S(1)}) custom-call(f32[4,2,3,3,1,8,1024]{6,5,4,3,2,1,0:T(8,128)S(1)} %get-tuple-element.50.rotated_ref, f32[4,2,3,3,1,8,1024]{6,5,4,3,2,1,0:T(8,128)S(1)} %copy-done, ...), custom_call_target="tpu_custom_call", output_to_operand_aliasing={{0}: (0, {})} | custom-call | tf_op jit(solution)/shard_map/yz_links/pallas_call | solution.py:716
  39.1 0.5 gradient_modes.3
  39.6 11.3 %all_to_all.22.spectral_ref = f32[16,13,4,128]{3,2,1,0:T(4,128)S(1)} all-to-all(f32[16,13,4,128]{3,2,1,0:T(4,128)S(1)} %bitcast.2), channel_id=1, replica_groups={{0,1,4,5,8,9,12,13,16,17,20,21,24,25,28,29},{2,3,6,7,10,11,14,15,18,19,..., dimensions={0} | all-to-all | bytes 851968 | tf_op jit(solution)/shard_map/all_to_all | solution.py:743
  50.8 0.6 filtered_modes.3
  51.4 2.8 %collective-permute-start.4 = (f32[16,512]{1,0:T(8,128)S(1)}, f32[16,512]{1,0:T(8,128)S(1)}, u32[]{:S(2)}, u32[]{:S(2)}) collective-permute-start(f32[16,512]{1,0:T(8,128)S(1)} %get-tuple-element.59.sent_ref), channel_id=1, source_target_pairs={{2,0},{3,1},{0,2},{1,3},{6,4},{7,5},{4,6},{5,7},{10,8},{11,9},{8,1... | collective-permute-start | bytes 98312 | tf_op jit(solution)/shard_map/ppermute | solution.py:730
  54.6 2.4 %collective-permute-done.4.arrived_ref = f32[16,512]{1,0:T(8,128)S(1)} collective-permute-done((f32[16,512]{1,0:T(8,128)S(1)}, f32[16,512]{1,0:T(8,128)S(1)}, u32[]{:S(2)}, u32[]{:S(2)}) %collective-permute-start.4) | collective-permute-done | bytes 32800 | tf_op jit(solution)/shard_map/ppermute | solution.py:730
  57.3 10.7 %all_to_all.23.spectral_ref = f32[16,13,4,128]{3,2,1,0:T(4,128)S(1)} all-to-all(f32[16,13,4,128]{3,2,1,0:T(4,128)S(1)} %coupled_halves.3), channel_id=1, replica_groups={{0,1,4,5,8,9,12,13,16,17,20,21,24,25,28,29},{2,3,6,7,10,11,14,15,18,19,..., dimensions={0} | all-to-all | bytes 851968 | tf_op jit(solution)/shard_map/all_to_all | solution.py:743
  68.0 0.5 smooth_field.3
  68.8 1.8 %last_space_links.1 = (f32[3,2,3,3,1,8,1024]{6,5,4,3,2,1,0:T(8,128)S(1)}, f32[12,8,1024]{2,1,0:T(8,128)S(1)}) custom-call(f32[4,2,3,3,1,8,1024]{6,5,4,3,2,1,0:T(8,128)S(1)} %get-tuple-element.54.links_ref, f32[8,8,1024]{2,1,0:T(8,128)S(1)} %get-tuple-element.61.smooth_ref, f32[8,8,128]{2,1,0:T(8,128)S(1)} %get-tuple-element.62.after_ref), custom_call_target="tpu_custom_call" | custom-call | tf_op jit(solution)/shard_map/last_space_links/pallas_call | solution.py:716
  70.6 1.4 %last_time_links.1 = f32[4,2,3,3,1,8,1024]{6,5,4,3,2,1,0:T(8,128)} custom-call(f32[12,8,1024]{2,1,0:T(8,128)S(1)} %get-tuple-element.63.turned_ref, f32[8,8,1024]{2,1,0:T(8,128)S(1)} %get-tuple-element.64.part_ref, f32[8,8,1024]{2,1,0:T(8,128)S(1)} %collective-permute-done.5.arrived_ref, f32[3,2,3,3,1,8,1024]{6,5,4,3,2,1,0:T(8,128)S(1)} %get-tuple-element.66.space_ref), custom_call_target="tpu_custom_call" | custom-call | tf_op jit(solution)/shard_map/last_time_links/pallas_call | solution.py:716
  (25 shorter events, 1.8 us)
Async XLA Ops:
  0.0 1.8 %copy-start = (f32[4,2,3,3,1,8,1024]{6,5,4,3,2,1,0:T(8,128)S(1)}, f32[4,2,3,3,1,8,1024]{6,5,4,3,2,1,0:T(8,128)}, u32[]{:S(2)}) copy-start(f32[4,2,3,3,1,8,1024]{6,5,4,3,2,1,0:T(8,128)} %links_ref.5) | copy-start | bytes 7077892
  1.3 1.8 %collective-permute-start = (f32[8,8,1024]{2,1,0:T(8,128)S(1)}, f32[8,8,1024]{2,1,0:T(8,128)S(1)}, u32[]{:S(2)}, u32[]{:S(2)}) collective-permute-start(f32[8,8,1024]{2,1,0:T(8,128)S(1)} %time_gradient.1.time_ref), channel_id=1, source_target_pairs={{0,4},{4,0},{8,12},{12,8},{16,20},{20,16},{24,28},{28,24},{1,5},{5... | collective-permute-start | bytes 786440 | tf_op jit(solution)/shard_map/ppermute | solution.py:734
  3.0 14.6 %copy-start.2 = (bf16[2,256,144]{2,1,0:T(8,128)(2,1)S(1)}, bf16[2,256,144]{2,1,0:T(8,128)(2,1)}, u32[]{:S(2)}) copy-start(bf16[2,256,144]{2,1,0:T(8,128)(2,1)} %constant.14.clone.table_ref) | copy-start | bytes 442372
  3.0 14.6 %copy-start.5 = (f32[256,128]{1,0:T(8,128)S(1)}, f32[256,128]{1,0:T(8,128)}, u32[]{:S(2)}) copy-start(f32[256,128]{1,0:T(8,128)} %constant.18.clone.line_ref) | copy-start | bytes 393220
  3.0 14.6 %copy-start.6 = (bf16[2,16,256]{2,1,0:T(8,128)(2,1)S(1)}, bf16[2,16,256]{2,1,0:T(8,128)(2,1)}, u32[]{:S(2)}) copy-start(bf16[2,16,256]{2,1,0:T(8,128)(2,1)} %constant.15.clone.edges_ref) | copy-start | bytes 49156
  3.0 14.6 %copy-start.7 = (f32[8,1,128]{2,1,0:T(1,128)S(1)}, f32[8,1,128]{2,1,0:T(1,128)}, u32[]{:S(2)}) copy-start(f32[8,1,128]{2,1,0:T(1,128)} %constant.20.clone.plane_ref) | copy-start | bytes 12292
  3.1 17.8 %copy-start.4 = (bf16[2,128,256]{2,1,0:T(8,128)(2,1)S(1)}, bf16[2,128,256]{2,1,0:T(8,128)(2,1)}, u32[]{:S(2)}) copy-start(bf16[2,128,256]{2,1,0:T(8,128)(2,1)} %constant.16.clone.table_ref) | copy-start | bytes 393220
  3.1 20.1 %copy-start.1 = (f32[8,17,8,128]{3,2,1,0:T(8,128)S(1)}, f32[8,17,8,128]{3,2,1,0:T(8,128)}, u32[]{:S(2)}) copy-start(f32[8,17,8,128]{3,2,1,0:T(8,128)} %constant.19.clone.response_ref) | copy-start | bytes 1671172
  3.1 20.1 %copy-start.3 = (bf16[2,144,144]{2,1,0:T(8,128)(2,1)S(1)}, bf16[2,144,144]{2,1,0:T(8,128)(2,1)}, u32[]{:S(2)}) copy-start(bf16[2,144,144]{2,1,0:T(8,128)(2,1)} %constant.17.clone.table_ref) | copy-start | bytes 248836
  18.2 5.0 %collective-permute-start.1 = (f32[16,512]{1,0:T(8,128)S(1)}, f32[16,512]{1,0:T(8,128)S(1)}, u32[]{:S(2)}, u32[]{:S(2)}) collective-permute-start(f32[16,512]{1,0:T(8,128)S(1)} %get-tuple-element.41.sent_ref), channel_id=1, source_target_pairs={{2,0},{3,1},{0,2},{1,3},{6,4},{7,5},{4,6},{5,7},{10,8},{11,9},{8,1... | collective-permute-start | bytes 98312 | tf_op jit(solution)/shard_map/ppermute | solution.py:730
  35.3 1.6 %collective-permute-start.2 = (f32[8,8,1024]{2,1,0:T(8,128)S(1)}, f32[8,8,1024]{2,1,0:T(8,128)S(1)}, u32[]{:S(2)}, u32[]{:S(2)}) collective-permute-start(f32[8,8,1024]{2,1,0:T(8,128)S(1)} %get-tuple-element.49), channel_id=1, source_target_pairs={{0,4},{4,0},{8,12},{12,8},{16,20},{20,16},{24,28},{28,24},{1,5},{5... | collective-permute-start | bytes 786440 | tf_op jit(solution)/shard_map/ppermute | solution.py:734
  37.5 1.6 %collective-permute-start.3 = (f32[8,8,1024]{2,1,0:T(8,128)S(1)}, f32[8,8,1024]{2,1,0:T(8,128)S(1)}, u32[]{:S(2)}, u32[]{:S(2)}) collective-permute-start(f32[8,8,1024]{2,1,0:T(8,128)S(1)} %get-tuple-element.56.time_ref), channel_id=1, source_target_pairs={{0,4},{4,0},{8,12},{12,8},{16,20},{20,16},{24,28},{28,24},{1,5},{5... | collective-permute-start | bytes 786440 | tf_op jit(solution)/shard_map/ppermute | solution.py:734
  51.4 5.5 %collective-permute-start.4 = (f32[16,512]{1,0:T(8,128)S(1)}, f32[16,512]{1,0:T(8,128)S(1)}, u32[]{:S(2)}, u32[]{:S(2)}) collective-permute-start(f32[16,512]{1,0:T(8,128)S(1)} %get-tuple-element.59.sent_ref), channel_id=1, source_target_pairs={{2,0},{3,1},{0,2},{1,3},{6,4},{7,5},{4,6},{5,7},{10,8},{11,9},{8,1... | collective-permute-start | bytes 98312 | tf_op jit(solution)/shard_map/ppermute | solution.py:730
  68.5 2.1 %collective-permute-start.5 = (f32[8,8,1024]{2,1,0:T(8,128)S(1)}, f32[8,8,1024]{2,1,0:T(8,128)S(1)}, u32[]{:S(2)}, u32[]{:S(2)}) collective-permute-start(f32[8,8,1024]{2,1,0:T(8,128)S(1)} %get-tuple-element.65), channel_id=1, source_target_pairs={{0,4},{4,0},{8,12},{12,8},{16,20},{20,16},{24,28},{28,24},{1,5},{5... | collective-permute-start | bytes 786440 | tf_op jit(solution)/shard_map/ppermute | solution.py:734

commit v4 on v2

--- a/solution.py
+++ b/solution.py
@@ -48,16 +48,24 @@
     along_t = hartley(time_length) / np.sqrt(time_length)
     along_z = hartley(depth_length) / np.sqrt(depth_length)
     same_t = np.eye(time_length)
-    forward = np.concatenate([np.kron(along_t, along_z[:, :half]), np.kron(along_t, along_z[:, half : half + 1])], axis=1)
-    edges = np.concatenate([np.kron(same_t, along_z[z : z + 1]) for z in (half, 0)], axis=0)
-    inward = np.kron(along_t, along_z[:half])
     spread = np.zeros((time_length, half + 1, half + 1, time_length))
     for z in range(half + 1):
         spread[:, z, z, :] = along_t
     spread = np.concatenate([spread[:, :half].reshape(time_length * half, -1), spread[:, half].reshape(time_length, -1)])
-    forward = padded(forward, forward.shape[0], rounded_up(forward.shape[1]))
-    spread = padded(spread, rounded_up(spread.shape[0]), rounded_up(spread.shape[1]))
-    return [jnp.asarray(split_table(t)) for t in (forward, edges, inward, spread)]
+    size = rounded_up(spread.shape[0])
+    spread = padded(spread, size, size)
+    forward = padded(np.kron(along_z[:, : half + 1], same_t), depth_length * time_length, size)
+    inward = np.kron(along_z[:half], same_t)
+    return [jnp.asarray(split_table(t)) for t in (spread.T, forward, inward, spread)]
+
+
+def distance_table(time_length, depth_length, plane_sum):
+    half = depth_length // 2
+    total = plane_sum[:, None, None, :] + eigenvalues(time_length)[None, None, :, None]
+    total = total + eigenvalues(depth_length)[None, :, None, None]
+    weight = np.where(total == 0.0, 0.0, 16.0 / np.where(total == 0.0, 1.0, total))
+    angle = 2.0 * np.pi * np.outer(np.arange(half + 1), np.arange(depth_length)) / depth_length
+    return jnp.asarray(np.einsum("dk,ckts->cdts", np.cos(angle) / depth_length, weight).astype(np.float32))
 
 
 def response_table(time_length, depth_length, plane_sum):
@@ -89,42 +97,39 @@
     )
 
 
+def summed(terms):
+    total = terms[0]
+    for term in terms[1:]:
+        total = total + term
+    return total
+
+
 def product(left, right):
-    rows = len(left)
+    left_sum = [[a + b for a, b in row] for row in left]
+    right_sum = [[a + b for a, b in row] for row in right]
     out = []
-    for i in range(rows):
+    for i in range(len(left)):
         row = []
         for j in range(3):
-            real = None
-            imag = None
-            for k in range(3):
-                ar, ai = left[i][k]
-                br, bi = right[k][j]
-                tr = ar * br - ai * bi
-                ti = ar * bi + ai * br
-                real = tr if real is None else real + tr
-                imag = ti if imag is None else imag + ti
-            row.append((real, imag))
+            real = summed([left[i][k][0] * right[k][j][0] for k in range(3)])
+            imag = summed([left[i][k][1] * right[k][j][1] for k in range(3)])
+            both = summed([left_sum[i][k] * right_sum[k][j] for k in range(3)])
+            row.append((real - imag, both - (real + imag)))
         out.append(row)
     return out
 
 
 def product_adjoint(left, right):
-    rows = len(left)
+    left_sum = [[a + b for a, b in row] for row in left]
+    right_sum = [[a - b for a, b in row] for row in right]
     out = []
-    for i in range(rows):
+    for i in range(len(left)):
         row = []
         for j in range(3):
-            real = None
-            imag = None
-            for k in range(3):
-                ar, ai = left[i][k]
-                br, bi = right[j][k]
-                tr = ar * br + ai * bi
-                ti = ai * br - ar * bi
-                real = tr if real is None else real + tr
-                imag = ti if imag is None else imag + ti
-            row.append((real, imag))
+            real = summed([left[i][k][0] * right[j][k][0] for k in range(3)])
+            imag = summed([left[i][k][1] * right[j][k][1] for k in range(3)])
+            both = summed([left_sum[i][k] * right_sum[j][k] for k in range(3)])
+            row.append((real + imag, both - (real - imag)))
         out.append(row)
     return out
 
@@ -137,8 +142,8 @@
         (afr, afi), (abr, abi) = first[f], first[b]
         (bfr, bfi), (bbr, bbi) = second[f], second[b]
         real = afr * bbr - afi * bbi - (abr * bfr - abi * bfi)
-        imag = afr * bbi + afi * bbr - (abr * bfi + abi * bfr)
-        out.append((real, -imag))
+        imag = abr * bfi + abi * bfr - (afr * bbi + afi * bbr)
+        out.append((real, imag))
     return out
 
 
@@ -381,7 +386,7 @@
         add_z_difference(gradient_part(load_link(links_ref, 2, at)), delta, space_ref, edge_ref, at, row)
         return carry
 
-    lax.fori_loop(0, links_ref.shape[-1] // LANES, body, 0, unroll=2)
+    lax.fori_loop(0, links_ref.shape[-1] // LANES, body, 0, unroll=4)
     add_y_difference(space_ref, y_ref)
 
 
@@ -403,8 +408,12 @@
     return (lax.axis_index(time_axis) * half + lax.rem(lax.axis_index(depth_axis), half)) // group_count
 
 
-def modes_kernel(
-    group_count, half_devices, spectral_ref, table_ref, edges_ref, line_ref, plane_ref, modes_ref, sent_ref, total_ref
+def repeated(value, comps):
+    return value if comps == 1 else jnp.concatenate([value] * comps, axis=1)
+
+
+def interface_kernel(
+    group_count, half_devices, spectral_ref, table_ref, distance_ref, anchor_ref, modes_ref, sent_ref, total_ref
 ):
     count, _, comps, width = spectral_ref.shape
     times = count // half_devices
@@ -431,20 +440,27 @@
         pieces.append(jnp.concatenate([own, after] + tail, axis=0))
     data = pieces[0] if comps == 1 else jnp.concatenate(pieces, axis=1)
     data = table_product(table_ref, data)
-    summed = line_ref[...] + plane_ref[group]
+    modes_ref[...] = data
+    sites = 8 * half_devices
+    distance = [repeated(distance_ref[group, d], comps) for d in range(sites + 1)]
+    ahead = None
+    first = None
+    total = None
+    for z in range(sites + 1):
+        part = data[z * times : (z + 1) * times]
+        ahead = distance[sites - z] * part if z == 0 else ahead + distance[sites - z] * part
+        first = distance[z] * part if z == 0 else first + distance[z] * part
+        total = part if z == 0 else total + part
+    sent_ref[0:times] = ahead
+    sent_ref[times:] = first
+    total_ref[...] = total * repeated(anchor_ref[group], comps)
+
+
+def inward_kernel(group_count, comps, modes_ref, forward_ref, inward_ref, line_ref, plane_ref, own_ref, *plane_refs):
+    summed = line_ref[...] + plane_ref[group_of_device("ta", "gz", group_count)]
     weight = jnp.where(summed == 0.0, 0.0, 16.0 / jnp.where(summed == 0.0, 1.0, summed))
-    anchor = jnp.where(summed[0:8] == 0.0, 1.0, 0.0)
-    if comps > 1:
-        weight = jnp.concatenate([weight] * comps, axis=1)
-        anchor = jnp.concatenate([anchor] * comps, axis=1)
-    total_ref[...] = data[0:8] * anchor
-    data = data * weight
-    modes_ref[...] = data
-    sent_ref[...] = table_product(edges_ref, data)
-
-
-def inward_kernel(modes_ref, table_ref, own_ref, *plane_refs):
-    own_ref[...] = table_product(table_ref, modes_ref[...])
+    data = table_product(forward_ref, modes_ref[...]) * repeated(weight, comps)
+    own_ref[...] = table_product(inward_ref, data)
     for plane_ref in plane_refs:
         fill_plane_table(plane_ref, True)
 
@@ -464,21 +480,17 @@
     sites = 8 * half_devices
     columns = own_ref.shape[1]
     group = group_of_device("ta", "gz", group_count)
+    own = own_ref[...]
     first = arrived_ref[0:times]
     after_last = arrived_ref[times:]
     total = total_ref[...]
-    if times > 8:
-        total = jnp.concatenate([total, jnp.zeros((times - 8, columns), jnp.float32)], axis=0)
-    response = [response_ref[group, z] for z in range(sites + 1)]
-    if comps > 1:
-        response = [jnp.concatenate([r] * comps, axis=1) for r in response]
+    response = [repeated(response_ref[group, z], comps) for z in range(sites + 1)]
     rows = []
     for z in range(sites):
         left = sites - z
-        bend = 16.0 / (2.0 * sites) ** 0.5 * 0.5 * z * left
-        value = response[z] * first
+        value = own[z * times : (z + 1) * times] + response[z] * first
         if z:
-            value = value + response[left] * after_last + bend * total
+            value = value + response[left] * after_last + (z * left) * total
         rows.append(value)
     rows.append(after_last + sent_ref[0:times])
     rest = table_ref.shape[2] - (sites + 1) * times
@@ -486,7 +498,7 @@
         rows.append(jnp.zeros((rest, columns), jnp.float32))
     spread = table_product(table_ref, jnp.concatenate(rows, axis=0))
     lines = times * sites
-    data = own_ref[...] + spread[:lines]
+    data = spread[:lines]
     beyond = spread[lines : lines + times]
     every = []
     later = []
@@ -607,7 +619,7 @@
         turn_time(links_ref, at, own, turned_ref)
         return carry
 
-    lax.fori_loop(0, links_ref.shape[-1] // LANES, body, 0, unroll=2)
+    lax.fori_loop(0, links_ref.shape[-1] // LANES, body, 0, unroll=4)
 
 
 def time_links_kernel(rotated_ref, turned_ref, part_ref, arrived_ref, links_out_ref, time_ref):
@@ -620,7 +632,7 @@
             time_ref[c, :, at] = part[c]
         return carry
 
-    lax.fori_loop(0, arrived_ref.shape[-1] // LANES, body, 0, unroll=2)
+    lax.fori_loop(0, arrived_ref.shape[-1] // LANES, body, 0, unroll=4)
 
 
 def yz_links_kernel(
@@ -643,7 +655,7 @@
         add_z_difference(gradient_part(link), delta, space_ref, edge_ref, at, row_index((8, LANES)))
         return carry
 
-    lax.fori_loop(0, chunks, body, 0, unroll=2)
+    lax.fori_loop(0, chunks, body, 0, unroll=4)
     add_y_difference(space_ref, y_ref)
 
 
@@ -661,7 +673,7 @@
         turn_time(links_ref, at, own, turned_ref)
         return carry
 
-    lax.fori_loop(0, chunks, body, 0, unroll=2)
+    lax.fori_loop(0, chunks, body, 0, unroll=4)
 
 
 def last_time_links_kernel(turned_ref, part_ref, arrived_ref, space_ref, out_hbm, time_ref, sent):
@@ -676,7 +688,7 @@
         return carry
 
     for part in range(2):
-        lax.fori_loop(part * chunks // 2, (part + 1) * chunks // 2, body, 0, unroll=2)
+        lax.fori_loop(part * chunks // 2, (part + 1) * chunks // 2, body, 0, unroll=4)
         at = pl.ds(part * sites // 2, sites // 2)
         source = time_ref.at[:, :, :, :, :, :, at]
         target = out_hbm.at[3:4, :, :, :, :, :, at]
@@ -760,11 +772,14 @@
     columns = sites // width
 
     plane_table = pltpu.VMEM((2, sites * 3 // 4, sites // 2), jnp.bfloat16)
-    line_forward, line_edges, line_inward, line_spread = line_tables(time_length, depth_length)
-    line_sum = (eigenvalues(time_length)[:, None] + eigenvalues(depth_length)[None, :]).reshape(-1, 1)
+    line_modes, line_forward, line_inward, line_sites = line_tables(time_length, depth_length)
+    line_sum = (eigenvalues(depth_length)[:, None] + eigenvalues(time_length)[None, :]).reshape(-1, 1)
     line_sum = jnp.asarray(np.broadcast_to(line_sum, (time_length * depth_length, width)).astype(np.float32))
     plane_sum = (eigenvalues(LY)[wave_order()][:, None] + eigenvalues(LX)[None, :]).reshape(columns, width)
     response = response_table(time_length, depth_length, plane_sum)
+    distance = distance_table(time_length, depth_length, plane_sum)
+    anchor = np.where(plane_sum[:, None, :] + eigenvalues(time_length)[None, :, None] == 0.0, 8.0 / depth_length, 0.0)
+    anchor = jnp.asarray(anchor.astype(np.float32))
     plane_sum = jnp.asarray(plane_sum.astype(np.float32).reshape(columns, 1, width))
 
     field = (COMPS, 8, sites)
@@ -796,31 +811,31 @@
     for iteration in range(ITERS):
         spectral = exchanged(spectral.reshape(devices, 13, comps, width))
         modes, sent, total = call(
-            functools.partial(modes_kernel, group_count, half_devices),
-            "filtered_modes",
-            [spectral, line_forward, line_edges, line_sum, plane_sum],
+            functools.partial(interface_kernel, group_count, half_devices),
+            "interface_modes",
+            [spectral, line_modes, distance, anchor],
             [in_vmem()] * 3,
             [
-                shaped(time_length * depth_length, comps * width),
+                shaped(line_modes.shape[1], comps * width),
                 shaped(2 * time_length, comps * width),
-                shaped(8, comps * width),
+                shaped(time_length, comps * width),
             ],
         )
         arrived = passed(sent, "gz", half_devices)
-        first = iteration == 0
+        start = iteration == 0
         own, *tables = call(
-            inward_kernel,
+            functools.partial(inward_kernel, group_count, comps),
             "own_half",
-            [modes, line_inward],
-            [in_vmem()] * (1 + first),
-            [shaped(devices * 8, comps * width)] + [plane_table] * first,
+            [modes, line_forward, line_inward, line_sum, plane_sum],
+            [in_vmem()] * (1 + start),
+            [shaped(devices * 8, comps * width)] + [plane_table] * start,
         )
-        if first:
+        if start:
             backward = tables[0]
         spectral = call(
             functools.partial(couple_kernel, group_count, half_devices),
             "coupled_halves",
-            [own, sent, arrived, total, response, line_spread],
+            [own, sent, arrived, total, response, line_sites],
             in_vmem(),
             shaped(devices, 13, comps, width),
         )

time: 72.1 us -> 71.6 us (level)
  transfers between devices with their start and end apart: 6 -> 6, of which waited for: 4 -> 4; matrix products, arithmetic and copies ran while one was open for 0% -> 0% of each run, Pallas kernels for 8% -> 9%
where the time goes in v4:
time: 71.6 us; the launch traced here: 71.3 us
  blocking collectives  47 us (66%)
  Pallas kernels  12.9 us (18%)
  starting transfers between devices  6.97 us (10%)
  waiting for transfers between devices  4.18 us (6%)
    all_to_all x4, blocking collectives, exchanged(): lax.all_to_all(block, ('ta', 'gz'), split_axis=0, concat_axis=0, axis_ind...  47 us
    pallas_call x17, Pallas kernels, call(): pl.pallas_call(kernel, in_specs=in_specs, out_specs=out_specs, out_shape=...  12.9 us
    ppermute x2, starting transfers between devices, passed(): lax.ppermute(block, axis, [((i - distance) % size, i) for i in range(size)])  5.55 us
    ppermute x2, waiting for transfers between devices, passed(): lax.ppermute(block, axis, [((i - distance) % size, i) for i in range(size)])  3.4 us
  transfers between devices with their start and end apart: 6, of which 4 were waited for; matrix products, arithmetic and copies ran while one was open for 0% of the time, Pallas kernels for 9%

profile of v4, /device:TPU:0, one launch (start us, length us, event | category | flops | bytes accessed | tf_op | source)
XLA Modules:
  0.0 71.3 jit_solution(11986055078765662432)
XLA Ops:
  0.0 1.3 %time_gradient.1 = (bf16[2,768,512]{2,1,0:T(8,128)(2,1)S(1)}, f32[8,8,1024]{2,1,0:T(8,128)S(1)}) custom-call(f32[4,2,3,3,1,8,1024]{6,5,4,3,2,1,0:T(8,128)} %links_ref.5), custom_call_target="tpu_custom_call" | custom-call | tf_op jit(solution)/shard_map/time_gradient/pallas_call | solution.py:725
  1.3 0.5 collective-permute-start
  1.8 0.5 space_gradient.1
  2.4 0.6 collective-permute-done.arrived_ref
  3.0 0.5 gradient_modes.2
  3.5 13.9 %all_to_all.20.spectral_ref = f32[16,13,4,128]{3,2,1,0:T(4,128)S(1)} all-to-all(f32[16,13,4,128]{3,2,1,0:T(4,128)S(1)} %bitcast.3), channel_id=1, replica_groups={{0,1,4,5,8,9,12,13,16,17,20,21,24,25,28,29},{2,3,6,7,10,11,14,15,18,19,..., dimensions={0} | all-to-all | bytes 851968 | tf_op jit(solution)/shard_map/all_to_all | solution.py:752
  17.8 2.7 %collective-permute-start.1 = (f32[16,512]{1,0:T(8,128)S(1)}, f32[16,512]{1,0:T(8,128)S(1)}, u32[]{:S(2)}, u32[]{:S(2)}) collective-permute-start(f32[16,512]{1,0:T(8,128)S(1)} %get-tuple-element.43.sent_ref), channel_id=1, source_target_pairs={{2,0},{3,1},{0,2},{1,3},{6,4},{7,5},{4,6},{5,7},{10,8},{11,9},{8,1... | collective-permute-start | bytes 98312 | tf_op jit(solution)/shard_map/ppermute | solution.py:739
  20.5 1.0 %own_half.2 = (f32[128,512]{1,0:T(8,128)S(1)}, bf16[2,768,512]{2,1,0:T(8,128)(2,1)S(1)}) custom-call(f32[144,512]{1,0:T(8,128)S(1)} %get-tuple-element.41.modes_ref, bf16[2,256,144]{2,1,0:T(8,128)(2,1)S(1)} %copy-done.3, bf16[2,128,256]{2,1,0:T(8,128)(2,1)S(1)} %copy-done.7, f32[256,128]{1,0:T(8,128)S(1)} %copy-done.6, f32[8,1,128]{2,1,0:T(1,128)S(1)} %copy-done.9), custom_call_target="tpu_custom_call" | custom-call | tf_op jit(solution)/shard_map/own_half/pallas_call | solution.py:725
  21.5 1.3 %collective-permute-done.1.arrived_ref = f32[16,512]{1,0:T(8,128)S(1)} collective-permute-done((f32[16,512]{1,0:T(8,128)S(1)}, f32[16,512]{1,0:T(8,128)S(1)}, u32[]{:S(2)}, u32[]{:S(2)}) %collective-permute-start.1) | collective-permute-done | bytes 32800 | tf_op jit(solution)/shard_map/ppermute | solution.py:739
  23.2 11.2 %all_to_all.21.spectral_ref = f32[16,13,4,128]{3,2,1,0:T(4,128)S(1)} all-to-all(f32[16,13,4,128]{3,2,1,0:T(4,128)S(1)} %coupled_halves.2), channel_id=1, replica_groups={{0,1,4,5,8,9,12,13,16,17,20,21,24,25,28,29},{2,3,6,7,10,11,14,15,18,19,..., dimensions={0} | all-to-all | bytes 851968 | tf_op jit(solution)/shard_map/all_to_all | solution.py:752
  34.4 0.5 smooth_field.2
  35.2 1.4 %x_links.1 = (f32[4,2,3,3,1,8,1024]{6,5,4,3,2,1,0:T(8,128)S(1)}, f32[18,8,1024]{2,1,0:T(8,128)S(1)}, f32[18,8,128]{2,1,0:T(8,128)S(1)}, f32[12,8,1024]{2,1,0:T(8,128)S(1)}, f32[8,8,1024]{2,1,0:T(8,128)S(1)}) custom-call(f32[4,2,3,3,1,8,1024]{6,5,4,3,2,1,0:T(8,128)S(1)} %copy-done, f32[8,8,1024]{2,1,0:T(8,128)S(1)} %get-tuple-element.46.smooth_ref, ...), custom_call_target="tpu_custom_call" | custom-call | tf_op jit(solution)/shard_map/x_links/pallas_call | solution.py:725
  36.6 0.5 time_links.1
  37.2 0.4 collective-permute-start.3
  37.5 1.1 %yz_links.1 = (f32[4,2,3,3,1,8,1024]{6,5,4,3,2,1,0:T(8,128)S(1)}, f32[8,8,1024]{2,1,0:T(8,128)S(1)}, f32[2,8,1024]{2,1,0:T(8,128)S(1)}) custom-call(f32[4,2,3,3,1,8,1024]{6,5,4,3,2,1,0:T(8,128)S(1)} %get-tuple-element.52.rotated_ref, f32[4,2,3,3,1,8,1024]{6,5,4,3,2,1,0:T(8,128)S(1)} %copy-done, ...), custom_call_target="tpu_custom_call", output_to_operand_aliasing={{0}: (0, {})} | custom-call | tf_op jit(solution)/shard_map/yz_links/pallas_call | solution.py:725
  38.8 0.5 gradient_modes.3
  39.2 11.2 %all_to_all.22.spectral_ref = f32[16,13,4,128]{3,2,1,0:T(4,128)S(1)} all-to-all(f32[16,13,4,128]{3,2,1,0:T(4,128)S(1)} %bitcast.2), channel_id=1, replica_groups={{0,1,4,5,8,9,12,13,16,17,20,21,24,25,28,29},{2,3,6,7,10,11,14,15,18,19,..., dimensions={0} | all-to-all | bytes 851968 | tf_op jit(solution)/shard_map/all_to_all | solution.py:752
  50.8 2.9 %collective-permute-start.4 = (f32[16,512]{1,0:T(8,128)S(1)}, f32[16,512]{1,0:T(8,128)S(1)}, u32[]{:S(2)}, u32[]{:S(2)}) collective-permute-start(f32[16,512]{1,0:T(8,128)S(1)} %get-tuple-element.61.sent_ref), channel_id=1, source_target_pairs={{2,0},{3,1},{0,2},{1,3},{6,4},{7,5},{4,6},{5,7},{10,8},{11,9},{8,1... | collective-permute-start | bytes 98312 | tf_op jit(solution)/shard_map/ppermute | solution.py:739
  53.7 0.6 own_half.3.own_ref
  54.3 2.1 %collective-permute-done.4.arrived_ref = f32[16,512]{1,0:T(8,128)S(1)} collective-permute-done((f32[16,512]{1,0:T(8,128)S(1)}, f32[16,512]{1,0:T(8,128)S(1)}, u32[]{:S(2)}, u32[]{:S(2)}) %collective-permute-start.4) | collective-permute-done | bytes 32800 | tf_op jit(solution)/shard_map/ppermute | solution.py:739
  56.8 10.7 %all_to_all.23.spectral_ref = f32[16,13,4,128]{3,2,1,0:T(4,128)S(1)} all-to-all(f32[16,13,4,128]{3,2,1,0:T(4,128)S(1)} %coupled_halves.3), channel_id=1, replica_groups={{0,1,4,5,8,9,12,13,16,17,20,21,24,25,28,29},{2,3,6,7,10,11,14,15,18,19,..., dimensions={0} | all-to-all | bytes 851968 | tf_op jit(solution)/shard_map/all_to_all | solution.py:752
  67.4 0.5 smooth_field.3
  68.2 1.7 %last_space_links.1 = (f32[3,2,3,3,1,8,1024]{6,5,4,3,2,1,0:T(8,128)S(1)}, f32[12,8,1024]{2,1,0:T(8,128)S(1)}) custom-call(f32[4,2,3,3,1,8,1024]{6,5,4,3,2,1,0:T(8,128)S(1)} %get-tuple-element.56.links_ref, f32[8,8,1024]{2,1,0:T(8,128)S(1)} %get-tuple-element.63.smooth_ref, f32[8,8,128]{2,1,0:T(8,128)S(1)} %get-tuple-element.64.after_ref), custom_call_target="tpu_custom_call" | custom-call | tf_op jit(solution)/shard_map/last_space_links/pallas_call | solution.py:725
  69.9 1.4 %last_time_links.1 = f32[4,2,3,3,1,8,1024]{6,5,4,3,2,1,0:T(8,128)} custom-call(f32[12,8,1024]{2,1,0:T(8,128)S(1)} %get-tuple-element.65.turned_ref, f32[8,8,1024]{2,1,0:T(8,128)S(1)} %get-tuple-element.66.part_ref, f32[8,8,1024]{2,1,0:T(8,128)S(1)} %collective-permute-done.5.arrived_ref, f32[3,2,3,3,1,8,1024]{6,5,4,3,2,1,0:T(8,128)S(1)} %get-tuple-element.68.space_ref), custom_call_target="tpu_custom_call" | custom-call | tf_op jit(solution)/shard_map/last_time_links/pallas_call | solution.py:725
  (29 shorter events, 2.2 us)
Async XLA Ops:
  0.0 1.8 %copy-start = (f32[4,2,3,3,1,8,1024]{6,5,4,3,2,1,0:T(8,128)S(1)}, f32[4,2,3,3,1,8,1024]{6,5,4,3,2,1,0:T(8,128)}, u32[]{:S(2)}) copy-start(f32[4,2,3,3,1,8,1024]{6,5,4,3,2,1,0:T(8,128)} %links_ref.5) | copy-start | bytes 7077892
  1.3 1.7 %collective-permute-start = (f32[8,8,1024]{2,1,0:T(8,128)S(1)}, f32[8,8,1024]{2,1,0:T(8,128)S(1)}, u32[]{:S(2)}, u32[]{:S(2)}) collective-permute-start(f32[8,8,1024]{2,1,0:T(8,128)S(1)} %get-tuple-element.38.time_ref), channel_id=1, source_target_pairs={{0,4},{4,0},{8,12},{12,8},{16,20},{20,16},{24,28},{28,24},{1,5},{5... | collective-permute-start | bytes 786440 | tf_op jit(solution)/shard_map/ppermute | solution.py:743
  2.3 15.1 %copy-start.2 = (f32[8,17,8,128]{3,2,1,0:T(8,128)S(1)}, f32[8,17,8,128]{3,2,1,0:T(8,128)}, u32[]{:S(2)}) copy-start(f32[8,17,8,128]{3,2,1,0:T(8,128)} %constant.24.clone.distance_ref) | copy-start | bytes 1671172
  2.3 15.1 %copy-start.5 = (bf16[2,144,144]{2,1,0:T(8,128)(2,1)S(1)}, bf16[2,144,144]{2,1,0:T(8,128)(2,1)}, u32[]{:S(2)}) copy-start(bf16[2,144,144]{2,1,0:T(8,128)(2,1)} %constant.18.clone.table_ref) | copy-start | bytes 248836
  2.3 15.1 %copy-start.8 = (f32[8,8,128]{2,1,0:T(8,128)S(1)}, f32[8,8,128]{2,1,0:T(8,128)}, u32[]{:S(2)}) copy-start(f32[8,8,128]{2,1,0:T(8,128)} %constant.25.clone.anchor_ref) | copy-start | bytes 98308
  3.0 17.5 %copy-start.3 = (bf16[2,256,144]{2,1,0:T(8,128)(2,1)S(1)}, bf16[2,256,144]{2,1,0:T(8,128)(2,1)}, u32[]{:S(2)}) copy-start(bf16[2,256,144]{2,1,0:T(8,128)(2,1)} %constant.19.clone.forward_ref) | copy-start | bytes 442372
  3.0 17.5 %copy-start.6 = (f32[256,128]{1,0:T(8,128)S(1)}, f32[256,128]{1,0:T(8,128)}, u32[]{:S(2)}) copy-start(f32[256,128]{1,0:T(8,128)} %constant.22.clone.line_ref) | copy-start | bytes 393220
  3.0 17.5 %copy-start.7 = (bf16[2,128,256]{2,1,0:T(8,128)(2,1)S(1)}, bf16[2,128,256]{2,1,0:T(8,128)(2,1)}, u32[]{:S(2)}) copy-start(bf16[2,128,256]{2,1,0:T(8,128)(2,1)} %constant.20.clone.inward_ref) | copy-start | bytes 393220
  3.0 17.5 %copy-start.9 = (f32[8,1,128]{2,1,0:T(1,128)S(1)}, f32[8,1,128]{2,1,0:T(1,128)}, u32[]{:S(2)}) copy-start(f32[8,1,128]{2,1,0:T(1,128)} %constant.26.clone.plane_ref) | copy-start | bytes 12292
  3.0 19.9 %copy-start.1 = (f32[8,17,8,128]{3,2,1,0:T(8,128)S(1)}, f32[8,17,8,128]{3,2,1,0:T(8,128)}, u32[]{:S(2)}) copy-start(f32[8,17,8,128]{3,2,1,0:T(8,128)} %constant.23.clone.response_ref) | copy-start | bytes 1671172
  3.0 19.9 %copy-start.4 = (bf16[2,144,144]{2,1,0:T(8,128)(2,1)S(1)}, bf16[2,144,144]{2,1,0:T(8,128)(2,1)}, u32[]{:S(2)}) copy-start(bf16[2,144,144]{2,1,0:T(8,128)(2,1)} %constant.21.clone.table_ref) | copy-start | bytes 248836
  17.8 5.0 %collective-permute-start.1 = (f32[16,512]{1,0:T(8,128)S(1)}, f32[16,512]{1,0:T(8,128)S(1)}, u32[]{:S(2)}, u32[]{:S(2)}) collective-permute-start(f32[16,512]{1,0:T(8,128)S(1)} %get-tuple-element.43.sent_ref), channel_id=1, source_target_pairs={{2,0},{3,1},{0,2},{1,3},{6,4},{7,5},{4,6},{5,7},{10,8},{11,9},{8,1... | collective-permute-start | bytes 98312 | tf_op jit(solution)/shard_map/ppermute | solution.py:739
  35.0 1.6 %collective-permute-start.2 = (f32[8,8,1024]{2,1,0:T(8,128)S(1)}, f32[8,8,1024]{2,1,0:T(8,128)S(1)}, u32[]{:S(2)}, u32[]{:S(2)}) collective-permute-start(f32[8,8,1024]{2,1,0:T(8,128)S(1)} %get-tuple-element.51), channel_id=1, source_target_pairs={{0,4},{4,0},{8,12},{12,8},{16,20},{20,16},{24,28},{28,24},{1,5},{5... | collective-permute-start | bytes 786440 | tf_op jit(solution)/shard_map/ppermute | solution.py:743
  37.2 1.6 %collective-permute-start.3 = (f32[8,8,1024]{2,1,0:T(8,128)S(1)}, f32[8,8,1024]{2,1,0:T(8,128)S(1)}, u32[]{:S(2)}, u32[]{:S(2)}) collective-permute-start(f32[8,8,1024]{2,1,0:T(8,128)S(1)} %get-tuple-element.58.time_ref), channel_id=1, source_target_pairs={{0,4},{4,0},{8,12},{12,8},{16,20},{20,16},{24,28},{28,24},{1,5},{5... | collective-permute-start | bytes 786440 | tf_op jit(solution)/shard_map/ppermute | solution.py:743
  50.8 5.6 %collective-permute-start.4 = (f32[16,512]{1,0:T(8,128)S(1)}, f32[16,512]{1,0:T(8,128)S(1)}, u32[]{:S(2)}, u32[]{:S(2)}) collective-permute-start(f32[16,512]{1,0:T(8,128)S(1)} %get-tuple-element.61.sent_ref), channel_id=1, source_target_pairs={{2,0},{3,1},{0,2},{1,3},{6,4},{7,5},{4,6},{5,7},{10,8},{11,9},{8,1... | collective-permute-start | bytes 98312 | tf_op jit(solution)/shard_map/ppermute | solution.py:739
  68.0 1.9 %collective-permute-start.5 = (f32[8,8,1024]{2,1,0:T(8,128)S(1)}, f32[8,8,1024]{2,1,0:T(8,128)S(1)}, u32[]{:S(2)}, u32[]{:S(2)}) collective-permute-start(f32[8,8,1024]{2,1,0:T(8,128)S(1)} %get-tuple-element.67), channel_id=1, source_target_pairs={{0,4},{4,0},{8,12},{12,8},{16,20},{20,16},{24,28},{28,24},{1,5},{5... | collective-permute-start | bytes 786440 | tf_op jit(solution)/shard_map/ppermute | solution.py:743

commit v5 on v4

--- a/solution.py
+++ b/solution.py
@@ -521,7 +521,7 @@
 
 
 def smooth_kernel(
-    group_count, spectral_ref, table_ref, smooth_ref, after_ref, part_ref, sent_ref, rows_ref
+    group_count, spectral_ref, table_ref, smooth_ref, after_ref, part_ref, sent_ref
 ):
     count, _, _, width = spectral_ref.shape
     pieces = ([], [], [])
@@ -539,10 +539,9 @@
     smooth_ref[...] = smooth
     part_ref[...] = part
     sent_ref[...] = jnp.where(first_core(), part, smooth)
-    rows_ref[...] = total[rows + 4 * COMPS :]
-    for c in range(COMPS):
-        for k in range(sites // LANES):
-            after_ref[c, k : k + 1, :] = rows_ref[c : c + 1, k * LANES : (k + 1) * LANES]
+    after = total[rows + 4 * COMPS :]
+    for k in range(sites // LANES):
+        after_ref[:, k, :] = after[:, k * LANES : (k + 1) * LANES]
 
 
 def first_core():
@@ -659,25 +658,36 @@
     add_y_difference(space_ref, y_ref)
 
 
-def last_space_links_kernel(links_ref, smooth_ref, after_ref, out_ref, turned_ref, gauge_ref, beyond_ref):
+def last_space_links_kernel(
+    links_ref, smooth_ref, after_ref, out_hbm, yz_ref, turned_ref, x_ref, gauge_ref, beyond_ref, sent
+):
     chunks = links_ref.shape[-1] // LANES
     gauge_matrices(smooth_ref, after_ref, gauge_ref, beyond_ref)
 
-    def body(step, carry):
+    def along_x(step, carry):
+        at = chunk_at(step)
+        own = [gauge_ref[n, :, at] for n in range(18)]
+        store_link(x_ref, 0, at, rotate_x(links_ref, at, own))
+        return carry
+
+    def along_yz(step, carry):
         at = chunk_at(step)
         at_next = chunk_at(lax.rem(step + 1, chunks))
         own = [gauge_ref[n, :, at] for n in range(18)]
-        store_link(out_ref, 0, at, rotate_x(links_ref, at, own))
-        store_link(out_ref, 1, at, rotate_y(links_ref, at, own, gauge_ref, at_next))
-        store_link(out_ref, 2, at, rotate_z(links_ref, at, own, beyond_ref, step))
+        store_link(yz_ref, 0, at, rotate_y(links_ref, at, own, gauge_ref, at_next))
+        store_link(yz_ref, 1, at, rotate_z(links_ref, at, own, beyond_ref, step))
         turn_time(links_ref, at, own, turned_ref)
         return carry
 
-    lax.fori_loop(0, chunks, body, 0, unroll=4)
-
-
-def last_time_links_kernel(turned_ref, part_ref, arrived_ref, space_ref, out_hbm, time_ref, sent):
-    copies = [pltpu.make_async_copy(space_ref, out_hbm.at[0:3], sent.at[0])]
+    lax.fori_loop(0, chunks, along_x, 0, unroll=4)
+    copy = pltpu.make_async_copy(x_ref, out_hbm.at[0:1], sent)
+    copy.start()
+    lax.fori_loop(0, chunks, along_yz, 0, unroll=4)
+    copy.wait()
+
+
+def last_time_links_kernel(turned_ref, part_ref, arrived_ref, yz_ref, x_hbm, out_hbm, time_ref, sent):
+    copies = [pltpu.make_async_copy(yz_ref, out_hbm.at[1:3], sent.at[0])]
     copies[0].start()
     sites = arrived_ref.shape[-1]
     chunks = sites // LANES
@@ -846,7 +856,6 @@
             [spectral, backward],
             [in_vmem()] * 4,
             [shaped(*field), shaped(COMPS, chunks, LANES), shaped(*field), shaped(*field)],
-            [scratch(COMPS, sites)],
         )
         arrived = from_other_core(sent)
         gauge_scratch = [scratch(18, 8, sites), scratch(18, chunks, LANES)]
@@ -886,21 +895,23 @@
                 send_kernel, "gradient_modes", [space, time, arrived, edge, forward], in_vmem(), sent_shape
             )
         else:
-            space_links, turned = call(
+            rotated, yz_links, turned = call(
                 last_space_links_kernel,
                 "last_space_links",
                 [links, smooth, after],
-                [in_vmem()] * 2,
-                [shaped(3, *local[1:]), shaped(12, 8, sites)],
-                gauge_scratch,
+                [in_hbm(), in_vmem(), in_vmem()],
+                [pltpu.HBM(local, jnp.float32), shaped(2, *local[1:]), shaped(12, 8, sites)],
+                [scratch(1, *local[1:])] + gauge_scratch + [pltpu.SemaphoreType.DMA],
             )
             rotated = call(
                 last_time_links_kernel,
                 "last_time_links",
-                [turned, part, arrived, space_links],
+                [turned, part, arrived, yz_links, rotated],
                 in_hbm(),
                 pltpu.HBM(local, jnp.float32),
                 [scratch(1, *local[1:]), pltpu.SemaphoreType.DMA((3,))],
+                in_specs=[in_vmem()] * 4 + [in_hbm()],
+                aliases={4: 0},
             )
     return rotated
 

time: 71.6 us -> 71.6 us (level)
  no operation moved by 1% of the time
where the time goes in v5:
time: 71.6 us; the launch traced here: 71.3 us
  blocking collectives  47 us (66%)
  Pallas kernels  12.8 us (18%)
  starting transfers between devices  6.97 us (10%)
  waiting for transfers between devices  4.18 us (6%)
    all_to_all x4, blocking collectives, exchanged(): lax.all_to_all(block, ('ta', 'gz'), split_axis=0, concat_axis=0, axis_ind...  47 us
    pallas_call x17, Pallas kernels, call(): pl.pallas_call(kernel, in_specs=in_specs, out_specs=out_specs, out_shape=...  12.8 us
    ppermute x2, starting transfers between devices, passed(): lax.ppermute(block, axis, [((i - distance) % size, i) for i in range(size)])  5.55 us
    ppermute x2, waiting for transfers between devices, passed(): lax.ppermute(block, axis, [((i - distance) % size, i) for i in range(size)])  3.4 us
  transfers between devices with their start and end apart: 6, of which 4 were waited for; matrix products, arithmetic and copies ran while one was open for 0% of the time, Pallas kernels for 9%

profile of v5, /device:TPU:0, one launch (start us, length us, event | category | flops | bytes accessed | tf_op | source)
XLA Modules:
  0.0 71.3 jit_solution(17107815365237616227)
XLA Ops:
  0.0 1.3 %time_gradient.1 = (bf16[2,768,512]{2,1,0:T(8,128)(2,1)S(1)}, f32[8,8,1024]{2,1,0:T(8,128)S(1)}) custom-call(f32[4,2,3,3,1,8,1024]{6,5,4,3,2,1,0:T(8,128)} %links_ref.5), custom_call_target="tpu_custom_call" | custom-call | tf_op jit(solution)/shard_map/time_gradient/pallas_call | solution.py:735
  1.3 0.5 collective-permute-start
  1.8 0.5 space_gradient.1
  2.4 0.6 collective-permute-done.arrived_ref
  3.0 0.5 gradient_modes.2
  3.5 13.9 %all_to_all.20.spectral_ref = f32[16,13,4,128]{3,2,1,0:T(4,128)S(1)} all-to-all(f32[16,13,4,128]{3,2,1,0:T(4,128)S(1)} %bitcast.3), channel_id=1, replica_groups={{0,1,4,5,8,9,12,13,16,17,20,21,24,25,28,29},{2,3,6,7,10,11,14,15,18,19,..., dimensions={0} | all-to-all | bytes 851968 | tf_op jit(solution)/shard_map/all_to_all | solution.py:762
  17.8 2.7 %collective-permute-start.1 = (f32[16,512]{1,0:T(8,128)S(1)}, f32[16,512]{1,0:T(8,128)S(1)}, u32[]{:S(2)}, u32[]{:S(2)}) collective-permute-start(f32[16,512]{1,0:T(8,128)S(1)} %get-tuple-element.44.sent_ref), channel_id=1, source_target_pairs={{2,0},{3,1},{0,2},{1,3},{6,4},{7,5},{4,6},{5,7},{10,8},{11,9},{8,1... | collective-permute-start | bytes 98312 | tf_op jit(solution)/shard_map/ppermute | solution.py:749
  20.5 1.0 %own_half.2 = (f32[128,512]{1,0:T(8,128)S(1)}, bf16[2,768,512]{2,1,0:T(8,128)(2,1)S(1)}) custom-call(f32[144,512]{1,0:T(8,128)S(1)} %get-tuple-element.42.modes_ref, bf16[2,256,144]{2,1,0:T(8,128)(2,1)S(1)} %copy-done.3, bf16[2,128,256]{2,1,0:T(8,128)(2,1)S(1)} %copy-done.7, f32[256,128]{1,0:T(8,128)S(1)} %copy-done.6, f32[8,1,128]{2,1,0:T(1,128)S(1)} %copy-done.9), custom_call_target="tpu_custom_call" | custom-call | tf_op jit(solution)/shard_map/own_half/pallas_call | solution.py:735
  21.5 1.3 %collective-permute-done.1.arrived_ref = f32[16,512]{1,0:T(8,128)S(1)} collective-permute-done((f32[16,512]{1,0:T(8,128)S(1)}, f32[16,512]{1,0:T(8,128)S(1)}, u32[]{:S(2)}, u32[]{:S(2)}) %collective-permute-start.1) | collective-permute-done | bytes 32800 | tf_op jit(solution)/shard_map/ppermute | solution.py:749
  23.2 11.2 %all_to_all.21.spectral_ref = f32[16,13,4,128]{3,2,1,0:T(4,128)S(1)} all-to-all(f32[16,13,4,128]{3,2,1,0:T(4,128)S(1)} %coupled_halves.2), channel_id=1, replica_groups={{0,1,4,5,8,9,12,13,16,17,20,21,24,25,28,29},{2,3,6,7,10,11,14,15,18,19,..., dimensions={0} | all-to-all | bytes 851968 | tf_op jit(solution)/shard_map/all_to_all | solution.py:762
  34.4 0.5 smooth_field.2
  35.2 1.4 %x_links.1 = (f32[4,2,3,3,1,8,1024]{6,5,4,3,2,1,0:T(8,128)S(1)}, f32[18,8,1024]{2,1,0:T(8,128)S(1)}, f32[18,8,128]{2,1,0:T(8,128)S(1)}, f32[12,8,1024]{2,1,0:T(8,128)S(1)}, f32[8,8,1024]{2,1,0:T(8,128)S(1)}) custom-call(f32[4,2,3,3,1,8,1024]{6,5,4,3,2,1,0:T(8,128)S(1)} %copy-done, f32[8,8,1024]{2,1,0:T(8,128)S(1)} %get-tuple-element.47.smooth_ref, ...), custom_call_target="tpu_custom_call" | custom-call | tf_op jit(solution)/shard_map/x_links/pallas_call | solution.py:735
  36.6 0.5 time_links.1
  37.2 0.4 collective-permute-start.3
  37.5 1.1 %yz_links.1 = (f32[4,2,3,3,1,8,1024]{6,5,4,3,2,1,0:T(8,128)S(1)}, f32[8,8,1024]{2,1,0:T(8,128)S(1)}, f32[2,8,1024]{2,1,0:T(8,128)S(1)}) custom-call(f32[4,2,3,3,1,8,1024]{6,5,4,3,2,1,0:T(8,128)S(1)} %get-tuple-element.53.rotated_ref, f32[4,2,3,3,1,8,1024]{6,5,4,3,2,1,0:T(8,128)S(1)} %copy-done, ...), custom_call_target="tpu_custom_call", output_to_operand_aliasing={{0}: (0, {})} | custom-call | tf_op jit(solution)/shard_map/yz_links/pallas_call | solution.py:735
  38.8 0.5 gradient_modes.3
  39.2 11.2 %all_to_all.22.spectral_ref = f32[16,13,4,128]{3,2,1,0:T(4,128)S(1)} all-to-all(f32[16,13,4,128]{3,2,1,0:T(4,128)S(1)} %bitcast.2), channel_id=1, replica_groups={{0,1,4,5,8,9,12,13,16,17,20,21,24,25,28,29},{2,3,6,7,10,11,14,15,18,19,..., dimensions={0} | all-to-all | bytes 851968 | tf_op jit(solution)/shard_map/all_to_all | solution.py:762
  50.8 2.9 %collective-permute-start.4 = (f32[16,512]{1,0:T(8,128)S(1)}, f32[16,512]{1,0:T(8,128)S(1)}, u32[]{:S(2)}, u32[]{:S(2)}) collective-permute-start(f32[16,512]{1,0:T(8,128)S(1)} %get-tuple-element.62.sent_ref), channel_id=1, source_target_pairs={{2,0},{3,1},{0,2},{1,3},{6,4},{7,5},{4,6},{5,7},{10,8},{11,9},{8,1... | collective-permute-start | bytes 98312 | tf_op jit(solution)/shard_map/ppermute | solution.py:749
  53.7 0.6 own_half.3.own_ref
  54.3 2.1 %collective-permute-done.4.arrived_ref = f32[16,512]{1,0:T(8,128)S(1)} collective-permute-done((f32[16,512]{1,0:T(8,128)S(1)}, f32[16,512]{1,0:T(8,128)S(1)}, u32[]{:S(2)}, u32[]{:S(2)}) %collective-permute-start.4) | collective-permute-done | bytes 32800 | tf_op jit(solution)/shard_map/ppermute | solution.py:749
  56.8 10.7 %all_to_all.23.spectral_ref = f32[16,13,4,128]{3,2,1,0:T(4,128)S(1)} all-to-all(f32[16,13,4,128]{3,2,1,0:T(4,128)S(1)} %coupled_halves.3), channel_id=1, replica_groups={{0,1,4,5,8,9,12,13,16,17,20,21,24,25,28,29},{2,3,6,7,10,11,14,15,18,19,..., dimensions={0} | all-to-all | bytes 851968 | tf_op jit(solution)/shard_map/all_to_all | solution.py:762
  67.4 0.5 smooth_field.3
  68.2 1.8 %last_space_links.1 = (f32[4,2,3,3,1,8,1024]{6,5,4,3,2,1,0:T(8,128)}, f32[2,2,3,3,1,8,1024]{6,5,4,3,2,1,0:T(8,128)S(1)}, f32[12,8,1024]{2,1,0:T(8,128)S(1)}) custom-call(f32[4,2,3,3,1,8,1024]{6,5,4,3,2,1,0:T(8,128)S(1)} %get-tuple-element.57.links_ref, f32[8,8,1024]{2,1,0:T(8,128)S(1)} %get-tuple-element.64.smooth_ref, ...), custom_call_target="tpu_custom_call" | custom-call | tf_op jit(solution)/shard_map/last_space_links/pallas_call | solution.py:735
  70.0 1.2 %last_time_links.1 = f32[4,2,3,3,1,8,1024]{6,5,4,3,2,1,0:T(8,128)} custom-call(f32[12,8,1024]{2,1,0:T(8,128)S(1)} %get-tuple-element.66.turned_ref, f32[8,8,1024]{2,1,0:T(8,128)S(1)} %get-tuple-element.67.part_ref, f32[8,8,1024]{2,1,0:T(8,128)S(1)} %collective-permute-done.5.arrived_ref, ...), custom_call_target="tpu_custom_call", output_to_operand_aliasing={{}: (4, {})} | custom-call | tf_op jit(solution)/shard_map/last_time_links/pallas_call | solution.py:735
  (29 shorter events, 2.2 us)
Async XLA Ops:
  0.0 1.8 %copy-start = (f32[4,2,3,3,1,8,1024]{6,5,4,3,2,1,0:T(8,128)S(1)}, f32[4,2,3,3,1,8,1024]{6,5,4,3,2,1,0:T(8,128)}, u32[]{:S(2)}) copy-start(f32[4,2,3,3,1,8,1024]{6,5,4,3,2,1,0:T(8,128)} %links_ref.5) | copy-start | bytes 7077892
  1.3 1.7 %collective-permute-start = (f32[8,8,1024]{2,1,0:T(8,128)S(1)}, f32[8,8,1024]{2,1,0:T(8,128)S(1)}, u32[]{:S(2)}, u32[]{:S(2)}) collective-permute-start(f32[8,8,1024]{2,1,0:T(8,128)S(1)} %get-tuple-element.39.time_ref), channel_id=1, source_target_pairs={{0,4},{4,0},{8,12},{12,8},{16,20},{20,16},{24,28},{28,24},{1,5},{5... | collective-permute-start | bytes 786440 | tf_op jit(solution)/shard_map/ppermute | solution.py:753
  2.3 15.1 %copy-start.2 = (f32[8,17,8,128]{3,2,1,0:T(8,128)S(1)}, f32[8,17,8,128]{3,2,1,0:T(8,128)}, u32[]{:S(2)}) copy-start(f32[8,17,8,128]{3,2,1,0:T(8,128)} %constant.24.clone.distance_ref) | copy-start | bytes 1671172
  2.3 15.1 %copy-start.5 = (bf16[2,144,144]{2,1,0:T(8,128)(2,1)S(1)}, bf16[2,144,144]{2,1,0:T(8,128)(2,1)}, u32[]{:S(2)}) copy-start(bf16[2,144,144]{2,1,0:T(8,128)(2,1)} %constant.18.clone.table_ref) | copy-start | bytes 248836
  2.3 15.1 %copy-start.8 = (f32[8,8,128]{2,1,0:T(8,128)S(1)}, f32[8,8,128]{2,1,0:T(8,128)}, u32[]{:S(2)}) copy-start(f32[8,8,128]{2,1,0:T(8,128)} %constant.25.clone.anchor_ref) | copy-start | bytes 98308
  3.0 17.5 %copy-start.3 = (bf16[2,256,144]{2,1,0:T(8,128)(2,1)S(1)}, bf16[2,256,144]{2,1,0:T(8,128)(2,1)}, u32[]{:S(2)}) copy-start(bf16[2,256,144]{2,1,0:T(8,128)(2,1)} %constant.19.clone.forward_ref) | copy-start | bytes 442372
  3.0 17.5 %copy-start.6 = (f32[256,128]{1,0:T(8,128)S(1)}, f32[256,128]{1,0:T(8,128)}, u32[]{:S(2)}) copy-start(f32[256,128]{1,0:T(8,128)} %constant.22.clone.line_ref) | copy-start | bytes 393220
  3.0 17.5 %copy-start.7 = (bf16[2,128,256]{2,1,0:T(8,128)(2,1)S(1)}, bf16[2,128,256]{2,1,0:T(8,128)(2,1)}, u32[]{:S(2)}) copy-start(bf16[2,128,256]{2,1,0:T(8,128)(2,1)} %constant.20.clone.inward_ref) | copy-start | bytes 393220
  3.0 17.5 %copy-start.9 = (f32[8,1,128]{2,1,0:T(1,128)S(1)}, f32[8,1,128]{2,1,0:T(1,128)}, u32[]{:S(2)}) copy-start(f32[8,1,128]{2,1,0:T(1,128)} %constant.26.clone.plane_ref) | copy-start | bytes 12292
  3.0 19.9 %copy-start.1 = (f32[8,17,8,128]{3,2,1,0:T(8,128)S(1)}, f32[8,17,8,128]{3,2,1,0:T(8,128)}, u32[]{:S(2)}) copy-start(f32[8,17,8,128]{3,2,1,0:T(8,128)} %constant.23.clone.response_ref) | copy-start | bytes 1671172
  3.0 19.9 %copy-start.4 = (bf16[2,144,144]{2,1,0:T(8,128)(2,1)S(1)}, bf16[2,144,144]{2,1,0:T(8,128)(2,1)}, u32[]{:S(2)}) copy-start(bf16[2,144,144]{2,1,0:T(8,128)(2,1)} %constant.21.clone.table_ref) | copy-start | bytes 248836
  17.8 5.0 %collective-permute-start.1 = (f32[16,512]{1,0:T(8,128)S(1)}, f32[16,512]{1,0:T(8,128)S(1)}, u32[]{:S(2)}, u32[]{:S(2)}) collective-permute-start(f32[16,512]{1,0:T(8,128)S(1)} %get-tuple-element.44.sent_ref), channel_id=1, source_target_pairs={{2,0},{3,1},{0,2},{1,3},{6,4},{7,5},{4,6},{5,7},{10,8},{11,9},{8,1... | collective-permute-start | bytes 98312 | tf_op jit(solution)/shard_map/ppermute | solution.py:749
  35.0 1.6 %collective-permute-start.2 = (f32[8,8,1024]{2,1,0:T(8,128)S(1)}, f32[8,8,1024]{2,1,0:T(8,128)S(1)}, u32[]{:S(2)}, u32[]{:S(2)}) collective-permute-start(f32[8,8,1024]{2,1,0:T(8,128)S(1)} %get-tuple-element.52), channel_id=1, source_target_pairs={{0,4},{4,0},{8,12},{12,8},{16,20},{20,16},{24,28},{28,24},{1,5},{5... | collective-permute-start | bytes 786440 | tf_op jit(solution)/shard_map/ppermute | solution.py:753
  37.2 1.6 %collective-permute-start.3 = (f32[8,8,1024]{2,1,0:T(8,128)S(1)}, f32[8,8,1024]{2,1,0:T(8,128)S(1)}, u32[]{:S(2)}, u32[]{:S(2)}) collective-permute-start(f32[8,8,1024]{2,1,0:T(8,128)S(1)} %get-tuple-element.59.time_ref), channel_id=1, source_target_pairs={{0,4},{4,0},{8,12},{12,8},{16,20},{20,16},{24,28},{28,24},{1,5},{5... | collective-permute-start | bytes 786440 | tf_op jit(solution)/shard_map/ppermute | solution.py:753
  50.8 5.6 %collective-permute-start.4 = (f32[16,512]{1,0:T(8,128)S(1)}, f32[16,512]{1,0:T(8,128)S(1)}, u32[]{:S(2)}, u32[]{:S(2)}) collective-permute-start(f32[16,512]{1,0:T(8,128)S(1)} %get-tuple-element.62.sent_ref), channel_id=1, source_target_pairs={{2,0},{3,1},{0,2},{1,3},{6,4},{7,5},{4,6},{5,7},{10,8},{11,9},{8,1... | collective-permute-start | bytes 98312 | tf_op jit(solution)/shard_map/ppermute | solution.py:749
  67.9 2.1 %collective-permute-start.5 = (f32[8,8,1024]{2,1,0:T(8,128)S(1)}, f32[8,8,1024]{2,1,0:T(8,128)S(1)}, u32[]{:S(2)}, u32[]{:S(2)}) collective-permute-start(f32[8,8,1024]{2,1,0:T(8,128)S(1)} %get-tuple-element.68), channel_id=1, source_target_pairs={{0,4},{4,0},{8,12},{12,8},{16,20},{20,16},{24,28},{28,24},{1,5},{5... | collective-permute-start | bytes 786440 | tf_op jit(solution)/shard_map/ppermute | solution.py:753

commit v6 on v5

--- a/solution.py
+++ b/solution.py
@@ -548,20 +548,17 @@
     return lax.rem(lax.axis_index("ta"), 2) == 0
 
 
-def gauge_matrices(smooth_ref, after_ref, gauge_ref, beyond_ref):
-    chunks = smooth_ref.shape[-1] // LANES
+def gauge_after(after_ref, beyond_ref):
     beyond = flat(exponential([after_ref[c] for c in range(COMPS)]))
     for n in range(18):
         beyond_ref[n] = beyond[n]
 
-    def matrices(step, carry):
-        at = chunk_at(step)
-        gauge = flat(exponential([smooth_ref[c, :, at] for c in range(COMPS)]))
-        for n in range(18):
-            gauge_ref[n, :, at] = gauge[n]
-        return carry
-
-    lax.fori_loop(0, chunks, matrices, 0, unroll=4)
+
+def gauge_here(smooth_ref, gauge_ref, at):
+    gauge = flat(exponential([smooth_ref[c, :, at] for c in range(COMPS)]))
+    for n in range(18):
+        gauge_ref[n, :, at] = gauge[n]
+    return gauge
 
 
 def rotate_x(links_ref, at, own):
@@ -604,12 +601,12 @@
 def x_links_kernel(
     links_ref, smooth_ref, after_ref, links_out_ref, gauge_ref, beyond_ref, turned_ref, delta_ref
 ):
-    gauge_matrices(smooth_ref, after_ref, gauge_ref, beyond_ref)
+    gauge_after(after_ref, beyond_ref)
 
     def body(step, carry):
         at = chunk_at(step)
         first_x = lane_index((8, LANES)) % LX == 0
-        own = [gauge_ref[n, :, at] for n in range(18)]
+        own = gauge_here(smooth_ref, gauge_ref, at)
         link = rotate_x(links_ref, at, own)
         store_link(links_out_ref, 0, at, link)
         part = gradient_part(link)
@@ -662,11 +659,11 @@
     links_ref, smooth_ref, after_ref, out_hbm, yz_ref, turned_ref, x_ref, gauge_ref, beyond_ref, sent
 ):
     chunks = links_ref.shape[-1] // LANES
-    gauge_matrices(smooth_ref, after_ref, gauge_ref, beyond_ref)
+    gauge_after(after_ref, beyond_ref)
 
     def along_x(step, carry):
         at = chunk_at(step)
-        own = [gauge_ref[n, :, at] for n in range(18)]
+        own = gauge_here(smooth_ref, gauge_ref, at)
         store_link(x_ref, 0, at, rotate_x(links_ref, at, own))
         return carry
 

time: 71.6 us -> 71.4 us (level)
  transfers between devices with their start and end apart: 6 -> 6, of which waited for: 4 -> 5; matrix products, arithmetic and copies ran while one was open for 0% -> 0% of each run, Pallas kernels for 9% -> 8%
where the time goes in v6:
time: 71.4 us; the launch traced here: 71.1 us
  blocking collectives  47.1 us (66%)
  Pallas kernels  12.5 us (18%)
  starting transfers between devices  6.87 us (10%)
  waiting for transfers between devices  4.48 us (6%)
    all_to_all x4, blocking collectives, exchanged(): lax.all_to_all(block, ('ta', 'gz'), split_axis=0, concat_axis=0, axis_ind...  47.1 us
    pallas_call x17, Pallas kernels, call(): pl.pallas_call(kernel, in_specs=in_specs, out_specs=out_specs, out_shape=...  12.5 us
    ppermute x2, starting transfers between devices, passed(): lax.ppermute(block, axis, [((i - distance) % size, i) for i in range(size)])  5.55 us
    ppermute x2, waiting for transfers between devices, passed(): lax.ppermute(block, axis, [((i - distance) % size, i) for i in range(size)])  3.4 us
  transfers between devices with their start and end apart: 6, of which 5 were waited for; matrix products, arithmetic and copies ran while one was open for 0% of the time, Pallas kernels for 8%

profile of v6, /device:TPU:0, one launch (start us, length us, event | category | flops | bytes accessed | tf_op | source)
XLA Modules:
  0.0 71.1 jit_solution(5067347665726649837)
XLA Ops:
  0.0 1.3 %time_gradient.1 = (bf16[2,768,512]{2,1,0:T(8,128)(2,1)S(1)}, f32[8,8,1024]{2,1,0:T(8,128)S(1)}) custom-call(f32[4,2,3,3,1,8,1024]{6,5,4,3,2,1,0:T(8,128)} %links_ref.5), custom_call_target="tpu_custom_call" | custom-call | tf_op jit(solution)/shard_map/time_gradient/pallas_call | solution.py:732
  1.3 0.5 collective-permute-start
  1.8 0.5 space_gradient.1
  2.4 0.6 collective-permute-done.arrived_ref
  3.0 0.5 gradient_modes.2
  3.5 13.9 %all_to_all.20.spectral_ref = f32[16,13,4,128]{3,2,1,0:T(4,128)S(1)} all-to-all(f32[16,13,4,128]{3,2,1,0:T(4,128)S(1)} %bitcast.3), channel_id=1, replica_groups={{0,1,4,5,8,9,12,13,16,17,20,21,24,25,28,29},{2,3,6,7,10,11,14,15,18,19,..., dimensions={0} | all-to-all | bytes 851968 | tf_op jit(solution)/shard_map/all_to_all | solution.py:759
  17.8 2.7 %collective-permute-start.1 = (f32[16,512]{1,0:T(8,128)S(1)}, f32[16,512]{1,0:T(8,128)S(1)}, u32[]{:S(2)}, u32[]{:S(2)}) collective-permute-start(f32[16,512]{1,0:T(8,128)S(1)} %get-tuple-element.44.sent_ref), channel_id=1, source_target_pairs={{2,0},{3,1},{0,2},{1,3},{6,4},{7,5},{4,6},{5,7},{10,8},{11,9},{8,1... | collective-permute-start | bytes 98312 | tf_op jit(solution)/shard_map/ppermute | solution.py:746
  20.5 1.0 %own_half.2 = (f32[128,512]{1,0:T(8,128)S(1)}, bf16[2,768,512]{2,1,0:T(8,128)(2,1)S(1)}) custom-call(f32[144,512]{1,0:T(8,128)S(1)} %get-tuple-element.42.modes_ref, bf16[2,256,144]{2,1,0:T(8,128)(2,1)S(1)} %copy-done.3, bf16[2,128,256]{2,1,0:T(8,128)(2,1)S(1)} %copy-done.7, f32[256,128]{1,0:T(8,128)S(1)} %copy-done.6, f32[8,1,128]{2,1,0:T(1,128)S(1)} %copy-done.9), custom_call_target="tpu_custom_call" | custom-call | tf_op jit(solution)/shard_map/own_half/pallas_call | solution.py:732
  21.5 1.3 %collective-permute-done.1.arrived_ref = f32[16,512]{1,0:T(8,128)S(1)} collective-permute-done((f32[16,512]{1,0:T(8,128)S(1)}, f32[16,512]{1,0:T(8,128)S(1)}, u32[]{:S(2)}, u32[]{:S(2)}) %collective-permute-start.1) | collective-permute-done | bytes 32800 | tf_op jit(solution)/shard_map/ppermute | solution.py:746
  22.9 0.4 coupled_halves.2
  23.2 11.2 %all_to_all.21.spectral_ref = f32[16,13,4,128]{3,2,1,0:T(4,128)S(1)} all-to-all(f32[16,13,4,128]{3,2,1,0:T(4,128)S(1)} %coupled_halves.2), channel_id=1, replica_groups={{0,1,4,5,8,9,12,13,16,17,20,21,24,25,28,29},{2,3,6,7,10,11,14,15,18,19,..., dimensions={0} | all-to-all | bytes 851968 | tf_op jit(solution)/shard_map/all_to_all | solution.py:759
  34.4 0.5 smooth_field.2
  35.2 1.1 %x_links.1 = (f32[4,2,3,3,1,8,1024]{6,5,4,3,2,1,0:T(8,128)S(1)}, f32[18,8,1024]{2,1,0:T(8,128)S(1)}, f32[18,8,128]{2,1,0:T(8,128)S(1)}, f32[12,8,1024]{2,1,0:T(8,128)S(1)}, f32[8,8,1024]{2,1,0:T(8,128)S(1)}) custom-call(f32[4,2,3,3,1,8,1024]{6,5,4,3,2,1,0:T(8,128)S(1)} %copy-done, f32[8,8,1024]{2,1,0:T(8,128)S(1)} %get-tuple-element.47.smooth_ref, ...), custom_call_target="tpu_custom_call" | custom-call | tf_op jit(solution)/shard_map/x_links/pallas_call | solution.py:732
  36.6 0.5 time_links.1
  37.4 1.1 %yz_links.1 = (f32[4,2,3,3,1,8,1024]{6,5,4,3,2,1,0:T(8,128)S(1)}, f32[8,8,1024]{2,1,0:T(8,128)S(1)}, f32[2,8,1024]{2,1,0:T(8,128)S(1)}) custom-call(f32[4,2,3,3,1,8,1024]{6,5,4,3,2,1,0:T(8,128)S(1)} %get-tuple-element.53.rotated_ref, f32[4,2,3,3,1,8,1024]{6,5,4,3,2,1,0:T(8,128)S(1)} %copy-done, ...), custom_call_target="tpu_custom_call", output_to_operand_aliasing={{0}: (0, {})} | custom-call | tf_op jit(solution)/shard_map/yz_links/pallas_call | solution.py:732
  38.7 0.5 gradient_modes.3
  39.2 11.3 %all_to_all.22.spectral_ref = f32[16,13,4,128]{3,2,1,0:T(4,128)S(1)} all-to-all(f32[16,13,4,128]{3,2,1,0:T(4,128)S(1)} %bitcast.2), channel_id=1, replica_groups={{0,1,4,5,8,9,12,13,16,17,20,21,24,25,28,29},{2,3,6,7,10,11,14,15,18,19,..., dimensions={0} | all-to-all | bytes 851968 | tf_op jit(solution)/shard_map/all_to_all | solution.py:759
  50.8 2.9 %collective-permute-start.4 = (f32[16,512]{1,0:T(8,128)S(1)}, f32[16,512]{1,0:T(8,128)S(1)}, u32[]{:S(2)}, u32[]{:S(2)}) collective-permute-start(f32[16,512]{1,0:T(8,128)S(1)} %get-tuple-element.62.sent_ref), channel_id=1, source_target_pairs={{2,0},{3,1},{0,2},{1,3},{6,4},{7,5},{4,6},{5,7},{10,8},{11,9},{8,1... | collective-permute-start | bytes 98312 | tf_op jit(solution)/shard_map/ppermute | solution.py:746
  53.7 0.6 own_half.3.own_ref
  54.3 2.1 %collective-permute-done.4.arrived_ref = f32[16,512]{1,0:T(8,128)S(1)} collective-permute-done((f32[16,512]{1,0:T(8,128)S(1)}, f32[16,512]{1,0:T(8,128)S(1)}, u32[]{:S(2)}, u32[]{:S(2)}) %collective-permute-start.4) | collective-permute-done | bytes 32800 | tf_op jit(solution)/shard_map/ppermute | solution.py:746
  56.8 10.7 %all_to_all.23.spectral_ref = f32[16,13,4,128]{3,2,1,0:T(4,128)S(1)} all-to-all(f32[16,13,4,128]{3,2,1,0:T(4,128)S(1)} %coupled_halves.3), channel_id=1, replica_groups={{0,1,4,5,8,9,12,13,16,17,20,21,24,25,28,29},{2,3,6,7,10,11,14,15,18,19,..., dimensions={0} | all-to-all | bytes 851968 | tf_op jit(solution)/shard_map/all_to_all | solution.py:759
  67.4 0.5 smooth_field.3
  68.2 1.7 %last_space_links.1 = (f32[4,2,3,3,1,8,1024]{6,5,4,3,2,1,0:T(8,128)}, f32[2,2,3,3,1,8,1024]{6,5,4,3,2,1,0:T(8,128)S(1)}, f32[12,8,1024]{2,1,0:T(8,128)S(1)}) custom-call(f32[4,2,3,3,1,8,1024]{6,5,4,3,2,1,0:T(8,128)S(1)} %get-tuple-element.57.links_ref, f32[8,8,1024]{2,1,0:T(8,128)S(1)} %get-tuple-element.64.smooth_ref, ...), custom_call_target="tpu_custom_call" | custom-call | tf_op jit(solution)/shard_map/last_space_links/pallas_call | solution.py:732
  69.9 1.2 %last_time_links.1 = f32[4,2,3,3,1,8,1024]{6,5,4,3,2,1,0:T(8,128)} custom-call(f32[12,8,1024]{2,1,0:T(8,128)S(1)} %get-tuple-element.66.turned_ref, f32[8,8,1024]{2,1,0:T(8,128)S(1)} %get-tuple-element.67.part_ref, f32[8,8,1024]{2,1,0:T(8,128)S(1)} %collective-permute-done.5.arrived_ref, ...), custom_call_target="tpu_custom_call", output_to_operand_aliasing={{}: (4, {})} | custom-call | tf_op jit(solution)/shard_map/last_time_links/pallas_call | solution.py:732
  (29 shorter events, 2.4 us)
Async XLA Ops:
  0.0 1.8 %copy-start = (f32[4,2,3,3,1,8,1024]{6,5,4,3,2,1,0:T(8,128)S(1)}, f32[4,2,3,3,1,8,1024]{6,5,4,3,2,1,0:T(8,128)}, u32[]{:S(2)}) copy-start(f32[4,2,3,3,1,8,1024]{6,5,4,3,2,1,0:T(8,128)} %links_ref.5) | copy-start | bytes 7077892
  1.3 1.7 %collective-permute-start = (f32[8,8,1024]{2,1,0:T(8,128)S(1)}, f32[8,8,1024]{2,1,0:T(8,128)S(1)}, u32[]{:S(2)}, u32[]{:S(2)}) collective-permute-start(f32[8,8,1024]{2,1,0:T(8,128)S(1)} %get-tuple-element.39.time_ref), channel_id=1, source_target_pairs={{0,4},{4,0},{8,12},{12,8},{16,20},{20,16},{24,28},{28,24},{1,5},{5... | collective-permute-start | bytes 786440 | tf_op jit(solution)/shard_map/ppermute | solution.py:750
  2.3 15.1 %copy-start.2 = (f32[8,17,8,128]{3,2,1,0:T(8,128)S(1)}, f32[8,17,8,128]{3,2,1,0:T(8,128)}, u32[]{:S(2)}) copy-start(f32[8,17,8,128]{3,2,1,0:T(8,128)} %constant.24.clone.distance_ref) | copy-start | bytes 1671172
  2.3 15.1 %copy-start.5 = (bf16[2,144,144]{2,1,0:T(8,128)(2,1)S(1)}, bf16[2,144,144]{2,1,0:T(8,128)(2,1)}, u32[]{:S(2)}) copy-start(bf16[2,144,144]{2,1,0:T(8,128)(2,1)} %constant.18.clone.table_ref) | copy-start | bytes 248836
  2.3 15.1 %copy-start.8 = (f32[8,8,128]{2,1,0:T(8,128)S(1)}, f32[8,8,128]{2,1,0:T(8,128)}, u32[]{:S(2)}) copy-start(f32[8,8,128]{2,1,0:T(8,128)} %constant.25.clone.anchor_ref) | copy-start | bytes 98308
  3.0 17.5 %copy-start.3 = (bf16[2,256,144]{2,1,0:T(8,128)(2,1)S(1)}, bf16[2,256,144]{2,1,0:T(8,128)(2,1)}, u32[]{:S(2)}) copy-start(bf16[2,256,144]{2,1,0:T(8,128)(2,1)} %constant.19.clone.forward_ref) | copy-start | bytes 442372
  3.0 17.5 %copy-start.6 = (f32[256,128]{1,0:T(8,128)S(1)}, f32[256,128]{1,0:T(8,128)}, u32[]{:S(2)}) copy-start(f32[256,128]{1,0:T(8,128)} %constant.22.clone.line_ref) | copy-start | bytes 393220
  3.0 17.5 %copy-start.7 = (bf16[2,128,256]{2,1,0:T(8,128)(2,1)S(1)}, bf16[2,128,256]{2,1,0:T(8,128)(2,1)}, u32[]{:S(2)}) copy-start(bf16[2,128,256]{2,1,0:T(8,128)(2,1)} %constant.20.clone.inward_ref) | copy-start | bytes 393220
  3.0 17.5 %copy-start.9 = (f32[8,1,128]{2,1,0:T(1,128)S(1)}, f32[8,1,128]{2,1,0:T(1,128)}, u32[]{:S(2)}) copy-start(f32[8,1,128]{2,1,0:T(1,128)} %constant.26.clone.plane_ref) | copy-start | bytes 12292
  3.0 19.9 %copy-start.1 = (f32[8,17,8,128]{3,2,1,0:T(8,128)S(1)}, f32[8,17,8,128]{3,2,1,0:T(8,128)}, u32[]{:S(2)}) copy-start(f32[8,17,8,128]{3,2,1,0:T(8,128)} %constant.23.clone.response_ref) | copy-start | bytes 1671172
  3.0 19.9 %copy-start.4 = (bf16[2,144,144]{2,1,0:T(8,128)(2,1)S(1)}, bf16[2,144,144]{2,1,0:T(8,128)(2,1)}, u32[]{:S(2)}) copy-start(bf16[2,144,144]{2,1,0:T(8,128)(2,1)} %constant.21.clone.table_ref) | copy-start | bytes 248836
  17.8 5.0 %collective-permute-start.1 = (f32[16,512]{1,0:T(8,128)S(1)}, f32[16,512]{1,0:T(8,128)S(1)}, u32[]{:S(2)}, u32[]{:S(2)}) collective-permute-start(f32[16,512]{1,0:T(8,128)S(1)} %get-tuple-element.44.sent_ref), channel_id=1, source_target_pairs={{2,0},{3,1},{0,2},{1,3},{6,4},{7,5},{4,6},{5,7},{10,8},{11,9},{8,1... | collective-permute-start | bytes 98312 | tf_op jit(solution)/shard_map/ppermute | solution.py:746
  35.0 1.6 %collective-permute-start.2 = (f32[8,8,1024]{2,1,0:T(8,128)S(1)}, f32[8,8,1024]{2,1,0:T(8,128)S(1)}, u32[]{:S(2)}, u32[]{:S(2)}) collective-permute-start(f32[8,8,1024]{2,1,0:T(8,128)S(1)} %get-tuple-element.52), channel_id=1, source_target_pairs={{0,4},{4,0},{8,12},{12,8},{16,20},{20,16},{24,28},{28,24},{1,5},{5... | collective-permute-start | bytes 786440 | tf_op jit(solution)/shard_map/ppermute | solution.py:750
  37.1 1.6 %collective-permute-start.3 = (f32[8,8,1024]{2,1,0:T(8,128)S(1)}, f32[8,8,1024]{2,1,0:T(8,128)S(1)}, u32[]{:S(2)}, u32[]{:S(2)}) collective-permute-start(f32[8,8,1024]{2,1,0:T(8,128)S(1)} %get-tuple-element.59.time_ref), channel_id=1, source_target_pairs={{0,4},{4,0},{8,12},{12,8},{16,20},{20,16},{24,28},{28,24},{1,5},{5... | collective-permute-start | bytes 786440 | tf_op jit(solution)/shard_map/ppermute | solution.py:750
  50.8 5.6 %collective-permute-start.4 = (f32[16,512]{1,0:T(8,128)S(1)}, f32[16,512]{1,0:T(8,128)S(1)}, u32[]{:S(2)}, u32[]{:S(2)}) collective-permute-start(f32[16,512]{1,0:T(8,128)S(1)} %get-tuple-element.62.sent_ref), channel_id=1, source_target_pairs={{2,0},{3,1},{0,2},{1,3},{6,4},{7,5},{4,6},{5,7},{10,8},{11,9},{8,1... | collective-permute-start | bytes 98312 | tf_op jit(solution)/shard_map/ppermute | solution.py:746
  67.9 1.9 %collective-permute-start.5 = (f32[8,8,1024]{2,1,0:T(8,128)S(1)}, f32[8,8,1024]{2,1,0:T(8,128)S(1)}, u32[]{:S(2)}, u32[]{:S(2)}) collective-permute-start(f32[8,8,1024]{2,1,0:T(8,128)S(1)} %get-tuple-element.68), channel_id=1, source_target_pairs={{0,4},{4,0},{8,12},{12,8},{16,20},{20,16},{24,28},{28,24},{1,5},{5... | collective-permute-start | bytes 786440 | tf_op jit(solution)/shard_map/ppermute | solution.py:750

commit v7 on v6

--- a/solution.py
+++ b/solution.py
@@ -656,7 +656,7 @@
 
 
 def last_space_links_kernel(
-    links_ref, smooth_ref, after_ref, out_hbm, yz_ref, turned_ref, x_ref, gauge_ref, beyond_ref, sent
+    links_ref, smooth_ref, after_ref, out_hbm, z_ref, turned_ref, xy_ref, gauge_ref, beyond_ref, sent
 ):
     chunks = links_ref.shape[-1] // LANES
     gauge_after(after_ref, beyond_ref)
@@ -664,27 +664,35 @@
     def along_x(step, carry):
         at = chunk_at(step)
         own = gauge_here(smooth_ref, gauge_ref, at)
-        store_link(x_ref, 0, at, rotate_x(links_ref, at, own))
+        store_link(xy_ref, 0, at, rotate_x(links_ref, at, own))
         return carry
 
-    def along_yz(step, carry):
+    def along_y(step, carry):
         at = chunk_at(step)
         at_next = chunk_at(lax.rem(step + 1, chunks))
         own = [gauge_ref[n, :, at] for n in range(18)]
-        store_link(yz_ref, 0, at, rotate_y(links_ref, at, own, gauge_ref, at_next))
-        store_link(yz_ref, 1, at, rotate_z(links_ref, at, own, beyond_ref, step))
+        store_link(xy_ref, 1, at, rotate_y(links_ref, at, own, gauge_ref, at_next))
+        return carry
+
+    def along_z(step, carry):
+        at = chunk_at(step)
+        own = [gauge_ref[n, :, at] for n in range(18)]
+        store_link(z_ref, 0, at, rotate_z(links_ref, at, own, beyond_ref, step))
         turn_time(links_ref, at, own, turned_ref)
         return carry
 
+    copies = [pltpu.make_async_copy(xy_ref.at[mu], out_hbm.at[mu], sent.at[mu]) for mu in range(2)]
     lax.fori_loop(0, chunks, along_x, 0, unroll=4)
-    copy = pltpu.make_async_copy(x_ref, out_hbm.at[0:1], sent)
-    copy.start()
-    lax.fori_loop(0, chunks, along_yz, 0, unroll=4)
-    copy.wait()
-
-
-def last_time_links_kernel(turned_ref, part_ref, arrived_ref, yz_ref, x_hbm, out_hbm, time_ref, sent):
-    copies = [pltpu.make_async_copy(yz_ref, out_hbm.at[1:3], sent.at[0])]
+    copies[0].start()
+    lax.fori_loop(0, chunks, along_y, 0, unroll=4)
+    copies[1].start()
+    lax.fori_loop(0, chunks, along_z, 0, unroll=4)
+    for copy in copies:
+        copy.wait()
+
+
+def last_time_links_kernel(turned_ref, part_ref, arrived_ref, z_ref, xy_hbm, out_hbm, time_ref, sent):
+    copies = [pltpu.make_async_copy(z_ref, out_hbm.at[2:3], sent.at[0])]
     copies[0].start()
     sites = arrived_ref.shape[-1]
     chunks = sites // LANES
@@ -892,18 +900,18 @@
                 send_kernel, "gradient_modes", [space, time, arrived, edge, forward], in_vmem(), sent_shape
             )
         else:
-            rotated, yz_links, turned = call(
+            rotated, z_links, turned = call(
                 last_space_links_kernel,
                 "last_space_links",
                 [links, smooth, after],
                 [in_hbm(), in_vmem(), in_vmem()],
-                [pltpu.HBM(local, jnp.float32), shaped(2, *local[1:]), shaped(12, 8, sites)],
-                [scratch(1, *local[1:])] + gauge_scratch + [pltpu.SemaphoreType.DMA],
+                [pltpu.HBM(local, jnp.float32), shaped(1, *local[1:]), shaped(12, 8, sites)],
+                [scratch(2, *local[1:])] + gauge_scratch + [pltpu.SemaphoreType.DMA((2,))],
             )
             rotated = call(
                 last_time_links_kernel,
                 "last_time_links",
-                [turned, part, arrived, yz_links, rotated],
+                [turned, part, arrived, z_links, rotated],
                 in_hbm(),
                 pltpu.HBM(local, jnp.float32),
                 [scratch(1, *local[1:]), pltpu.SemaphoreType.DMA((3,))],

time: 71.4 us -> 71.8 us (level)
  transfers between devices with their start and end apart: 6 -> 6, of which waited for: 5 -> 5; matrix products, arithmetic and copies ran while one was open for 0% -> 0% of each run, Pallas kernels for 8% -> 9%
where the time goes in v7:
time: 71.8 us; the launch traced here: 71.5 us
  blocking collectives  47.1 us (66%)
  Pallas kernels  12.8 us (18%)
  starting transfers between devices  6.87 us (10%)
  waiting for transfers between devices  4.48 us (6%)
    all_to_all x4, blocking collectives, exchanged(): lax.all_to_all(block, ('ta', 'gz'), split_axis=0, concat_axis=0, axis_ind...  47.1 us
    pallas_call x17, Pallas kernels, call(): pl.pallas_call(kernel, in_specs=in_specs, out_specs=out_specs, out_shape=...  12.8 us
    ppermute x2, starting transfers between devices, passed(): lax.ppermute(block, axis, [((i - distance) % size, i) for i in range(size)])  5.55 us
    ppermute x2, waiting for transfers between devices, passed(): lax.ppermute(block, axis, [((i - distance) % size, i) for i in range(size)])  3.4 us
  transfers between devices with their start and end apart: 6, of which 5 were waited for; matrix products, arithmetic and copies ran while one was open for 0% of the time, Pallas kernels for 9%

profile of v7, /device:TPU:0, one launch (start us, length us, event | category | flops | bytes accessed | tf_op | source)
XLA Modules:
  0.0 71.5 jit_solution(9248260542900508140)
XLA Ops:
  0.0 1.3 %time_gradient.1 = (bf16[2,768,512]{2,1,0:T(8,128)(2,1)S(1)}, f32[8,8,1024]{2,1,0:T(8,128)S(1)}) custom-call(f32[4,2,3,3,1,8,1024]{6,5,4,3,2,1,0:T(8,128)} %links_ref.5), custom_call_target="tpu_custom_call" | custom-call | tf_op jit(solution)/shard_map/time_gradient/pallas_call | solution.py:740
  1.3 0.5 collective-permute-start
  1.8 0.5 space_gradient.1
  2.4 0.6 collective-permute-done.arrived_ref
  3.0 0.5 gradient_modes.2
  3.5 13.9 %all_to_all.20.spectral_ref = f32[16,13,4,128]{3,2,1,0:T(4,128)S(1)} all-to-all(f32[16,13,4,128]{3,2,1,0:T(4,128)S(1)} %bitcast.3), channel_id=1, replica_groups={{0,1,4,5,8,9,12,13,16,17,20,21,24,25,28,29},{2,3,6,7,10,11,14,15,18,19,..., dimensions={0} | all-to-all | bytes 851968 | tf_op jit(solution)/shard_map/all_to_all | solution.py:767
  17.8 2.7 %collective-permute-start.1 = (f32[16,512]{1,0:T(8,128)S(1)}, f32[16,512]{1,0:T(8,128)S(1)}, u32[]{:S(2)}, u32[]{:S(2)}) collective-permute-start(f32[16,512]{1,0:T(8,128)S(1)} %get-tuple-element.44.sent_ref), channel_id=1, source_target_pairs={{2,0},{3,1},{0,2},{1,3},{6,4},{7,5},{4,6},{5,7},{10,8},{11,9},{8,1... | collective-permute-start | bytes 98312 | tf_op jit(solution)/shard_map/ppermute | solution.py:754
  20.5 1.0 %own_half.2 = (f32[128,512]{1,0:T(8,128)S(1)}, bf16[2,768,512]{2,1,0:T(8,128)(2,1)S(1)}) custom-call(f32[144,512]{1,0:T(8,128)S(1)} %get-tuple-element.42.modes_ref, bf16[2,256,144]{2,1,0:T(8,128)(2,1)S(1)} %copy-done.3, bf16[2,128,256]{2,1,0:T(8,128)(2,1)S(1)} %copy-done.7, f32[256,128]{1,0:T(8,128)S(1)} %copy-done.6, f32[8,1,128]{2,1,0:T(1,128)S(1)} %copy-done.9), custom_call_target="tpu_custom_call" | custom-call | tf_op jit(solution)/shard_map/own_half/pallas_call | solution.py:740
  21.5 1.3 %collective-permute-done.1.arrived_ref = f32[16,512]{1,0:T(8,128)S(1)} collective-permute-done((f32[16,512]{1,0:T(8,128)S(1)}, f32[16,512]{1,0:T(8,128)S(1)}, u32[]{:S(2)}, u32[]{:S(2)}) %collective-permute-start.1) | collective-permute-done | bytes 32800 | tf_op jit(solution)/shard_map/ppermute | solution.py:754
  22.9 0.4 coupled_halves.2
  23.2 11.2 %all_to_all.21.spectral_ref = f32[16,13,4,128]{3,2,1,0:T(4,128)S(1)} all-to-all(f32[16,13,4,128]{3,2,1,0:T(4,128)S(1)} %coupled_halves.2), channel_id=1, replica_groups={{0,1,4,5,8,9,12,13,16,17,20,21,24,25,28,29},{2,3,6,7,10,11,14,15,18,19,..., dimensions={0} | all-to-all | bytes 851968 | tf_op jit(solution)/shard_map/all_to_all | solution.py:767
  34.4 0.5 smooth_field.2
  35.2 1.1 %x_links.1 = (f32[4,2,3,3,1,8,1024]{6,5,4,3,2,1,0:T(8,128)S(1)}, f32[18,8,1024]{2,1,0:T(8,128)S(1)}, f32[18,8,128]{2,1,0:T(8,128)S(1)}, f32[12,8,1024]{2,1,0:T(8,128)S(1)}, f32[8,8,1024]{2,1,0:T(8,128)S(1)}) custom-call(f32[4,2,3,3,1,8,1024]{6,5,4,3,2,1,0:T(8,128)S(1)} %copy-done, f32[8,8,1024]{2,1,0:T(8,128)S(1)} %get-tuple-element.47.smooth_ref, ...), custom_call_target="tpu_custom_call" | custom-call | tf_op jit(solution)/shard_map/x_links/pallas_call | solution.py:740
  36.6 0.5 time_links.1
  37.4 1.1 %yz_links.1 = (f32[4,2,3,3,1,8,1024]{6,5,4,3,2,1,0:T(8,128)S(1)}, f32[8,8,1024]{2,1,0:T(8,128)S(1)}, f32[2,8,1024]{2,1,0:T(8,128)S(1)}) custom-call(f32[4,2,3,3,1,8,1024]{6,5,4,3,2,1,0:T(8,128)S(1)} %get-tuple-element.53.rotated_ref, f32[4,2,3,3,1,8,1024]{6,5,4,3,2,1,0:T(8,128)S(1)} %copy-done, ...), custom_call_target="tpu_custom_call", output_to_operand_aliasing={{0}: (0, {})} | custom-call | tf_op jit(solution)/shard_map/yz_links/pallas_call | solution.py:740
  38.7 0.5 gradient_modes.3
  39.2 11.3 %all_to_all.22.spectral_ref = f32[16,13,4,128]{3,2,1,0:T(4,128)S(1)} all-to-all(f32[16,13,4,128]{3,2,1,0:T(4,128)S(1)} %bitcast.2), channel_id=1, replica_groups={{0,1,4,5,8,9,12,13,16,17,20,21,24,25,28,29},{2,3,6,7,10,11,14,15,18,19,..., dimensions={0} | all-to-all | bytes 851968 | tf_op jit(solution)/shard_map/all_to_all | solution.py:767
  50.8 2.9 %collective-permute-start.4 = (f32[16,512]{1,0:T(8,128)S(1)}, f32[16,512]{1,0:T(8,128)S(1)}, u32[]{:S(2)}, u32[]{:S(2)}) collective-permute-start(f32[16,512]{1,0:T(8,128)S(1)} %get-tuple-element.62.sent_ref), channel_id=1, source_target_pairs={{2,0},{3,1},{0,2},{1,3},{6,4},{7,5},{4,6},{5,7},{10,8},{11,9},{8,1... | collective-permute-start | bytes 98312 | tf_op jit(solution)/shard_map/ppermute | solution.py:754
  53.7 0.6 own_half.3.own_ref
  54.3 2.1 %collective-permute-done.4.arrived_ref = f32[16,512]{1,0:T(8,128)S(1)} collective-permute-done((f32[16,512]{1,0:T(8,128)S(1)}, f32[16,512]{1,0:T(8,128)S(1)}, u32[]{:S(2)}, u32[]{:S(2)}) %collective-permute-start.4) | collective-permute-done | bytes 32800 | tf_op jit(solution)/shard_map/ppermute | solution.py:754
  56.8 10.7 %all_to_all.23.spectral_ref = f32[16,13,4,128]{3,2,1,0:T(4,128)S(1)} all-to-all(f32[16,13,4,128]{3,2,1,0:T(4,128)S(1)} %coupled_halves.3), channel_id=1, replica_groups={{0,1,4,5,8,9,12,13,16,17,20,21,24,25,28,29},{2,3,6,7,10,11,14,15,18,19,..., dimensions={0} | all-to-all | bytes 851968 | tf_op jit(solution)/shard_map/all_to_all | solution.py:767
  67.4 0.5 smooth_field.3
  68.2 2.0 %last_space_links.1 = (f32[4,2,3,3,1,8,1024]{6,5,4,3,2,1,0:T(8,128)}, f32[1,2,3,3,1,8,1024]{6,5,4,3,2,1,0:T(8,128)S(1)}, f32[12,8,1024]{2,1,0:T(8,128)S(1)}) custom-call(f32[4,2,3,3,1,8,1024]{6,5,4,3,2,1,0:T(8,128)S(1)} %get-tuple-element.57.links_ref, f32[8,8,1024]{2,1,0:T(8,128)S(1)} %get-tuple-element.64.smooth_ref, ...), custom_call_target="tpu_custom_call" | custom-call | tf_op jit(solution)/shard_map/last_space_links/pallas_call | solution.py:740
  70.3 1.2 %last_time_links.1 = f32[4,2,3,3,1,8,1024]{6,5,4,3,2,1,0:T(8,128)} custom-call(f32[12,8,1024]{2,1,0:T(8,128)S(1)} %get-tuple-element.66.turned_ref, f32[8,8,1024]{2,1,0:T(8,128)S(1)} %get-tuple-element.67.part_ref, f32[8,8,1024]{2,1,0:T(8,128)S(1)} %collective-permute-done.5.arrived_ref, ...), custom_call_target="tpu_custom_call", output_to_operand_aliasing={{}: (4, {})} | custom-call | tf_op jit(solution)/shard_map/last_time_links/pallas_call | solution.py:740
  (29 shorter events, 2.4 us)
Async XLA Ops:
  0.0 1.8 %copy-start = (f32[4,2,3,3,1,8,1024]{6,5,4,3,2,1,0:T(8,128)S(1)}, f32[4,2,3,3,1,8,1024]{6,5,4,3,2,1,0:T(8,128)}, u32[]{:S(2)}) copy-start(f32[4,2,3,3,1,8,1024]{6,5,4,3,2,1,0:T(8,128)} %links_ref.5) | copy-start | bytes 7077892
  1.3 1.7 %collective-permute-start = (f32[8,8,1024]{2,1,0:T(8,128)S(1)}, f32[8,8,1024]{2,1,0:T(8,128)S(1)}, u32[]{:S(2)}, u32[]{:S(2)}) collective-permute-start(f32[8,8,1024]{2,1,0:T(8,128)S(1)} %get-tuple-element.39.time_ref), channel_id=1, source_target_pairs={{0,4},{4,0},{8,12},{12,8},{16,20},{20,16},{24,28},{28,24},{1,5},{5... | collective-permute-start | bytes 786440 | tf_op jit(solution)/shard_map/ppermute | solution.py:758
  2.3 15.1 %copy-start.2 = (f32[8,17,8,128]{3,2,1,0:T(8,128)S(1)}, f32[8,17,8,128]{3,2,1,0:T(8,128)}, u32[]{:S(2)}) copy-start(f32[8,17,8,128]{3,2,1,0:T(8,128)} %constant.24.clone.distance_ref) | copy-start | bytes 1671172
  2.3 15.1 %copy-start.5 = (bf16[2,144,144]{2,1,0:T(8,128)(2,1)S(1)}, bf16[2,144,144]{2,1,0:T(8,128)(2,1)}, u32[]{:S(2)}) copy-start(bf16[2,144,144]{2,1,0:T(8,128)(2,1)} %constant.18.clone.table_ref) | copy-start | bytes 248836
  2.3 15.1 %copy-start.8 = (f32[8,8,128]{2,1,0:T(8,128)S(1)}, f32[8,8,128]{2,1,0:T(8,128)}, u32[]{:S(2)}) copy-start(f32[8,8,128]{2,1,0:T(8,128)} %constant.25.clone.anchor_ref) | copy-start | bytes 98308
  3.0 17.5 %copy-start.3 = (bf16[2,256,144]{2,1,0:T(8,128)(2,1)S(1)}, bf16[2,256,144]{2,1,0:T(8,128)(2,1)}, u32[]{:S(2)}) copy-start(bf16[2,256,144]{2,1,0:T(8,128)(2,1)} %constant.19.clone.forward_ref) | copy-start | bytes 442372
  3.0 17.5 %copy-start.6 = (f32[256,128]{1,0:T(8,128)S(1)}, f32[256,128]{1,0:T(8,128)}, u32[]{:S(2)}) copy-start(f32[256,128]{1,0:T(8,128)} %constant.22.clone.line_ref) | copy-start | bytes 393220
  3.0 17.5 %copy-start.7 = (bf16[2,128,256]{2,1,0:T(8,128)(2,1)S(1)}, bf16[2,128,256]{2,1,0:T(8,128)(2,1)}, u32[]{:S(2)}) copy-start(bf16[2,128,256]{2,1,0:T(8,128)(2,1)} %constant.20.clone.inward_ref) | copy-start | bytes 393220
  3.0 17.5 %copy-start.9 = (f32[8,1,128]{2,1,0:T(1,128)S(1)}, f32[8,1,128]{2,1,0:T(1,128)}, u32[]{:S(2)}) copy-start(f32[8,1,128]{2,1,0:T(1,128)} %constant.26.clone.plane_ref) | copy-start | bytes 12292
  3.0 19.9 %copy-start.1 = (f32[8,17,8,128]{3,2,1,0:T(8,128)S(1)}, f32[8,17,8,128]{3,2,1,0:T(8,128)}, u32[]{:S(2)}) copy-start(f32[8,17,8,128]{3,2,1,0:T(8,128)} %constant.23.clone.response_ref) | copy-start | bytes 1671172
  3.0 19.9 %copy-start.4 = (bf16[2,144,144]{2,1,0:T(8,128)(2,1)S(1)}, bf16[2,144,144]{2,1,0:T(8,128)(2,1)}, u32[]{:S(2)}) copy-start(bf16[2,144,144]{2,1,0:T(8,128)(2,1)} %constant.21.clone.table_ref) | copy-start | bytes 248836
  17.8 5.0 %collective-permute-start.1 = (f32[16,512]{1,0:T(8,128)S(1)}, f32[16,512]{1,0:T(8,128)S(1)}, u32[]{:S(2)}, u32[]{:S(2)}) collective-permute-start(f32[16,512]{1,0:T(8,128)S(1)} %get-tuple-element.44.sent_ref), channel_id=1, source_target_pairs={{2,0},{3,1},{0,2},{1,3},{6,4},{7,5},{4,6},{5,7},{10,8},{11,9},{8,1... | collective-permute-start | bytes 98312 | tf_op jit(solution)/shard_map/ppermute | solution.py:754
  35.0 1.6 %collective-permute-start.2 = (f32[8,8,1024]{2,1,0:T(8,128)S(1)}, f32[8,8,1024]{2,1,0:T(8,128)S(1)}, u32[]{:S(2)}, u32[]{:S(2)}) collective-permute-start(f32[8,8,1024]{2,1,0:T(8,128)S(1)} %get-tuple-element.52), channel_id=1, source_target_pairs={{0,4},{4,0},{8,12},{12,8},{16,20},{20,16},{24,28},{28,24},{1,5},{5... | collective-permute-start | bytes 786440 | tf_op jit(solution)/shard_map/ppermute | solution.py:758
  37.1 1.6 %collective-permute-start.3 = (f32[8,8,1024]{2,1,0:T(8,128)S(1)}, f32[8,8,1024]{2,1,0:T(8,128)S(1)}, u32[]{:S(2)}, u32[]{:S(2)}) collective-permute-start(f32[8,8,1024]{2,1,0:T(8,128)S(1)} %get-tuple-element.59.time_ref), channel_id=1, source_target_pairs={{0,4},{4,0},{8,12},{12,8},{16,20},{20,16},{24,28},{28,24},{1,5},{5... | collective-permute-start | bytes 786440 | tf_op jit(solution)/shard_map/ppermute | solution.py:758
  50.8 5.6 %collective-permute-start.4 = (f32[16,512]{1,0:T(8,128)S(1)}, f32[16,512]{1,0:T(8,128)S(1)}, u32[]{:S(2)}, u32[]{:S(2)}) collective-permute-start(f32[16,512]{1,0:T(8,128)S(1)} %get-tuple-element.62.sent_ref), channel_id=1, source_target_pairs={{2,0},{3,1},{0,2},{1,3},{6,4},{7,5},{4,6},{5,7},{10,8},{11,9},{8,1... | collective-permute-start | bytes 98312 | tf_op jit(solution)/shard_map/ppermute | solution.py:754
  67.9 2.3 %collective-permute-start.5 = (f32[8,8,1024]{2,1,0:T(8,128)S(1)}, f32[8,8,1024]{2,1,0:T(8,128)S(1)}, u32[]{:S(2)}, u32[]{:S(2)}) collective-permute-start(f32[8,8,1024]{2,1,0:T(8,128)S(1)} %get-tuple-element.68), channel_id=1, source_target_pairs={{0,4},{4,0},{8,12},{12,8},{16,20},{20,16},{24,28},{28,24},{1,5},{5... | collective-permute-start | bytes 786440 | tf_op jit(solution)/shard_map/ppermute | solution.py:758

commit v8 on v6

--- a/solution.py
+++ b/solution.py
@@ -676,10 +676,10 @@
         turn_time(links_ref, at, own, turned_ref)
         return carry
 
-    lax.fori_loop(0, chunks, along_x, 0, unroll=4)
+    lax.fori_loop(0, chunks, along_x, 0, unroll=2)
     copy = pltpu.make_async_copy(x_ref, out_hbm.at[0:1], sent)
     copy.start()
-    lax.fori_loop(0, chunks, along_yz, 0, unroll=4)
+    lax.fori_loop(0, chunks, along_yz, 0, unroll=2)
     copy.wait()
 
 

time: 71.4 us -> 71.5 us (level)
  transfers between devices with their start and end apart: 6 -> 6, of which waited for: 5 -> 5; matrix products, arithmetic and copies ran while one was open for 0% -> 0% of each run, Pallas kernels for 8% -> 9%
where the time goes in v8:
time: 71.5 us; the launch traced here: 71.3 us
  blocking collectives  47.1 us (66%)
  Pallas kernels  12.6 us (18%)
  starting transfers between devices  6.87 us (10%)
  waiting for transfers between devices  4.48 us (6%)
    all_to_all x4, blocking collectives, exchanged(): lax.all_to_all(block, ('ta', 'gz'), split_axis=0, concat_axis=0, axis_ind...  47.1 us
    pallas_call x17, Pallas kernels, call(): pl.pallas_call(kernel, in_specs=in_specs, out_specs=out_specs, out_shape=...  12.6 us
    ppermute x2, starting transfers between devices, passed(): lax.ppermute(block, axis, [((i - distance) % size, i) for i in range(size)])  5.55 us
    ppermute x2, waiting for transfers between devices, passed(): lax.ppermute(block, axis, [((i - distance) % size, i) for i in range(size)])  3.4 us
  transfers between devices with their start and end apart: 6, of which 5 were waited for; matrix products, arithmetic and copies ran while one was open for 0% of the time, Pallas kernels for 9%

profile of v8, /device:TPU:0, one launch (start us, length us, event | category | flops | bytes accessed | tf_op | source)
XLA Modules:
  0.0 71.3 jit_solution(5755541095102570602)
XLA Ops:
  0.0 1.3 %time_gradient.1 = (bf16[2,768,512]{2,1,0:T(8,128)(2,1)S(1)}, f32[8,8,1024]{2,1,0:T(8,128)S(1)}) custom-call(f32[4,2,3,3,1,8,1024]{6,5,4,3,2,1,0:T(8,128)} %links_ref.5), custom_call_target="tpu_custom_call" | custom-call | tf_op jit(solution)/shard_map/time_gradient/pallas_call | solution.py:732
  1.3 0.5 collective-permute-start
  1.8 0.5 space_gradient.1
  2.4 0.6 collective-permute-done.arrived_ref
  3.0 0.5 gradient_modes.2
  3.5 13.9 %all_to_all.20.spectral_ref = f32[16,13,4,128]{3,2,1,0:T(4,128)S(1)} all-to-all(f32[16,13,4,128]{3,2,1,0:T(4,128)S(1)} %bitcast.3), channel_id=1, replica_groups={{0,1,4,5,8,9,12,13,16,17,20,21,24,25,28,29},{2,3,6,7,10,11,14,15,18,19,..., dimensions={0} | all-to-all | bytes 851968 | tf_op jit(solution)/shard_map/all_to_all | solution.py:759
  17.8 2.7 %collective-permute-start.1 = (f32[16,512]{1,0:T(8,128)S(1)}, f32[16,512]{1,0:T(8,128)S(1)}, u32[]{:S(2)}, u32[]{:S(2)}) collective-permute-start(f32[16,512]{1,0:T(8,128)S(1)} %get-tuple-element.44.sent_ref), channel_id=1, source_target_pairs={{2,0},{3,1},{0,2},{1,3},{6,4},{7,5},{4,6},{5,7},{10,8},{11,9},{8,1... | collective-permute-start | bytes 98312 | tf_op jit(solution)/shard_map/ppermute | solution.py:746
  20.5 1.0 %own_half.2 = (f32[128,512]{1,0:T(8,128)S(1)}, bf16[2,768,512]{2,1,0:T(8,128)(2,1)S(1)}) custom-call(f32[144,512]{1,0:T(8,128)S(1)} %get-tuple-element.42.modes_ref, bf16[2,256,144]{2,1,0:T(8,128)(2,1)S(1)} %copy-done.3, bf16[2,128,256]{2,1,0:T(8,128)(2,1)S(1)} %copy-done.7, f32[256,128]{1,0:T(8,128)S(1)} %copy-done.6, f32[8,1,128]{2,1,0:T(1,128)S(1)} %copy-done.9), custom_call_target="tpu_custom_call" | custom-call | tf_op jit(solution)/shard_map/own_half/pallas_call | solution.py:732
  21.5 1.3 %collective-permute-done.1.arrived_ref = f32[16,512]{1,0:T(8,128)S(1)} collective-permute-done((f32[16,512]{1,0:T(8,128)S(1)}, f32[16,512]{1,0:T(8,128)S(1)}, u32[]{:S(2)}, u32[]{:S(2)}) %collective-permute-start.1) | collective-permute-done | bytes 32800 | tf_op jit(solution)/shard_map/ppermute | solution.py:746
  22.9 0.4 coupled_halves.2
  23.2 11.2 %all_to_all.21.spectral_ref = f32[16,13,4,128]{3,2,1,0:T(4,128)S(1)} all-to-all(f32[16,13,4,128]{3,2,1,0:T(4,128)S(1)} %coupled_halves.2), channel_id=1, replica_groups={{0,1,4,5,8,9,12,13,16,17,20,21,24,25,28,29},{2,3,6,7,10,11,14,15,18,19,..., dimensions={0} | all-to-all | bytes 851968 | tf_op jit(solution)/shard_map/all_to_all | solution.py:759
  34.4 0.5 smooth_field.2
  35.2 1.1 %x_links.1 = (f32[4,2,3,3,1,8,1024]{6,5,4,3,2,1,0:T(8,128)S(1)}, f32[18,8,1024]{2,1,0:T(8,128)S(1)}, f32[18,8,128]{2,1,0:T(8,128)S(1)}, f32[12,8,1024]{2,1,0:T(8,128)S(1)}, f32[8,8,1024]{2,1,0:T(8,128)S(1)}) custom-call(f32[4,2,3,3,1,8,1024]{6,5,4,3,2,1,0:T(8,128)S(1)} %copy-done, f32[8,8,1024]{2,1,0:T(8,128)S(1)} %get-tuple-element.47.smooth_ref, ...), custom_call_target="tpu_custom_call" | custom-call | tf_op jit(solution)/shard_map/x_links/pallas_call | solution.py:732
  36.6 0.5 time_links.1
  37.4 1.1 %yz_links.1 = (f32[4,2,3,3,1,8,1024]{6,5,4,3,2,1,0:T(8,128)S(1)}, f32[8,8,1024]{2,1,0:T(8,128)S(1)}, f32[2,8,1024]{2,1,0:T(8,128)S(1)}) custom-call(f32[4,2,3,3,1,8,1024]{6,5,4,3,2,1,0:T(8,128)S(1)} %get-tuple-element.53.rotated_ref, f32[4,2,3,3,1,8,1024]{6,5,4,3,2,1,0:T(8,128)S(1)} %copy-done, ...), custom_call_target="tpu_custom_call", output_to_operand_aliasing={{0}: (0, {})} | custom-call | tf_op jit(solution)/shard_map/yz_links/pallas_call | solution.py:732
  38.7 0.5 gradient_modes.3
  39.2 11.3 %all_to_all.22.spectral_ref = f32[16,13,4,128]{3,2,1,0:T(4,128)S(1)} all-to-all(f32[16,13,4,128]{3,2,1,0:T(4,128)S(1)} %bitcast.2), channel_id=1, replica_groups={{0,1,4,5,8,9,12,13,16,17,20,21,24,25,28,29},{2,3,6,7,10,11,14,15,18,19,..., dimensions={0} | all-to-all | bytes 851968 | tf_op jit(solution)/shard_map/all_to_all | solution.py:759
  50.8 2.9 %collective-permute-start.4 = (f32[16,512]{1,0:T(8,128)S(1)}, f32[16,512]{1,0:T(8,128)S(1)}, u32[]{:S(2)}, u32[]{:S(2)}) collective-permute-start(f32[16,512]{1,0:T(8,128)S(1)} %get-tuple-element.62.sent_ref), channel_id=1, source_target_pairs={{2,0},{3,1},{0,2},{1,3},{6,4},{7,5},{4,6},{5,7},{10,8},{11,9},{8,1... | collective-permute-start | bytes 98312 | tf_op jit(solution)/shard_map/ppermute | solution.py:746
  53.7 0.6 own_half.3.own_ref
  54.3 2.1 %collective-permute-done.4.arrived_ref = f32[16,512]{1,0:T(8,128)S(1)} collective-permute-done((f32[16,512]{1,0:T(8,128)S(1)}, f32[16,512]{1,0:T(8,128)S(1)}, u32[]{:S(2)}, u32[]{:S(2)}) %collective-permute-start.4) | collective-permute-done | bytes 32800 | tf_op jit(solution)/shard_map/ppermute | solution.py:746
  56.8 10.7 %all_to_all.23.spectral_ref = f32[16,13,4,128]{3,2,1,0:T(4,128)S(1)} all-to-all(f32[16,13,4,128]{3,2,1,0:T(4,128)S(1)} %coupled_halves.3), channel_id=1, replica_groups={{0,1,4,5,8,9,12,13,16,17,20,21,24,25,28,29},{2,3,6,7,10,11,14,15,18,19,..., dimensions={0} | all-to-all | bytes 851968 | tf_op jit(solution)/shard_map/all_to_all | solution.py:759
  67.4 0.5 smooth_field.3
  68.2 1.8 %last_space_links.1 = (f32[4,2,3,3,1,8,1024]{6,5,4,3,2,1,0:T(8,128)}, f32[2,2,3,3,1,8,1024]{6,5,4,3,2,1,0:T(8,128)S(1)}, f32[12,8,1024]{2,1,0:T(8,128)S(1)}) custom-call(f32[4,2,3,3,1,8,1024]{6,5,4,3,2,1,0:T(8,128)S(1)} %get-tuple-element.57.links_ref, f32[8,8,1024]{2,1,0:T(8,128)S(1)} %get-tuple-element.64.smooth_ref, ...), custom_call_target="tpu_custom_call" | custom-call | tf_op jit(solution)/shard_map/last_space_links/pallas_call | solution.py:732
  70.0 1.2 %last_time_links.1 = f32[4,2,3,3,1,8,1024]{6,5,4,3,2,1,0:T(8,128)} custom-call(f32[12,8,1024]{2,1,0:T(8,128)S(1)} %get-tuple-element.66.turned_ref, f32[8,8,1024]{2,1,0:T(8,128)S(1)} %get-tuple-element.67.part_ref, f32[8,8,1024]{2,1,0:T(8,128)S(1)} %collective-permute-done.5.arrived_ref, ...), custom_call_target="tpu_custom_call", output_to_operand_aliasing={{}: (4, {})} | custom-call | tf_op jit(solution)/shard_map/last_time_links/pallas_call | solution.py:732
  (29 shorter events, 2.4 us)
Async XLA Ops:
  0.0 1.8 %copy-start = (f32[4,2,3,3,1,8,1024]{6,5,4,3,2,1,0:T(8,128)S(1)}, f32[4,2,3,3,1,8,1024]{6,5,4,3,2,1,0:T(8,128)}, u32[]{:S(2)}) copy-start(f32[4,2,3,3,1,8,1024]{6,5,4,3,2,1,0:T(8,128)} %links_ref.5) | copy-start | bytes 7077892
  1.3 1.7 %collective-permute-start = (f32[8,8,1024]{2,1,0:T(8,128)S(1)}, f32[8,8,1024]{2,1,0:T(8,128)S(1)}, u32[]{:S(2)}, u32[]{:S(2)}) collective-permute-start(f32[8,8,1024]{2,1,0:T(8,128)S(1)} %get-tuple-element.39.time_ref), channel_id=1, source_target_pairs={{0,4},{4,0},{8,12},{12,8},{16,20},{20,16},{24,28},{28,24},{1,5},{5... | collective-permute-start | bytes 786440 | tf_op jit(solution)/shard_map/ppermute | solution.py:750
  2.3 15.1 %copy-start.2 = (f32[8,17,8,128]{3,2,1,0:T(8,128)S(1)}, f32[8,17,8,128]{3,2,1,0:T(8,128)}, u32[]{:S(2)}) copy-start(f32[8,17,8,128]{3,2,1,0:T(8,128)} %constant.24.clone.distance_ref) | copy-start | bytes 1671172
  2.3 15.1 %copy-start.5 = (bf16[2,144,144]{2,1,0:T(8,128)(2,1)S(1)}, bf16[2,144,144]{2,1,0:T(8,128)(2,1)}, u32[]{:S(2)}) copy-start(bf16[2,144,144]{2,1,0:T(8,128)(2,1)} %constant.18.clone.table_ref) | copy-start | bytes 248836
  2.3 15.1 %copy-start.8 = (f32[8,8,128]{2,1,0:T(8,128)S(1)}, f32[8,8,128]{2,1,0:T(8,128)}, u32[]{:S(2)}) copy-start(f32[8,8,128]{2,1,0:T(8,128)} %constant.25.clone.anchor_ref) | copy-start | bytes 98308
  3.0 17.5 %copy-start.3 = (bf16[2,256,144]{2,1,0:T(8,128)(2,1)S(1)}, bf16[2,256,144]{2,1,0:T(8,128)(2,1)}, u32[]{:S(2)}) copy-start(bf16[2,256,144]{2,1,0:T(8,128)(2,1)} %constant.19.clone.forward_ref) | copy-start | bytes 442372
  3.0 17.5 %copy-start.6 = (f32[256,128]{1,0:T(8,128)S(1)}, f32[256,128]{1,0:T(8,128)}, u32[]{:S(2)}) copy-start(f32[256,128]{1,0:T(8,128)} %constant.22.clone.line_ref) | copy-start | bytes 393220
  3.0 17.5 %copy-start.7 = (bf16[2,128,256]{2,1,0:T(8,128)(2,1)S(1)}, bf16[2,128,256]{2,1,0:T(8,128)(2,1)}, u32[]{:S(2)}) copy-start(bf16[2,128,256]{2,1,0:T(8,128)(2,1)} %constant.20.clone.inward_ref) | copy-start | bytes 393220
  3.0 17.5 %copy-start.9 = (f32[8,1,128]{2,1,0:T(1,128)S(1)}, f32[8,1,128]{2,1,0:T(1,128)}, u32[]{:S(2)}) copy-start(f32[8,1,128]{2,1,0:T(1,128)} %constant.26.clone.plane_ref) | copy-start | bytes 12292
  3.0 19.9 %copy-start.1 = (f32[8,17,8,128]{3,2,1,0:T(8,128)S(1)}, f32[8,17,8,128]{3,2,1,0:T(8,128)}, u32[]{:S(2)}) copy-start(f32[8,17,8,128]{3,2,1,0:T(8,128)} %constant.23.clone.response_ref) | copy-start | bytes 1671172
  3.0 19.9 %copy-start.4 = (bf16[2,144,144]{2,1,0:T(8,128)(2,1)S(1)}, bf16[2,144,144]{2,1,0:T(8,128)(2,1)}, u32[]{:S(2)}) copy-start(bf16[2,144,144]{2,1,0:T(8,128)(2,1)} %constant.21.clone.table_ref) | copy-start | bytes 248836
  17.8 5.0 %collective-permute-start.1 = (f32[16,512]{1,0:T(8,128)S(1)}, f32[16,512]{1,0:T(8,128)S(1)}, u32[]{:S(2)}, u32[]{:S(2)}) collective-permute-start(f32[16,512]{1,0:T(8,128)S(1)} %get-tuple-element.44.sent_ref), channel_id=1, source_target_pairs={{2,0},{3,1},{0,2},{1,3},{6,4},{7,5},{4,6},{5,7},{10,8},{11,9},{8,1... | collective-permute-start | bytes 98312 | tf_op jit(solution)/shard_map/ppermute | solution.py:746
  35.0 1.6 %collective-permute-start.2 = (f32[8,8,1024]{2,1,0:T(8,128)S(1)}, f32[8,8,1024]{2,1,0:T(8,128)S(1)}, u32[]{:S(2)}, u32[]{:S(2)}) collective-permute-start(f32[8,8,1024]{2,1,0:T(8,128)S(1)} %get-tuple-element.52), channel_id=1, source_target_pairs={{0,4},{4,0},{8,12},{12,8},{16,20},{20,16},{24,28},{28,24},{1,5},{5... | collective-permute-start | bytes 786440 | tf_op jit(solution)/shard_map/ppermute | solution.py:750
  37.1 1.6 %collective-permute-start.3 = (f32[8,8,1024]{2,1,0:T(8,128)S(1)}, f32[8,8,1024]{2,1,0:T(8,128)S(1)}, u32[]{:S(2)}, u32[]{:S(2)}) collective-permute-start(f32[8,8,1024]{2,1,0:T(8,128)S(1)} %get-tuple-element.59.time_ref), channel_id=1, source_target_pairs={{0,4},{4,0},{8,12},{12,8},{16,20},{20,16},{24,28},{28,24},{1,5},{5... | collective-permute-start | bytes 786440 | tf_op jit(solution)/shard_map/ppermute | solution.py:750
  50.8 5.6 %collective-permute-start.4 = (f32[16,512]{1,0:T(8,128)S(1)}, f32[16,512]{1,0:T(8,128)S(1)}, u32[]{:S(2)}, u32[]{:S(2)}) collective-permute-start(f32[16,512]{1,0:T(8,128)S(1)} %get-tuple-element.62.sent_ref), channel_id=1, source_target_pairs={{2,0},{3,1},{0,2},{1,3},{6,4},{7,5},{4,6},{5,7},{10,8},{11,9},{8,1... | collective-permute-start | bytes 98312 | tf_op jit(solution)/shard_map/ppermute | solution.py:746
  67.9 2.1 %collective-permute-start.5 = (f32[8,8,1024]{2,1,0:T(8,128)S(1)}, f32[8,8,1024]{2,1,0:T(8,128)S(1)}, u32[]{:S(2)}, u32[]{:S(2)}) collective-permute-start(f32[8,8,1024]{2,1,0:T(8,128)S(1)} %get-tuple-element.68), channel_id=1, source_target_pairs={{0,4},{4,0},{8,12},{12,8},{16,20},{20,16},{24,28},{28,24},{1,5},{5... | collective-permute-start | bytes 786440 | tf_op jit(solution)/shard_map/ppermute | solution.py:750

commit v9 on v8

--- a/solution.py
+++ b/solution.py
@@ -676,10 +676,10 @@
         turn_time(links_ref, at, own, turned_ref)
         return carry
 
-    lax.fori_loop(0, chunks, along_x, 0, unroll=2)
+    lax.fori_loop(0, chunks, along_x, 0, unroll=8)
     copy = pltpu.make_async_copy(x_ref, out_hbm.at[0:1], sent)
     copy.start()
-    lax.fori_loop(0, chunks, along_yz, 0, unroll=2)
+    lax.fori_loop(0, chunks, along_yz, 0, unroll=8)
     copy.wait()
 
 

time: 71.5 us -> 71.8 us (level)
  no operation moved by 1% of the time
where the time goes in v9:
time: 71.8 us; the launch traced here: 71.5 us
  blocking collectives  47.1 us (66%)
  Pallas kernels  12.8 us (18%)
  starting transfers between devices  6.87 us (10%)
  waiting for transfers between devices  4.48 us (6%)
    all_to_all x4, blocking collectives, exchanged(): lax.all_to_all(block, ('ta', 'gz'), split_axis=0, concat_axis=0, axis_ind...  47.1 us
    pallas_call x17, Pallas kernels, call(): pl.pallas_call(kernel, in_specs=in_specs, out_specs=out_specs, out_shape=...  12.8 us
    ppermute x2, starting transfers between devices, passed(): lax.ppermute(block, axis, [((i - distance) % size, i) for i in range(size)])  5.55 us
    ppermute x2, waiting for transfers between devices, passed(): lax.ppermute(block, axis, [((i - distance) % size, i) for i in range(size)])  3.4 us
  transfers between devices with their start and end apart: 6, of which 5 were waited for; matrix products, arithmetic and copies ran while one was open for 0% of the time, Pallas kernels for 9%

profile of v9, /device:TPU:0, one launch (start us, length us, event | category | flops | bytes accessed | tf_op | source)
XLA Modules:
  0.0 71.5 jit_solution(5032049256525901482)
XLA Ops:
  0.0 1.3 %time_gradient.1 = (bf16[2,768,512]{2,1,0:T(8,128)(2,1)S(1)}, f32[8,8,1024]{2,1,0:T(8,128)S(1)}) custom-call(f32[4,2,3,3,1,8,1024]{6,5,4,3,2,1,0:T(8,128)} %links_ref.5), custom_call_target="tpu_custom_call" | custom-call | tf_op jit(solution)/shard_map/time_gradient/pallas_call | solution.py:732
  1.3 0.5 collective-permute-start
  1.8 0.5 space_gradient.1
  2.4 0.6 collective-permute-done.arrived_ref
  3.0 0.5 gradient_modes.2
  3.5 13.9 %all_to_all.20.spectral_ref = f32[16,13,4,128]{3,2,1,0:T(4,128)S(1)} all-to-all(f32[16,13,4,128]{3,2,1,0:T(4,128)S(1)} %bitcast.3), channel_id=1, replica_groups={{0,1,4,5,8,9,12,13,16,17,20,21,24,25,28,29},{2,3,6,7,10,11,14,15,18,19,..., dimensions={0} | all-to-all | bytes 851968 | tf_op jit(solution)/shard_map/all_to_all | solution.py:759
  17.8 2.7 %collective-permute-start.1 = (f32[16,512]{1,0:T(8,128)S(1)}, f32[16,512]{1,0:T(8,128)S(1)}, u32[]{:S(2)}, u32[]{:S(2)}) collective-permute-start(f32[16,512]{1,0:T(8,128)S(1)} %get-tuple-element.44.sent_ref), channel_id=1, source_target_pairs={{2,0},{3,1},{0,2},{1,3},{6,4},{7,5},{4,6},{5,7},{10,8},{11,9},{8,1... | collective-permute-start | bytes 98312 | tf_op jit(solution)/shard_map/ppermute | solution.py:746
  20.5 1.0 %own_half.2 = (f32[128,512]{1,0:T(8,128)S(1)}, bf16[2,768,512]{2,1,0:T(8,128)(2,1)S(1)}) custom-call(f32[144,512]{1,0:T(8,128)S(1)} %get-tuple-element.42.modes_ref, bf16[2,256,144]{2,1,0:T(8,128)(2,1)S(1)} %copy-done.3, bf16[2,128,256]{2,1,0:T(8,128)(2,1)S(1)} %copy-done.7, f32[256,128]{1,0:T(8,128)S(1)} %copy-done.6, f32[8,1,128]{2,1,0:T(1,128)S(1)} %copy-done.9), custom_call_target="tpu_custom_call" | custom-call | tf_op jit(solution)/shard_map/own_half/pallas_call | solution.py:732
  21.5 1.3 %collective-permute-done.1.arrived_ref = f32[16,512]{1,0:T(8,128)S(1)} collective-permute-done((f32[16,512]{1,0:T(8,128)S(1)}, f32[16,512]{1,0:T(8,128)S(1)}, u32[]{:S(2)}, u32[]{:S(2)}) %collective-permute-start.1) | collective-permute-done | bytes 32800 | tf_op jit(solution)/shard_map/ppermute | solution.py:746
  22.9 0.4 coupled_halves.2
  23.2 11.2 %all_to_all.21.spectral_ref = f32[16,13,4,128]{3,2,1,0:T(4,128)S(1)} all-to-all(f32[16,13,4,128]{3,2,1,0:T(4,128)S(1)} %coupled_halves.2), channel_id=1, replica_groups={{0,1,4,5,8,9,12,13,16,17,20,21,24,25,28,29},{2,3,6,7,10,11,14,15,18,19,..., dimensions={0} | all-to-all | bytes 851968 | tf_op jit(solution)/shard_map/all_to_all | solution.py:759
  34.4 0.5 smooth_field.2
  35.2 1.1 %x_links.1 = (f32[4,2,3,3,1,8,1024]{6,5,4,3,2,1,0:T(8,128)S(1)}, f32[18,8,1024]{2,1,0:T(8,128)S(1)}, f32[18,8,128]{2,1,0:T(8,128)S(1)}, f32[12,8,1024]{2,1,0:T(8,128)S(1)}, f32[8,8,1024]{2,1,0:T(8,128)S(1)}) custom-call(f32[4,2,3,3,1,8,1024]{6,5,4,3,2,1,0:T(8,128)S(1)} %copy-done, f32[8,8,1024]{2,1,0:T(8,128)S(1)} %get-tuple-element.47.smooth_ref, ...), custom_call_target="tpu_custom_call" | custom-call | tf_op jit(solution)/shard_map/x_links/pallas_call | solution.py:732
  36.6 0.5 time_links.1
  37.4 1.1 %yz_links.1 = (f32[4,2,3,3,1,8,1024]{6,5,4,3,2,1,0:T(8,128)S(1)}, f32[8,8,1024]{2,1,0:T(8,128)S(1)}, f32[2,8,1024]{2,1,0:T(8,128)S(1)}) custom-call(f32[4,2,3,3,1,8,1024]{6,5,4,3,2,1,0:T(8,128)S(1)} %get-tuple-element.53.rotated_ref, f32[4,2,3,3,1,8,1024]{6,5,4,3,2,1,0:T(8,128)S(1)} %copy-done, ...), custom_call_target="tpu_custom_call", output_to_operand_aliasing={{0}: (0, {})} | custom-call | tf_op jit(solution)/shard_map/yz_links/pallas_call | solution.py:732
  38.7 0.5 gradient_modes.3
  39.2 11.3 %all_to_all.22.spectral_ref = f32[16,13,4,128]{3,2,1,0:T(4,128)S(1)} all-to-all(f32[16,13,4,128]{3,2,1,0:T(4,128)S(1)} %bitcast.2), channel_id=1, replica_groups={{0,1,4,5,8,9,12,13,16,17,20,21,24,25,28,29},{2,3,6,7,10,11,14,15,18,19,..., dimensions={0} | all-to-all | bytes 851968 | tf_op jit(solution)/shard_map/all_to_all | solution.py:759
  50.8 2.9 %collective-permute-start.4 = (f32[16,512]{1,0:T(8,128)S(1)}, f32[16,512]{1,0:T(8,128)S(1)}, u32[]{:S(2)}, u32[]{:S(2)}) collective-permute-start(f32[16,512]{1,0:T(8,128)S(1)} %get-tuple-element.62.sent_ref), channel_id=1, source_target_pairs={{2,0},{3,1},{0,2},{1,3},{6,4},{7,5},{4,6},{5,7},{10,8},{11,9},{8,1... | collective-permute-start | bytes 98312 | tf_op jit(solution)/shard_map/ppermute | solution.py:746
  53.7 0.6 own_half.3.own_ref
  54.3 2.1 %collective-permute-done.4.arrived_ref = f32[16,512]{1,0:T(8,128)S(1)} collective-permute-done((f32[16,512]{1,0:T(8,128)S(1)}, f32[16,512]{1,0:T(8,128)S(1)}, u32[]{:S(2)}, u32[]{:S(2)}) %collective-permute-start.4) | collective-permute-done | bytes 32800 | tf_op jit(solution)/shard_map/ppermute | solution.py:746
  56.8 10.7 %all_to_all.23.spectral_ref = f32[16,13,4,128]{3,2,1,0:T(4,128)S(1)} all-to-all(f32[16,13,4,128]{3,2,1,0:T(4,128)S(1)} %coupled_halves.3), channel_id=1, replica_groups={{0,1,4,5,8,9,12,13,16,17,20,21,24,25,28,29},{2,3,6,7,10,11,14,15,18,19,..., dimensions={0} | all-to-all | bytes 851968 | tf_op jit(solution)/shard_map/all_to_all | solution.py:759
  67.4 0.5 smooth_field.3
  68.2 2.0 %last_space_links.1 = (f32[4,2,3,3,1,8,1024]{6,5,4,3,2,1,0:T(8,128)}, f32[2,2,3,3,1,8,1024]{6,5,4,3,2,1,0:T(8,128)S(1)}, f32[12,8,1024]{2,1,0:T(8,128)S(1)}) custom-call(f32[4,2,3,3,1,8,1024]{6,5,4,3,2,1,0:T(8,128)S(1)} %get-tuple-element.57.links_ref, f32[8,8,1024]{2,1,0:T(8,128)S(1)} %get-tuple-element.64.smooth_ref, ...), custom_call_target="tpu_custom_call" | custom-call | tf_op jit(solution)/shard_map/last_space_links/pallas_call | solution.py:732
  70.2 1.2 %last_time_links.1 = f32[4,2,3,3,1,8,1024]{6,5,4,3,2,1,0:T(8,128)} custom-call(f32[12,8,1024]{2,1,0:T(8,128)S(1)} %get-tuple-element.66.turned_ref, f32[8,8,1024]{2,1,0:T(8,128)S(1)} %get-tuple-element.67.part_ref, f32[8,8,1024]{2,1,0:T(8,128)S(1)} %collective-permute-done.5.arrived_ref, ...), custom_call_target="tpu_custom_call", output_to_operand_aliasing={{}: (4, {})} | custom-call | tf_op jit(solution)/shard_map/last_time_links/pallas_call | solution.py:732
  (29 shorter events, 2.4 us)
Async XLA Ops:
  0.0 1.8 %copy-start = (f32[4,2,3,3,1,8,1024]{6,5,4,3,2,1,0:T(8,128)S(1)}, f32[4,2,3,3,1,8,1024]{6,5,4,3,2,1,0:T(8,128)}, u32[]{:S(2)}) copy-start(f32[4,2,3,3,1,8,1024]{6,5,4,3,2,1,0:T(8,128)} %links_ref.5) | copy-start | bytes 7077892
  1.3 1.7 %collective-permute-start = (f32[8,8,1024]{2,1,0:T(8,128)S(1)}, f32[8,8,1024]{2,1,0:T(8,128)S(1)}, u32[]{:S(2)}, u32[]{:S(2)}) collective-permute-start(f32[8,8,1024]{2,1,0:T(8,128)S(1)} %get-tuple-element.39.time_ref), channel_id=1, source_target_pairs={{0,4},{4,0},{8,12},{12,8},{16,20},{20,16},{24,28},{28,24},{1,5},{5... | collective-permute-start | bytes 786440 | tf_op jit(solution)/shard_map/ppermute | solution.py:750
  2.3 15.1 %copy-start.2 = (f32[8,17,8,128]{3,2,1,0:T(8,128)S(1)}, f32[8,17,8,128]{3,2,1,0:T(8,128)}, u32[]{:S(2)}) copy-start(f32[8,17,8,128]{3,2,1,0:T(8,128)} %constant.24.clone.distance_ref) | copy-start | bytes 1671172
  2.3 15.1 %copy-start.5 = (bf16[2,144,144]{2,1,0:T(8,128)(2,1)S(1)}, bf16[2,144,144]{2,1,0:T(8,128)(2,1)}, u32[]{:S(2)}) copy-start(bf16[2,144,144]{2,1,0:T(8,128)(2,1)} %constant.18.clone.table_ref) | copy-start | bytes 248836
  2.3 15.1 %copy-start.8 = (f32[8,8,128]{2,1,0:T(8,128)S(1)}, f32[8,8,128]{2,1,0:T(8,128)}, u32[]{:S(2)}) copy-start(f32[8,8,128]{2,1,0:T(8,128)} %constant.25.clone.anchor_ref) | copy-start | bytes 98308
  3.0 17.5 %copy-start.3 = (bf16[2,256,144]{2,1,0:T(8,128)(2,1)S(1)}, bf16[2,256,144]{2,1,0:T(8,128)(2,1)}, u32[]{:S(2)}) copy-start(bf16[2,256,144]{2,1,0:T(8,128)(2,1)} %constant.19.clone.forward_ref) | copy-start | bytes 442372
  3.0 17.5 %copy-start.6 = (f32[256,128]{1,0:T(8,128)S(1)}, f32[256,128]{1,0:T(8,128)}, u32[]{:S(2)}) copy-start(f32[256,128]{1,0:T(8,128)} %constant.22.clone.line_ref) | copy-start | bytes 393220
  3.0 17.5 %copy-start.7 = (bf16[2,128,256]{2,1,0:T(8,128)(2,1)S(1)}, bf16[2,128,256]{2,1,0:T(8,128)(2,1)}, u32[]{:S(2)}) copy-start(bf16[2,128,256]{2,1,0:T(8,128)(2,1)} %constant.20.clone.inward_ref) | copy-start | bytes 393220
  3.0 17.5 %copy-start.9 = (f32[8,1,128]{2,1,0:T(1,128)S(1)}, f32[8,1,128]{2,1,0:T(1,128)}, u32[]{:S(2)}) copy-start(f32[8,1,128]{2,1,0:T(1,128)} %constant.26.clone.plane_ref) | copy-start | bytes 12292
  3.0 19.9 %copy-start.1 = (f32[8,17,8,128]{3,2,1,0:T(8,128)S(1)}, f32[8,17,8,128]{3,2,1,0:T(8,128)}, u32[]{:S(2)}) copy-start(f32[8,17,8,128]{3,2,1,0:T(8,128)} %constant.23.clone.response_ref) | copy-start | bytes 1671172
  3.0 19.9 %copy-start.4 = (bf16[2,144,144]{2,1,0:T(8,128)(2,1)S(1)}, bf16[2,144,144]{2,1,0:T(8,128)(2,1)}, u32[]{:S(2)}) copy-start(bf16[2,144,144]{2,1,0:T(8,128)(2,1)} %constant.21.clone.table_ref) | copy-start | bytes 248836
  17.8 5.0 %collective-permute-start.1 = (f32[16,512]{1,0:T(8,128)S(1)}, f32[16,512]{1,0:T(8,128)S(1)}, u32[]{:S(2)}, u32[]{:S(2)}) collective-permute-start(f32[16,512]{1,0:T(8,128)S(1)} %get-tuple-element.44.sent_ref), channel_id=1, source_target_pairs={{2,0},{3,1},{0,2},{1,3},{6,4},{7,5},{4,6},{5,7},{10,8},{11,9},{8,1... | collective-permute-start | bytes 98312 | tf_op jit(solution)/shard_map/ppermute | solution.py:746
  35.0 1.6 %collective-permute-start.2 = (f32[8,8,1024]{2,1,0:T(8,128)S(1)}, f32[8,8,1024]{2,1,0:T(8,128)S(1)}, u32[]{:S(2)}, u32[]{:S(2)}) collective-permute-start(f32[8,8,1024]{2,1,0:T(8,128)S(1)} %get-tuple-element.52), channel_id=1, source_target_pairs={{0,4},{4,0},{8,12},{12,8},{16,20},{20,16},{24,28},{28,24},{1,5},{5... | collective-permute-start | bytes 786440 | tf_op jit(solution)/shard_map/ppermute | solution.py:750
  37.1 1.6 %collective-permute-start.3 = (f32[8,8,1024]{2,1,0:T(8,128)S(1)}, f32[8,8,1024]{2,1,0:T(8,128)S(1)}, u32[]{:S(2)}, u32[]{:S(2)}) collective-permute-start(f32[8,8,1024]{2,1,0:T(8,128)S(1)} %get-tuple-element.59.time_ref), channel_id=1, source_target_pairs={{0,4},{4,0},{8,12},{12,8},{16,20},{20,16},{24,28},{28,24},{1,5},{5... | collective-permute-start | bytes 786440 | tf_op jit(solution)/shard_map/ppermute | solution.py:750
  50.8 5.6 %collective-permute-start.4 = (f32[16,512]{1,0:T(8,128)S(1)}, f32[16,512]{1,0:T(8,128)S(1)}, u32[]{:S(2)}, u32[]{:S(2)}) collective-permute-start(f32[16,512]{1,0:T(8,128)S(1)} %get-tuple-element.62.sent_ref), channel_id=1, source_target_pairs={{2,0},{3,1},{0,2},{1,3},{6,4},{7,5},{4,6},{5,7},{10,8},{11,9},{8,1... | collective-permute-start | bytes 98312 | tf_op jit(solution)/shard_map/ppermute | solution.py:746
  67.9 2.3 %collective-permute-start.5 = (f32[8,8,1024]{2,1,0:T(8,128)S(1)}, f32[8,8,1024]{2,1,0:T(8,128)S(1)}, u32[]{:S(2)}, u32[]{:S(2)}) collective-permute-start(f32[8,8,1024]{2,1,0:T(8,128)S(1)} %get-tuple-element.68), channel_id=1, source_target_pairs={{0,4},{4,0},{8,12},{12,8},{16,20},{20,16},{24,28},{28,24},{1,5},{5... | collective-permute-start | bytes 786440 | tf_op jit(solution)/shard_map/ppermute | solution.py:750

commit v10 on v6

--- a/solution.py
+++ b/solution.py
@@ -56,7 +56,7 @@
     spread = padded(spread, size, size)
     forward = padded(np.kron(along_z[:, : half + 1], same_t), depth_length * time_length, size)
     inward = np.kron(along_z[:half], same_t)
-    return [jnp.asarray(split_table(t)) for t in (spread.T, forward, inward, spread)]
+    return [jnp.asarray(split_table(t)) for t in (spread.T, forward, inward, 0.04 * spread)]
 
 
 def distance_table(time_length, depth_length, plane_sum):
@@ -157,7 +157,7 @@
 
 
 def exponential(comps):
-    ar, ai, br, bi, cr, ci, d0, d1 = [0.04 * v for v in comps]
+    ar, ai, br, bi, cr, ci, d0, d1 = comps
     d2 = -(d0 + d1)
     a2 = ar * ar + ai * ai
     b2 = br * br + bi * bi

time: 71.4 us -> 71.4 us (level)
  no operation moved by 1% of the time
where the time goes in v10:
time: 71.4 us; the launch traced here: 71.1 us
  blocking collectives  47.1 us (66%)
  Pallas kernels  12.4 us (17%)
  starting transfers between devices  6.87 us (10%)
  waiting for transfers between devices  4.5 us (6%)
    all_to_all x4, blocking collectives, exchanged(): lax.all_to_all(block, ('ta', 'gz'), split_axis=0, concat_axis=0, axis_ind...  47.1 us
    pallas_call x17, Pallas kernels, call(): pl.pallas_call(kernel, in_specs=in_specs, out_specs=out_specs, out_shape=...  12.4 us
    ppermute x2, starting transfers between devices, passed(): lax.ppermute(block, axis, [((i - distance) % size, i) for i in range(size)])  5.55 us
    ppermute x2, waiting for transfers between devices, passed(): lax.ppermute(block, axis, [((i - distance) % size, i) for i in range(size)])  3.39 us
  transfers between devices with their start and end apart: 6, of which 5 were waited for; matrix products, arithmetic and copies ran while one was open for 0% of the time, Pallas kernels for 8%

profile of v10, /device:TPU:0, one launch (start us, length us, event | category | flops | bytes accessed | tf_op | source)
XLA Modules:
  0.0 71.1 jit_solution(12391153189569236054)
XLA Ops:
  0.0 1.3 %time_gradient.1 = (bf16[2,768,512]{2,1,0:T(8,128)(2,1)S(1)}, f32[8,8,1024]{2,1,0:T(8,128)S(1)}) custom-call(f32[4,2,3,3,1,8,1024]{6,5,4,3,2,1,0:T(8,128)} %links_ref.5), custom_call_target="tpu_custom_call" | custom-call | tf_op jit(solution)/shard_map/time_gradient/pallas_call | solution.py:732
  1.3 0.5 collective-permute-start
  1.8 0.5 space_gradient.1
  2.4 0.6 collective-permute-done.arrived_ref
  3.0 0.5 gradient_modes.2
  3.5 13.9 %all_to_all.20.spectral_ref = f32[16,13,4,128]{3,2,1,0:T(4,128)S(1)} all-to-all(f32[16,13,4,128]{3,2,1,0:T(4,128)S(1)} %bitcast.3), channel_id=1, replica_groups={{0,1,4,5,8,9,12,13,16,17,20,21,24,25,28,29},{2,3,6,7,10,11,14,15,18,19,..., dimensions={0} | all-to-all | bytes 851968 | tf_op jit(solution)/shard_map/all_to_all | solution.py:759
  17.8 2.7 %collective-permute-start.1 = (f32[16,512]{1,0:T(8,128)S(1)}, f32[16,512]{1,0:T(8,128)S(1)}, u32[]{:S(2)}, u32[]{:S(2)}) collective-permute-start(f32[16,512]{1,0:T(8,128)S(1)} %get-tuple-element.44.sent_ref), channel_id=1, source_target_pairs={{2,0},{3,1},{0,2},{1,3},{6,4},{7,5},{4,6},{5,7},{10,8},{11,9},{8,1... | collective-permute-start | bytes 98312 | tf_op jit(solution)/shard_map/ppermute | solution.py:746
  20.5 1.0 %own_half.2 = (f32[128,512]{1,0:T(8,128)S(1)}, bf16[2,768,512]{2,1,0:T(8,128)(2,1)S(1)}) custom-call(f32[144,512]{1,0:T(8,128)S(1)} %get-tuple-element.42.modes_ref, bf16[2,256,144]{2,1,0:T(8,128)(2,1)S(1)} %copy-done.3, bf16[2,128,256]{2,1,0:T(8,128)(2,1)S(1)} %copy-done.7, f32[256,128]{1,0:T(8,128)S(1)} %copy-done.6, f32[8,1,128]{2,1,0:T(1,128)S(1)} %copy-done.9), custom_call_target="tpu_custom_call" | custom-call | tf_op jit(solution)/shard_map/own_half/pallas_call | solution.py:732
  21.5 1.3 %collective-permute-done.1.arrived_ref = f32[16,512]{1,0:T(8,128)S(1)} collective-permute-done((f32[16,512]{1,0:T(8,128)S(1)}, f32[16,512]{1,0:T(8,128)S(1)}, u32[]{:S(2)}, u32[]{:S(2)}) %collective-permute-start.1) | collective-permute-done | bytes 32800 | tf_op jit(solution)/shard_map/ppermute | solution.py:746
  22.9 0.4 coupled_halves.2
  23.2 11.2 %all_to_all.21.spectral_ref = f32[16,13,4,128]{3,2,1,0:T(4,128)S(1)} all-to-all(f32[16,13,4,128]{3,2,1,0:T(4,128)S(1)} %coupled_halves.2), channel_id=1, replica_groups={{0,1,4,5,8,9,12,13,16,17,20,21,24,25,28,29},{2,3,6,7,10,11,14,15,18,19,..., dimensions={0} | all-to-all | bytes 851968 | tf_op jit(solution)/shard_map/all_to_all | solution.py:759
  34.4 0.5 smooth_field.2
  35.2 1.1 %x_links.1 = (f32[4,2,3,3,1,8,1024]{6,5,4,3,2,1,0:T(8,128)S(1)}, f32[18,8,1024]{2,1,0:T(8,128)S(1)}, f32[18,8,128]{2,1,0:T(8,128)S(1)}, f32[12,8,1024]{2,1,0:T(8,128)S(1)}, f32[8,8,1024]{2,1,0:T(8,128)S(1)}) custom-call(f32[4,2,3,3,1,8,1024]{6,5,4,3,2,1,0:T(8,128)S(1)} %copy-done, f32[8,8,1024]{2,1,0:T(8,128)S(1)} %get-tuple-element.47.smooth_ref, ...), custom_call_target="tpu_custom_call" | custom-call | tf_op jit(solution)/shard_map/x_links/pallas_call | solution.py:732
  36.6 0.5 time_links.1
  37.4 1.1 %yz_links.1 = (f32[4,2,3,3,1,8,1024]{6,5,4,3,2,1,0:T(8,128)S(1)}, f32[8,8,1024]{2,1,0:T(8,128)S(1)}, f32[2,8,1024]{2,1,0:T(8,128)S(1)}) custom-call(f32[4,2,3,3,1,8,1024]{6,5,4,3,2,1,0:T(8,128)S(1)} %get-tuple-element.53.rotated_ref, f32[4,2,3,3,1,8,1024]{6,5,4,3,2,1,0:T(8,128)S(1)} %copy-done, ...), custom_call_target="tpu_custom_call", output_to_operand_aliasing={{0}: (0, {})} | custom-call | tf_op jit(solution)/shard_map/yz_links/pallas_call | solution.py:732
  38.7 0.5 gradient_modes.3
  39.2 11.3 %all_to_all.22.spectral_ref = f32[16,13,4,128]{3,2,1,0:T(4,128)S(1)} all-to-all(f32[16,13,4,128]{3,2,1,0:T(4,128)S(1)} %bitcast.2), channel_id=1, replica_groups={{0,1,4,5,8,9,12,13,16,17,20,21,24,25,28,29},{2,3,6,7,10,11,14,15,18,19,..., dimensions={0} | all-to-all | bytes 851968 | tf_op jit(solution)/shard_map/all_to_all | solution.py:759
  50.8 2.9 %collective-permute-start.4 = (f32[16,512]{1,0:T(8,128)S(1)}, f32[16,512]{1,0:T(8,128)S(1)}, u32[]{:S(2)}, u32[]{:S(2)}) collective-permute-start(f32[16,512]{1,0:T(8,128)S(1)} %get-tuple-element.62.sent_ref), channel_id=1, source_target_pairs={{2,0},{3,1},{0,2},{1,3},{6,4},{7,5},{4,6},{5,7},{10,8},{11,9},{8,1... | collective-permute-start | bytes 98312 | tf_op jit(solution)/shard_map/ppermute | solution.py:746
  53.7 0.6 own_half.3.own_ref
  54.3 2.1 %collective-permute-done.4.arrived_ref = f32[16,512]{1,0:T(8,128)S(1)} collective-permute-done((f32[16,512]{1,0:T(8,128)S(1)}, f32[16,512]{1,0:T(8,128)S(1)}, u32[]{:S(2)}, u32[]{:S(2)}) %collective-permute-start.4) | collective-permute-done | bytes 32800 | tf_op jit(solution)/shard_map/ppermute | solution.py:746
  56.7 10.7 %all_to_all.23.spectral_ref = f32[16,13,4,128]{3,2,1,0:T(4,128)S(1)} all-to-all(f32[16,13,4,128]{3,2,1,0:T(4,128)S(1)} %coupled_halves.3), channel_id=1, replica_groups={{0,1,4,5,8,9,12,13,16,17,20,21,24,25,28,29},{2,3,6,7,10,11,14,15,18,19,..., dimensions={0} | all-to-all | bytes 851968 | tf_op jit(solution)/shard_map/all_to_all | solution.py:759
  67.4 0.5 smooth_field.3
  68.2 1.6 %last_space_links.1 = (f32[4,2,3,3,1,8,1024]{6,5,4,3,2,1,0:T(8,128)}, f32[2,2,3,3,1,8,1024]{6,5,4,3,2,1,0:T(8,128)S(1)}, f32[12,8,1024]{2,1,0:T(8,128)S(1)}) custom-call(f32[4,2,3,3,1,8,1024]{6,5,4,3,2,1,0:T(8,128)S(1)} %get-tuple-element.57.links_ref, f32[8,8,1024]{2,1,0:T(8,128)S(1)} %get-tuple-element.64.smooth_ref, ...), custom_call_target="tpu_custom_call" | custom-call | tf_op jit(solution)/shard_map/last_space_links/pallas_call | solution.py:732
  69.9 1.2 %last_time_links.1 = f32[4,2,3,3,1,8,1024]{6,5,4,3,2,1,0:T(8,128)} custom-call(f32[12,8,1024]{2,1,0:T(8,128)S(1)} %get-tuple-element.66.turned_ref, f32[8,8,1024]{2,1,0:T(8,128)S(1)} %get-tuple-element.67.part_ref, f32[8,8,1024]{2,1,0:T(8,128)S(1)} %collective-permute-done.5.arrived_ref, ...), custom_call_target="tpu_custom_call", output_to_operand_aliasing={{}: (4, {})} | custom-call | tf_op jit(solution)/shard_map/last_time_links/pallas_call | solution.py:732
  (29 shorter events, 2.4 us)
Async XLA Ops:
  0.0 1.8 %copy-start = (f32[4,2,3,3,1,8,1024]{6,5,4,3,2,1,0:T(8,128)S(1)}, f32[4,2,3,3,1,8,1024]{6,5,4,3,2,1,0:T(8,128)}, u32[]{:S(2)}) copy-start(f32[4,2,3,3,1,8,1024]{6,5,4,3,2,1,0:T(8,128)} %links_ref.5) | copy-start | bytes 7077892
  1.3 1.7 %collective-permute-start = (f32[8,8,1024]{2,1,0:T(8,128)S(1)}, f32[8,8,1024]{2,1,0:T(8,128)S(1)}, u32[]{:S(2)}, u32[]{:S(2)}) collective-permute-start(f32[8,8,1024]{2,1,0:T(8,128)S(1)} %get-tuple-element.39.time_ref), channel_id=1, source_target_pairs={{0,4},{4,0},{8,12},{12,8},{16,20},{20,16},{24,28},{28,24},{1,5},{5... | collective-permute-start | bytes 786440 | tf_op jit(solution)/shard_map/ppermute | solution.py:750
  2.3 15.1 %copy-start.2 = (f32[8,17,8,128]{3,2,1,0:T(8,128)S(1)}, f32[8,17,8,128]{3,2,1,0:T(8,128)}, u32[]{:S(2)}) copy-start(f32[8,17,8,128]{3,2,1,0:T(8,128)} %constant.24.clone.distance_ref) | copy-start | bytes 1671172
  2.3 15.1 %copy-start.5 = (bf16[2,144,144]{2,1,0:T(8,128)(2,1)S(1)}, bf16[2,144,144]{2,1,0:T(8,128)(2,1)}, u32[]{:S(2)}) copy-start(bf16[2,144,144]{2,1,0:T(8,128)(2,1)} %constant.18.clone.table_ref) | copy-start | bytes 248836
  2.3 15.1 %copy-start.8 = (f32[8,8,128]{2,1,0:T(8,128)S(1)}, f32[8,8,128]{2,1,0:T(8,128)}, u32[]{:S(2)}) copy-start(f32[8,8,128]{2,1,0:T(8,128)} %constant.25.clone.anchor_ref) | copy-start | bytes 98308
  3.0 17.5 %copy-start.3 = (bf16[2,256,144]{2,1,0:T(8,128)(2,1)S(1)}, bf16[2,256,144]{2,1,0:T(8,128)(2,1)}, u32[]{:S(2)}) copy-start(bf16[2,256,144]{2,1,0:T(8,128)(2,1)} %constant.19.clone.forward_ref) | copy-start | bytes 442372
  3.0 17.5 %copy-start.6 = (f32[256,128]{1,0:T(8,128)S(1)}, f32[256,128]{1,0:T(8,128)}, u32[]{:S(2)}) copy-start(f32[256,128]{1,0:T(8,128)} %constant.22.clone.line_ref) | copy-start | bytes 393220
  3.0 17.5 %copy-start.7 = (bf16[2,128,256]{2,1,0:T(8,128)(2,1)S(1)}, bf16[2,128,256]{2,1,0:T(8,128)(2,1)}, u32[]{:S(2)}) copy-start(bf16[2,128,256]{2,1,0:T(8,128)(2,1)} %constant.20.clone.inward_ref) | copy-start | bytes 393220
  3.0 17.5 %copy-start.9 = (f32[8,1,128]{2,1,0:T(1,128)S(1)}, f32[8,1,128]{2,1,0:T(1,128)}, u32[]{:S(2)}) copy-start(f32[8,1,128]{2,1,0:T(1,128)} %constant.26.clone.plane_ref) | copy-start | bytes 12292
  3.0 19.9 %copy-start.1 = (f32[8,17,8,128]{3,2,1,0:T(8,128)S(1)}, f32[8,17,8,128]{3,2,1,0:T(8,128)}, u32[]{:S(2)}) copy-start(f32[8,17,8,128]{3,2,1,0:T(8,128)} %constant.23.clone.response_ref) | copy-start | bytes 1671172
  3.0 19.9 %copy-start.4 = (bf16[2,144,144]{2,1,0:T(8,128)(2,1)S(1)}, bf16[2,144,144]{2,1,0:T(8,128)(2,1)}, u32[]{:S(2)}) copy-start(bf16[2,144,144]{2,1,0:T(8,128)(2,1)} %constant.21.clone.table_ref) | copy-start | bytes 248836
  17.8 5.0 %collective-permute-start.1 = (f32[16,512]{1,0:T(8,128)S(1)}, f32[16,512]{1,0:T(8,128)S(1)}, u32[]{:S(2)}, u32[]{:S(2)}) collective-permute-start(f32[16,512]{1,0:T(8,128)S(1)} %get-tuple-element.44.sent_ref), channel_id=1, source_target_pairs={{2,0},{3,1},{0,2},{1,3},{6,4},{7,5},{4,6},{5,7},{10,8},{11,9},{8,1... | collective-permute-start | bytes 98312 | tf_op jit(solution)/shard_map/ppermute | solution.py:746
  35.0 1.6 %collective-permute-start.2 = (f32[8,8,1024]{2,1,0:T(8,128)S(1)}, f32[8,8,1024]{2,1,0:T(8,128)S(1)}, u32[]{:S(2)}, u32[]{:S(2)}) collective-permute-start(f32[8,8,1024]{2,1,0:T(8,128)S(1)} %get-tuple-element.52), channel_id=1, source_target_pairs={{0,4},{4,0},{8,12},{12,8},{16,20},{20,16},{24,28},{28,24},{1,5},{5... | collective-permute-start | bytes 786440 | tf_op jit(solution)/shard_map/ppermute | solution.py:750
  37.1 1.6 %collective-permute-start.3 = (f32[8,8,1024]{2,1,0:T(8,128)S(1)}, f32[8,8,1024]{2,1,0:T(8,128)S(1)}, u32[]{:S(2)}, u32[]{:S(2)}) collective-permute-start(f32[8,8,1024]{2,1,0:T(8,128)S(1)} %get-tuple-element.59.time_ref), channel_id=1, source_target_pairs={{0,4},{4,0},{8,12},{12,8},{16,20},{20,16},{24,28},{28,24},{1,5},{5... | collective-permute-start | bytes 786440 | tf_op jit(solution)/shard_map/ppermute | solution.py:750
  50.8 5.6 %collective-permute-start.4 = (f32[16,512]{1,0:T(8,128)S(1)}, f32[16,512]{1,0:T(8,128)S(1)}, u32[]{:S(2)}, u32[]{:S(2)}) collective-permute-start(f32[16,512]{1,0:T(8,128)S(1)} %get-tuple-element.62.sent_ref), channel_id=1, source_target_pairs={{2,0},{3,1},{0,2},{1,3},{6,4},{7,5},{4,6},{5,7},{10,8},{11,9},{8,1... | collective-permute-start | bytes 98312 | tf_op jit(solution)/shard_map/ppermute | solution.py:746
  67.9 1.9 %collective-permute-start.5 = (f32[8,8,1024]{2,1,0:T(8,128)S(1)}, f32[8,8,1024]{2,1,0:T(8,128)S(1)}, u32[]{:S(2)}, u32[]{:S(2)}) collective-permute-start(f32[8,8,1024]{2,1,0:T(8,128)S(1)} %get-tuple-element.68), channel_id=1, source_target_pairs={{0,4},{4,0},{8,12},{12,8},{16,20},{20,16},{24,28},{28,24},{1,5},{5... | collective-permute-start | bytes 786440 | tf_op jit(solution)/shard_map/ppermute | solution.py:750
